TPU v7x, 32 devices: a whole 2x2x4 slice. The times are simulated.
32 devices in a mesh: frames: 8 (over z, x), tokens: 4 (over y, core).
Axes of the slice: x: 2, y: 2, z: 4, core: 2. Of those that a mesh axis runs over, the one named last changes fastest.
Arguments:
- encoder_out: bfloat16 [8, 512, 512], P('tokens', 'frames'), may hold values from -6 to 6
- encoder_weight: bfloat16 [512, 512], replicated, may hold values from -0.1875 to 0.1875
- encoder_bias: float32 [512], replicated, may hold values from -2 to 2
- predictor_out: bfloat16 [8, 24, 512], P('frames', 'tokens'), may hold values from -6 to 6
- predictor_weight: bfloat16 [512, 512], replicated, may hold values from -0.1875 to 0.1875
- predictor_bias: float32 [512], replicated, may hold values from -2 to 2
- output_weight: bfloat16 [512, 1024], replicated, may hold values from -0.5 to 0.5
- output_bias: float32 [1024], replicated, may hold values from -3 to 3
- labels: int32 [8, 24], P(None, 'tokens'), may hold values from 1 to 1023
- frame_lens: int32 [8], replicated, may hold values from 85 to 512, as said below
- token_lens: int32 [8], replicated, may hold values from 1 to 23, as said below
- loss_scale: float32 [8], replicated, may hold values from 0.5 to 1.5
Outputs:
- losses: float32 [8], P('frames')
- encoder_gradient: float32 [8, 512, 512], P('tokens', 'frames')
- predictor_gradient: float32 [8, 24, 512], P('frames', 'tokens')
- encoder_weight_gradient: float32 [512, 512], replicated
- encoder_bias_gradient: float32 [512], replicated
- predictor_weight_gradient: float32 [512, 512], replicated
- predictor_bias_gradient: float32 [512], replicated
- output_weight_gradient: float32 [512, 1024], replicated
- output_bias_gradient: float32 [1024], replicated
Inputs may be any that keep to these rules, and one draw needn't show every extreme that they name: `frame_lens`: some sequence, drawn from the seed, has all 512 frames. `token_lens`: the sequence with all 512 frames has 23 labels.
All inputs are finite; a program needn't handle non-finite values.
Results may differ from a plain program's by a relative error of at most 0.0087.
Values may be sent and summed in bfloat16 or wider, within the bound.
No kernel may reach another device: no remote copies, remote signals or barrier semaphores. Data moves between devices by JAX's collectives and lax.ppermute only.
A program may use at most 256 MiB of HBM per device.

v0:
```python
import math

import jax
import jax.numpy as jnp
from jax import lax
from jax.sharding import PartitionSpec as P

VERY_NEGATIVE = -1e30


def passed_along(array, axis, by):
    count = lax.axis_size(axis)
    pairs = [(i, i + by) for i in range(count) if 0 <= i + by < count]
    return lax.ppermute(array, axis, pairs)


def cut_along(array, dim, count):
    before, after = (array.shape[:dim], array.shape[dim + 1 :])
    return jnp.moveaxis(array.reshape(*before, count, -1, *after), dim, 0)


def sent_and_summed(array, axis, dim):
    count = lax.axis_size(axis)
    blocks = lax.all_to_all(cut_along(array, dim, count), axis, 0, 0, tiled=True)
    return jnp.sum(blocks.astype(jnp.float32), axis=0)


def side_by_side(arrays, axis, dim, along):
    widths = [math.prod(a.shape[along:]) for a in arrays]
    both = jnp.concatenate(
        [a.reshape(*a.shape[:along], w) for a, w in zip(arrays, widths)], axis=along
    )
    filled = sent_and_summed(both, axis, dim)
    blocks = jnp.split(filled, [sum(widths[:k]) for k in range(1, len(widths))], axis=along)
    return tuple(
        (b.reshape(*filled.shape[:along], *a.shape[along:]) for a, b in zip(arrays, blocks))
    )


def block_shape(seq_count, frame_count, unit_count):
    cell_count = frame_count * unit_count
    group_size = 1
    while seq_count % (group_size * 2) == 0 and group_size * 2 * cell_count <= 1024:
        group_size = group_size * 2
    return (group_size, frame_count)


def pick_block(block_number, frame_proj, token_proj, label_ids, group_size, frame_span):
    per_sequence = frame_proj.shape[1] // frame_span
    seq_start = block_number // per_sequence * group_size
    frame_start = block_number % per_sequence * frame_span
    frame_block = lax.dynamic_slice(
        frame_proj, (seq_start, frame_start, 0), (group_size, frame_span, frame_proj.shape[2])
    )
    token_block = lax.dynamic_slice(
        token_proj, (seq_start, 0, 0), (group_size, token_proj.shape[1], token_proj.shape[2])
    )
    label_block = lax.dynamic_slice(label_ids, (seq_start, 0), (group_size, label_ids.shape[1]))
    return (frame_block, token_block, label_block, seq_start, frame_start)


def joint_logits(frame_block, token_block, output_weight, output_bias):
    hidden = jnp.tanh(
        frame_block.astype(jnp.float32)[:, :, None, :]
        + token_block.astype(jnp.float32)[:, None, :, :]
    )
    hidden_low = hidden.astype(jnp.bfloat16)
    logits = (
        jnp.einsum("stud,dv->stuv", hidden_low, output_weight, preferred_element_type=jnp.float32)
        + output_bias
    )
    return (hidden, hidden_low, logits)


def label_logits(logits, label_block):
    chosen = jnp.broadcast_to(label_block[:, None, :, None], logits.shape[:3] + (1,))
    return jnp.take_along_axis(logits, chosen, axis=3)[..., 0]


def assemble(stacked, seq_count, group_size, frame_count, frame_span):
    trailing = stacked.shape[3:]
    shaped = stacked.reshape(
        (seq_count // group_size, frame_count // frame_span, group_size, frame_span) + trailing
    )
    order = (0, 2, 1, 3) + tuple(range(4, 4 + len(trailing)))
    return shaped.transpose(order).reshape((seq_count, frame_count) + trailing)


def exclusive_sum(rows):
    return jnp.concatenate(
        [jnp.zeros_like(rows[..., :1]), jnp.cumsum(rows[..., :-1], axis=-1)], axis=-1
    )


def forward_rows(entry_row, blank_rows, label_rows):

    def forward_frame_step(state_row, frame_row):
        row_blank, row_label = frame_row
        running = exclusive_sum(row_label)
        forward_log = running + lax.cumlogsumexp(state_row - running, axis=state_row.ndim - 1)
        leaving = forward_log + row_blank
        return (leaving, forward_log)

    return lax.scan(forward_frame_step, entry_row, (blank_rows, label_rows))


def backward_rows(incoming, blank_rows, label_rows, frame_times, frame_lens, terminal):
    lens_shaped = frame_lens.reshape((frame_lens.shape[0],) + (1,) * (incoming.ndim - 1))

    def backward_frame_step(state_row, frame_row):
        row_blank, row_label, frame_time = frame_row
        after_row = jnp.where(frame_time >= lens_shaped, VERY_NEGATIVE, state_row)
        after_row = jnp.where(frame_time == lens_shaped - 1, terminal, after_row)
        running = exclusive_sum(row_label)
        backward_log = (
            lax.cumlogsumexp(row_blank + after_row + running, axis=state_row.ndim - 1, reverse=True)
            - running
        )
        return (backward_log, (backward_log, after_row))

    return lax.scan(
        backward_frame_step, incoming, (blank_rows, label_rows, frame_times), reverse=True
    )


def per_device(
    encoder_out,
    encoder_weight,
    encoder_bias,
    predictor_out,
    predictor_weight,
    predictor_bias,
    output_weight,
    output_bias,
    labels,
    frame_lens,
    token_lens,
    loss_scale,
):
    seq_count = labels.shape[0]
    frame_count = encoder_out.shape[1]
    unit_count = predictor_out.shape[1]
    width = encoder_out.shape[2]
    vocab_size = output_weight.shape[1]
    token_place = lax.axis_index("tokens")
    frame_place = lax.axis_index("frames")
    own_frames = (
        jnp.einsum("std,de->ste", encoder_out, encoder_weight, preferred_element_type=jnp.float32)
        + encoder_bias
    ).astype(jnp.bfloat16)
    frame_proj = lax.all_gather(own_frames, "tokens", axis=0, tiled=True)
    own_tokens = (
        jnp.einsum(
            "sud,de->sue", predictor_out, predictor_weight, preferred_element_type=jnp.float32
        )
        + predictor_bias
    ).astype(jnp.bfloat16)
    token_proj = lax.all_gather(own_tokens, "frames", axis=0, tiled=True)
    group_size, frame_span = block_shape(seq_count, frame_count, unit_count)
    block_total = seq_count // group_size * (frame_count // frame_span)
    numbers = jnp.arange(block_total, dtype=jnp.int32)

    def forward_block(block_number):
        frame_block, token_block, label_block, seq_start, frame_start = pick_block(
            block_number, frame_proj, token_proj, labels, group_size, frame_span
        )
        hidden, hidden_low, logits = joint_logits(
            frame_block, token_block, output_weight, output_bias
        )
        log_total = jax.nn.logsumexp(logits, axis=3)
        return (logits[..., 0] - log_total, label_logits(logits, label_block) - log_total)

    blank_parts, label_parts = lax.map(forward_block, numbers)
    blank_local = assemble(blank_parts, seq_count, group_size, frame_count, frame_span)
    label_local = assemble(label_parts, seq_count, group_size, frame_count, frame_span)
    blank_full, label_full = (
        lax.all_gather(blank_local, "tokens", axis=2, tiled=True),
        lax.all_gather(label_local, "tokens", axis=2, tiled=True),
    )
    blank_rows = jnp.transpose(blank_full, (1, 0, 2))
    label_rows = jnp.transpose(label_full, (1, 0, 2))
    column_count = blank_rows.shape[2]
    columns = lax.broadcasted_iota(jnp.int32, (seq_count, column_count), 1)
    anchor_row = jnp.where(columns == 0, 0.0, VERY_NEGATIVE).astype(jnp.float32)
    terminal = jnp.where(columns == token_lens[:, None], 0.0, VERY_NEGATIVE).astype(jnp.float32)
    frame_times = frame_place * frame_count + jnp.arange(frame_count, dtype=jnp.int32)
    frame_chain = lax.axis_size("frames")
    empty_row = jnp.zeros((seq_count, column_count), jnp.float32)
    empty_logs = jnp.zeros((frame_count, seq_count, column_count), jnp.float32)

    def forward_turn(entry_row):
        exit_row, logs = forward_rows(entry_row, blank_rows, label_rows)
        return (logs, exit_row)

    def backward_turn(incoming):
        start_row, kept = backward_rows(
            incoming, blank_rows, label_rows, frame_times, frame_lens, terminal
        )
        return (kept[0], kept[1], start_row)

    def relay_forward(step, state):
        arriving = passed_along(state[1], "frames", 1)
        entry_row = jnp.where(frame_place == 0, anchor_row, arriving)
        return lax.cond(step == frame_place, forward_turn, lambda row: state, entry_row)

    forward_log = lax.fori_loop(0, frame_chain, relay_forward, (empty_logs, empty_row))[0]

    def relay_backward(step, state):
        incoming = passed_along(state[2], "frames", -1)
        return lax.cond(
            step == frame_chain - 1 - frame_place, backward_turn, lambda row: state, incoming
        )

    backward_log, after_rows, unused_row = lax.fori_loop(
        0, frame_chain, relay_backward, (empty_logs, empty_logs, empty_row)
    )
    local_log = jax.nn.logsumexp(forward_log[0] + blank_rows[0] + after_rows[0], axis=1)
    usable = frame_place * frame_count < frame_lens
    log_norm = jnp.where(usable, local_log, 0.0)[None, :, None]
    scale_rows = loss_scale[None, :, None]
    blank_tangent = -scale_rows * jnp.exp(forward_log + blank_rows + after_rows - log_norm)
    right_log = jnp.concatenate(
        [backward_log[..., 1:], jnp.full_like(backward_log[..., :1], VERY_NEGATIVE)], axis=2
    )
    label_tangent = -scale_rows * jnp.exp(forward_log + label_rows + right_log - log_norm)
    blank_own = lax.dynamic_slice_in_dim(
        jnp.transpose(blank_tangent, (1, 0, 2)), token_place * unit_count, unit_count, 2
    )
    label_own = lax.dynamic_slice_in_dim(
        jnp.transpose(label_tangent, (1, 0, 2)), token_place * unit_count, unit_count, 2
    )
    loss_terms = jnp.where(frame_place == 0, -local_log, 0.0)

    def backward_block(sums, block_number):
        frame_block, token_block, label_block, seq_start, frame_start = pick_block(
            block_number, frame_proj, token_proj, labels, group_size, frame_span
        )
        blank_part = lax.dynamic_slice(
            blank_own, (seq_start, frame_start, 0), (group_size, frame_span, unit_count)
        )
        label_part = lax.dynamic_slice(
            label_own, (seq_start, frame_start, 0), (group_size, frame_span, unit_count)
        )
        hidden, hidden_low, logits = joint_logits(
            frame_block, token_block, output_weight, output_bias
        )
        log_total = jax.nn.logsumexp(logits, axis=3)
        softmax_out = jnp.exp(logits - log_total[..., None])
        vocab_ids = lax.broadcasted_iota(jnp.int32, (1, 1, 1, vocab_size), 3)
        logit_tangent = (
            jnp.where(vocab_ids == 0, blank_part[..., None], 0.0)
            + jnp.where(vocab_ids == label_block[:, None, :, None], label_part[..., None], 0.0)
            - softmax_out * (blank_part + label_part)[..., None]
        )
        tangent_low = logit_tangent.astype(jnp.bfloat16)
        hidden_tangent = jnp.einsum(
            "stuv,dv->stud", tangent_low, output_weight, preferred_element_type=jnp.float32
        )
        inner_tangent = hidden_tangent * (1.0 - hidden * hidden)
        weight_sum = sums[0] + jnp.einsum(
            "stud,stuv->dv", hidden_low, tangent_low, preferred_element_type=jnp.float32
        )
        bias_sum = sums[1] + jnp.sum(tangent_low, axis=(0, 1, 2), dtype=jnp.float32)
        return (
            (weight_sum, bias_sum),
            (jnp.sum(inner_tangent, axis=2), jnp.sum(inner_tangent, axis=1)),
        )

    initial = (jnp.zeros((width, vocab_size), jnp.float32), jnp.zeros((vocab_size,), jnp.float32))
    output_sums, block_parts = lax.scan(backward_block, initial, numbers)
    frame_full = assemble(block_parts[0], seq_count, group_size, frame_count, frame_span)
    token_full = block_parts[1].reshape(
        (seq_count // group_size, frame_count // frame_span, group_size, unit_count, width)
    )
    token_full = jnp.sum(token_full, axis=1).reshape((seq_count, unit_count, width))
    frame_tangent = lax.psum_scatter(
        frame_full.astype(jnp.bfloat16), "tokens", scatter_dimension=0, tiled=True
    )
    token_sum, losses = side_by_side(
        (token_full.astype(jnp.bfloat16), loss_terms.astype(jnp.bfloat16)), "frames", 0, 1
    )
    token_tangent = token_sum.astype(jnp.bfloat16)
    encoder_gradient = jnp.einsum(
        "ste,de->std", frame_tangent, encoder_weight, preferred_element_type=jnp.float32
    )
    predictor_gradient = jnp.einsum(
        "sue,de->sud", token_tangent, predictor_weight, preferred_element_type=jnp.float32
    )
    encoder_weight_sum = jnp.einsum(
        "std,ste->de", encoder_out, frame_tangent, preferred_element_type=jnp.float32
    )
    encoder_bias_sum = jnp.sum(frame_tangent, axis=(0, 1), dtype=jnp.float32)
    predictor_weight_sum = jnp.einsum(
        "sud,sue->de", predictor_out, token_tangent, preferred_element_type=jnp.float32
    )
    predictor_bias_sum = jnp.sum(token_tangent, axis=(0, 1), dtype=jnp.float32)
    summed = lax.psum(
        (
            encoder_weight_sum,
            encoder_bias_sum,
            predictor_weight_sum,
            predictor_bias_sum,
            output_sums[0],
            output_sums[1],
        ),
        ("frames", "tokens"),
    )
    return (
        losses,
        encoder_gradient,
        predictor_gradient,
        summed[0],
        summed[1],
        summed[2],
        summed[3],
        summed[4],
        summed[5],
    )


def solution(mesh):
    placed = (
        P("tokens", "frames", None),
        P(),
        P(),
        P("frames", "tokens", None),
        P(),
        P(),
        P(),
        P(),
        P(None, "tokens"),
        P(),
        P(),
        P(),
    )
    return jax.shard_map(
        per_device,
        mesh=mesh,
        in_specs=placed,
        out_specs=(
            P("frames"),
            P("tokens", "frames", None),
            P("frames", "tokens", None),
            P(),
            P(),
            P(),
            P(),
            P(),
            P(),
        ),
        check_vma=False,
    )
```

profile of v0, /device:TPU:0, one launch (start us, length us, event | category | flops | bytes accessed | tf_op | source)
XLA Modules:
  0.0 3625.7 jit_solution(14881816628917838582)
XLA Ops:
  9.4 8.6 all_gather.12
  19.2 30.8 all-gather.1
  50.1 86.6 %while.102 = (s32[]{:T(128)}, f32[4,2,64,6]{2,1,0,3:T(2,128)S(1)}, f32[4,2,64,6]{2,1,0,3:T(2,128)S(1)}, s32[4]{0:T(128)S(1)}, bf16[8,64,512]{2,1,0:T(8,128)(2,1)...) while((s32[]{:T(128)}, f32[4,2,64,6]{2,1,0,3:T(2,128)S(1)}, ...), condition=%wide.region_3.4_spmd, body=%wide.region_0.3_spmd.sunk | while | flops 809337088 | bytes 20839048 | solution.py:173
  57.2 12.7 gather_fusion
  78.6 13.1 gather_fusion
  100.3 13.0 gather_fusion
  122.0 13.1 gather_fusion
  136.7 5.3 all_gather.15
  142.2 5.3 all_gather.14
  149.1 1714.1 %while.104 = (s32[]{:T(128)}, f32[64,8,24]{2,1,0:T(8,128)}, f32[64,8,24]{2,1,0:T(8,128)}, f32[8,24]{1,0:T(8,128)S(1)}, s32[]{:T(128)}, /*index=5*/s32[8]{0:T(128...) while((s32[]{:T(128)}, f32[64,8,24]{2,1,0:T(8,128)}, ...), condition=%wide.region_19.20_spmd.clone, body=%wide.region_12.19_spmd.clone.sunk | while | flops 41199 | bytes 127028 | solution.py:214
  193.8 1459.7 %collective-permute-done = f32[8,24]{1,0:T(8,128)S(1)} collective-permute-done((f32[8,24]{1,0:T(8,128)S(1)}, f32[8,24]{1,0:T(8,128)S(1)}, u32[]{:S(2)}, u32[]{:S(2)}) %collective-permute-start) | collective-permute-done | bytes 800 | tf_op jit(solution)/shard_map/while/body/eval_jaxpr/ppermute | solution.py:14
  1653.6 209.7 %conditional.7 = ((f32[64,8,24]{2,1,0:T(8,128)}, f32[64,8,24]{2,1,0:T(8,128)}, f32[8,24]{1,0:T(8,128)S(1)})) conditional(s32[]{:T(128)} %convert_element_type.203, (f32[64,8,24]{2,1,0:T(8,128)}, f32[64,8,24]{2,1,0:T(8,128)}, f32[8,24]{1,0:T(8,128)S(1)}) %tuple.229, (s32[8]{0:T(128)S(1)}, f32[64,8,24]{2,1,0:T(8,128)S(1)}, s32[]{:T(128)}, ...), branch_computations={%region_13.13_spmd, %region_14.18_spmd.clone} | conditional | flops 41195 | bytes 122681 | solution.py:210
  1655.1 208.2 %while.101 = (s32[]{:T(128)}, f32[8,24]{1,0:T(8,128)S(1)}, f32[64,8,24]{2,1,0:T(8,128)}, f32[64,8,24]{2,1,0:T(8,128)}, f32[64,8,24]{2,1,0:T(8,128)S(1)}, /*index...) while((s32[]{:T(128)}, f32[8,24]{1,0:T(8,128)S(1)}, ...), condition=%wide.region_18.17_spmd, body=%wide.region_15.16_spmd.sunk | while | flops 40747 | bytes 20605 | solution.py:121
  1864.6 780.5 %while.103 = (s32[]{:T(128)}, f32[64,8,24]{2,1,0:T(8,128)}, f32[8,24]{1,0:T(8,128)}, s32[]{:T(128)}, pred[]{:T(512)}, /*index=5*/f32[64,8,24]{2,1,0:T(8,128)S(1)...) while((s32[]{:T(128)}, f32[64,8,24]{2,1,0:T(8,128)}, f32[8,24]{1,0:T(8,128)}, s32[]{:T(128)}, ...), condition=%wide.region_11.12_spmd.clone, body=%wide.region_4.0_spmd.clone.sunk | while | flops 40342 | bytes 21073 | solution.py:206
  1867.4 185.8 %conditional.6 = ((f32[64,8,24]{2,1,0:T(8,128)}, f32[8,24]{1,0:T(8,128)})) conditional(s32[]{:T(128)} %convert_element_type.202, (f32[64,8,24]{2,1,0:T(8,128)}, f32[8,24]{1,0:T(8,128)}) %tuple.226, (pred[]{:T(512)}, f32[24]{0:T(128)S(1)}, f32[8,24]{1,0:T(8,128)S(1)}, f32[64,8,24]{2,1,0:T(8,128)S(1)}, f32[64,8,24]{2,1,0:T(8,128)S(1)}) %tuple.227), branch_computations={%region_5.5_spmd, %region_6.10_spmd} | conditional | flops 40338 | bytes 17798 | solution.py:204
  1868.0 185.3 %while.100 = (s32[]{:T(128)}, f32[8,24]{1,0:T(8,128)}, f32[64,8,24]{2,1,0:T(8,128)}, f32[64,8,24]{2,1,0:T(8,128)S(1)}, f32[64,8,24]{2,1,0:T(8,128)S(1)}, /*index=5*/s32[]{:T(128)}, f32[]{:T(128)}, f32[]{:T(128)}) while((s32[]{:T(128)}, f32[8,24]{1,0:T(8,128)}, f32[64,8,24]{2,1,0:T(8,128)}, f32[64,8,24]{2,1,0:T(8,128)S(1)}, ...), condition=%wide.region_10.9_spmd, body=%wide.region_7.8_spmd.sunk | while | flops 40146 | bytes 16069 | solution.py:104
  2056.0 190.0 %collective-permute-start.1 = (f32[8,24]{1,0:T(8,128)}, f32[8,24]{1,0:T(8,128)S(1)}, u32[]{:S(2)}, u32[]{:S(2)}) collective-permute-start(f32[8,24]{1,0:T(8,128)} %get-tuple-element.1921), channel_id=1, source_target_pairs={{0,4},{4,8},{8,12},{12,16},{16,20},{20,24},{24,28},{1,5},{5,9},{9,... | collective-permute-start | bytes 2312 | tf_op jit(solution)/shard_map/while/body/eval_jaxpr/ppermute | solution.py:14
  2253.3 188.7 %collective-permute-start.1 = (f32[8,24]{1,0:T(8,128)}, f32[8,24]{1,0:T(8,128)S(1)}, u32[]{:S(2)}, u32[]{:S(2)}) collective-permute-start(f32[8,24]{1,0:T(8,128)} %get-tuple-element.1921), channel_id=1, source_target_pairs={{0,4},{4,8},{8,12},{12,16},{16,20},{20,24},{24,28},{1,5},{5,9},{9,... | collective-permute-start | bytes 2312 | tf_op jit(solution)/shard_map/while/body/eval_jaxpr/ppermute | solution.py:14
  2450.1 186.9 %collective-permute-start.1 = (f32[8,24]{1,0:T(8,128)}, f32[8,24]{1,0:T(8,128)S(1)}, u32[]{:S(2)}, u32[]{:S(2)}) collective-permute-start(f32[8,24]{1,0:T(8,128)} %get-tuple-element.1921), channel_id=1, source_target_pairs={{0,4},{4,8},{8,12},{12,16},{16,20},{20,24},{24,28},{1,5},{5,9},{9,... | collective-permute-start | bytes 2312 | tf_op jit(solution)/shard_map/while/body/eval_jaxpr/ppermute | solution.py:14
  2649.7 48.7 %while.105 = (s32[]{:T(128)}, f32[512,1024]{1,0:T(8,128)}, f32[1024]{0:T(1024)S(1)}, bf16[4,2,64,512]{3,2,1,0:T(8,128)(2,1)}, bf16[4,2,6,512]{3,2,1,0:T(8,128)(2...) while((s32[]{:T(128)}, f32[512,1024]{1,0:T(8,128)}, ...), condition=%wide.region_28.29_spmd.clone, body=%wide.region_22.28_spmd.clone.sunk | while | flops 2432714496 | bytes 26478496 | solution.py:270
  2698.8 753.3 %all_to_all.5 = bf16[8,1,3073]{2,1,0:T(2,128)(2,1)S(1)} all-to-all(bf16[8,1,3073]{2,1,0:T(2,128)(2,1)S(1)} %copy.101), channel_id=1, replica_groups=mesh['frames'=8,'tokens'=4] {'frames'}, dimensions={0} | all-to-all | bytes 98336 | tf_op jit(solution)/shard_map/all_to_all | solution.py:24
  3453.7 7.7 reduce-scatter.2.cloned.1.call-done
  3465.5 40.0 %all-reduce.3 = (f32[512]{0:T(512)}, f32[512]{0:T(512)}, f32[1024]{0:T(1024)}) all-reduce(f32[512]{0:T(512)S(1)} %convert_reduce_fusion.1, f32[512]{0:T(512)S(1)} %convert_reduce_fusion.3, f32[1024]{0:T(1024)S(1)} %get-tuple-element.991), channel_id=1, replica_groups=mesh['frames'=8,'tokens'=4] {'frames','tokens'}, use_global_device_ids=true, to_apply=%region_33.34 | all-reduce | flops 2048 | bytes 16384 | tf_op jit(solution)/shard_map/psum | solution.py:297
  3506.5 105.7 %all-reduce.7.cloned.1.call-done = (f32[512,512]{0,1:T(8,128)}, f32[512,512]{0,1:T(8,128)}, f32[512,1024]{1,0:T(8,128)}) async-done(((f32[512,512]{0,1:T(8,128)}, f32[512,512]{0,1:T(8,128)}, f32[512,1024]{1,0:T(8,128)}), (f32[512,512]{0,1:T(8,128)}, f32[512,512]{0,1:T(8,128)}, f32[512,1024]{1,0:T(8,128)})) %all-reduce.7.cloned.1.call-update) | async-done | bytes 4194320 | tf_op jit(solution)/shard_map/psum | solution.py:297
  (1141 shorter events, 569.6 us)
Async XLA Ops:
  7.2 3454.1 %reduce-scatter.2.cloned.1.call-start = ((), (), s32[]{:S(2)}) async-start(), calls=%async_computation.2 | async-start | bytes 655360 | tf_op jit(solution)/shard_map/reduce_scatter | solution.py:276
  50.1 99.1 %copy-start.7 = (s32[8]{0:T(128)S(1)}, s32[8]{0:T(128)}, u32[]{:S(2)}) copy-start(s32[8]{0:T(128)} %param.37) | copy-start | bytes 100
  50.1 99.1 %copy-start.9 = (s32[8]{0:T(128)S(1)}, s32[8]{0:T(128)}, u32[]{:S(2)}) copy-start(s32[8]{0:T(128)} %param.38) | copy-start | bytes 100
  149.1 5.5 collective-permute-start
  154.7 5.9 collective-permute-start
  160.5 6.4 collective-permute-start
  166.9 6.4 collective-permute-start
  173.3 6.4 collective-permute-start
  179.7 6.4 collective-permute-start
  186.1 6.4 collective-permute-start
  192.5 1461.0 %collective-permute-start = (f32[8,24]{1,0:T(8,128)S(1)}, f32[8,24]{1,0:T(8,128)S(1)}, u32[]{:S(2)}, u32[]{:S(2)}) collective-permute-start(f32[8,24]{1,0:T(8,128)S(1)} %get-tuple-element.1891), channel_id=1, source_target_pairs={{4,0},{8,4},{12,8},{16,12},{20,16},{24,20},{28,24},{5,1},{9,5},{13... | collective-permute-start | bytes 2312 | tf_op jit(solution)/shard_map/while/body/eval_jaxpr/ppermute | solution.py:14
  1863.3 784.6 %copy-start.11 = (f32[8]{0:T(128)S(1)}, f32[8]{0:T(128)}, u32[]{:S(2)}) copy-start(f32[8]{0:T(128)} %param.39) | copy-start | bytes 100
  1864.6 2.8 collective-permute-start.1
  2053.2 2.8 collective-permute-start.1
  2056.0 191.5 %collective-permute-start.1 = (f32[8,24]{1,0:T(8,128)}, f32[8,24]{1,0:T(8,128)S(1)}, u32[]{:S(2)}, u32[]{:S(2)}) collective-permute-start(f32[8,24]{1,0:T(8,128)} %get-tuple-element.1921), channel_id=1, source_target_pairs={{0,4},{4,8},{8,12},{12,16},{16,20},{20,24},{24,28},{1,5},{5,9},{9,... | collective-permute-start | bytes 2312 | tf_op jit(solution)/shard_map/while/body/eval_jaxpr/ppermute | solution.py:14
  2247.6 5.7 collective-permute-start.1
  2253.3 190.2 %collective-permute-start.1 = (f32[8,24]{1,0:T(8,128)}, f32[8,24]{1,0:T(8,128)S(1)}, u32[]{:S(2)}, u32[]{:S(2)}) collective-permute-start(f32[8,24]{1,0:T(8,128)} %get-tuple-element.1921), channel_id=1, source_target_pairs={{0,4},{4,8},{8,12},{12,16},{16,20},{20,24},{24,28},{1,5},{5,9},{9,... | collective-permute-start | bytes 2312 | tf_op jit(solution)/shard_map/while/body/eval_jaxpr/ppermute | solution.py:14
  2443.5 6.6 collective-permute-start.1
  2450.1 188.4 %collective-permute-start.1 = (f32[8,24]{1,0:T(8,128)}, f32[8,24]{1,0:T(8,128)S(1)}, u32[]{:S(2)}, u32[]{:S(2)}) collective-permute-start(f32[8,24]{1,0:T(8,128)} %get-tuple-element.1921), channel_id=1, source_target_pairs={{0,4},{4,8},{8,12},{12,16},{16,20},{20,24},{24,28},{1,5},{5,9},{9,... | collective-permute-start | bytes 2312 | tf_op jit(solution)/shard_map/while/body/eval_jaxpr/ppermute | solution.py:14
  2638.5 6.6 collective-permute-start.1
  2649.7 802.7 %copy-start.8 = (bf16[1,6,512]{2,1,0:T(8,128)(2,1)S(1)}, bf16[1,6,512]{2,1,0:T(8,128)(2,1)}, u32[]{:S(2)}) copy-start(bf16[1,6,512]{2,1,0:T(8,128)(2,1)} %param.31) | copy-start | bytes 18436
  2698.4 762.9 %copy-start.5 = (bf16[2,64,512]{2,1,0:T(8,128)(2,1)S(1)}, bf16[2,64,512]{2,1,0:T(8,128)(2,1)}, u32[]{:S(2)}) copy-start(bf16[2,64,512]{2,1,0:T(8,128)(2,1)} %param.28) | copy-start | bytes 393220
  2698.5 913.8 %all-reduce.7.cloned.1.call-start = ((), (), s32[]{:S(2)}) async-start(), calls=%async_computation.3 | async-start | bytes 8388608 | tf_op jit(solution)/shard_map/psum | solution.py:297
  3612.3 5.2 copy-start.2
  (12 other events, 29.8 us)
Sparse Core Ops, SparseCore 0:
  2698.6 762.6 reduce-scatter.1
  3468.7 143.5 all-reduce.6
where the time goes:
time: 3630 us
  waiting for transfers between devices  1620 us (45%)
  blocking collectives  844 us (23%)
  starting transfers between devices  593 us (16%)
  other arithmetic  369 us (10%)
  local copies, waits for them, and re-layouts  134 us (4%)
  matrix products  44.7 us (1%)
    ppermute x16, waiting for transfers between devices, passed_along(): return lax.ppermute(array, axis, pairs)  1510 us
    all_to_all x1, blocking collectives, sent_and_summed(): lax.all_to_all(cut_along(array, dim, count), axis, 0, 0, tiled=True)  753 us
    ppermute x16, starting transfers between devices, passed_along(): return lax.ppermute(array, axis, pairs)  593 us
    psum x1, waiting for transfers between devices, per_device(): lax.psum((encoder_weight_sum, encoder_bias_sum, predictor_weight_sum, pre...  106 us
    dynamic_update_slice x128, other arithmetic, forward_rows(): return lax.scan(forward_frame_step, entry_row, (blank_rows, label_rows))  85.7 us
  transfers between devices with their start and end apart: 18, of which 18 were waited for; matrix products, arithmetic and copies ran while one was open for 0% of the time, Pallas kernels for 0%

commit v1 on v0

v1 whole, which is shorter than its diff:
```python
import functools

import jax
import jax.numpy as jnp
from jax import lax
from jax.experimental import pallas as pl
from jax.experimental.pallas import tpu as pltpu
from jax.sharding import PartitionSpec as P

NEG = -1e30
LOG2E = 1.4426950408889634
LN2 = 0.6931471805599453
BF16 = jnp.bfloat16
F32 = jnp.float32
GROUP = 32
SUB_UNITS = 4
AXES = ("frames", "tokens")


def lane_ids(rows):
    return lax.broadcasted_iota(jnp.int32, (rows, 128), 1)


def log2_add(a, b):
    return jnp.maximum(a, b) + jnp.log2(1.0 + jnp.exp2(-jnp.abs(a - b)))


def both_ways(blank_ref, label_ref, units, steps, ahead, behind, keep=None):
    def one_step(i, state):
        ahead, behind = state
        back = steps - 1 - i
        here = pl.ds(pl.multiple_of(i * units, 8), units)
        there = pl.ds(pl.multiple_of(back * units, 8), units)
        if keep is not None:
            keep[0][here, :] = ahead
            keep[1][there, :] = behind
        from_left = pltpu.roll(ahead + label_ref[here, :], 1, 0)
        to_right = pltpu.roll(behind, units - 1, 0) + label_ref[there, :]
        ahead = log2_add(ahead + blank_ref[here, :], from_left)
        behind = log2_add(behind + blank_ref[there, :], to_right)
        return ahead, behind

    return lax.fori_loop(0, steps, one_step, (ahead, behind))


def packet_kernel(predictor_ref, labels_ref, packets_ref):
    seqs, units = labels_ref.shape
    width = packets_ref.shape[2]
    flat = jnp.zeros((1, width), F32)
    for s in range(seqs):
        row = labels_ref[s : s + 1, :].astype(F32)
        row = jnp.concatenate([row, jnp.zeros((1, width - units), F32)], axis=1)
        flat = flat + (pltpu.roll(row, s * units, 1) if s else row)
    high = jnp.floor(flat * (1.0 / 32.0))
    packet = jnp.concatenate(
        [predictor_ref[...].astype(F32), high, flat - high * 32.0], axis=0
    ).astype(BF16)
    for d in range(packets_ref.shape[0]):
        packets_ref[d] = packet


def block_counts(lens_ref, tokens_ref, first_seq, first_frame):
    counts = []
    for s in range(2):
        inside = first_frame < lens_ref[first_seq + s]
        counts.append(jnp.where(inside, tokens_ref[first_seq + s] // SUB_UNITS + 1, 0))
    return counts


def score_kernel(
    seqs_here,
    offset_ref,
    packets_ref,
    lens_hbm,
    tokens_hbm,
    encoder_hbm,
    encoder_weight_hbm,
    encoder_bias_hbm,
    predictor_weight_hbm,
    predictor_bias_hbm,
    weight_hbm,
    bias_hbm,
    softmax_ref,
    frame_ref,
    token_ref,
    label_table_ref,
    blank_ref,
    label_ref,
    encoder_ref,
    encoder_weight_ref,
    predictor_weight_ref,
    weight_ref,
    matrix_ref,
    label_rows_ref,
    encoder_bias_ref,
    predictor_bias_ref,
    bias_ref,
    lens_ref,
    tokens_ref,
    load_sems,
):
    loads = [
        pltpu.make_async_copy(source, target, load_sems.at[n])
        for n, (source, target) in enumerate(
            (
                (predictor_weight_hbm, predictor_weight_ref),
                (predictor_bias_hbm, predictor_bias_ref),
                (encoder_hbm, encoder_ref),
                (encoder_weight_hbm, encoder_weight_ref),
                (encoder_bias_hbm, encoder_bias_ref),
                (weight_hbm, weight_ref),
                (bias_hbm, bias_ref),
                (lens_hbm, lens_ref),
                (tokens_hbm, tokens_ref),
            )
        )
    ]
    for load in loads:
        load.start()
    seqs, frame_count, width = encoder_ref.shape
    units = token_ref.shape[0] // seqs
    shards = label_rows_ref.shape[0]
    shard_units = units // shards
    steps = frame_count + units - 1
    first_frame = lax.axis_index("frames") * frame_count
    first_seq = lax.axis_index("tokens") * seqs_here + offset_ref[0]
    vocab = weight_ref.shape[1]
    blank_ref[...] = jnp.zeros_like(blank_ref)
    label_ref[...] = jnp.full(label_ref.shape, NEG, F32)
    for s in range(seqs):
        for k in range(shards):
            rows = packets_ref[(first_seq + s) * shards + k]
            at = s * units + k * shard_units
            token_ref[at : at + shard_units, :] = rows[:shard_units].astype(F32)
    for k in range(shards):
        halves = packets_ref[k, shard_units:, :].astype(F32)
        label_rows_ref[k : k + 1, :] = halves[:1] * 32.0 + halves[1:2]
    loads[0].wait()
    loads[1].wait()
    token_ref[...] = (
        jnp.dot(token_ref[...].astype(BF16), predictor_weight_ref[...], preferred_element_type=F32)
        + predictor_bias_ref[...]
    ).astype(BF16).astype(F32)
    wide = lax.broadcasted_iota(jnp.int32, (1, width), 1)
    for s in range(seqs):
        for u in range(units):
            lane = (first_seq + s) * shard_units + u % shard_units
            row = label_rows_ref[u // shard_units : u // shard_units + 1, :]
            value = jnp.sum(jnp.where(wide == lane, row, 0.0), axis=1, keepdims=True)
            label_table_ref[s * units + u : s * units + u + 1, :] = jnp.broadcast_to(
                value, (1, 128)
            ).astype(jnp.int32)
    loads[2].wait()
    loads[3].wait()
    loads[4].wait()
    frame_ref[...] = (
        (
            jnp.dot(
                encoder_ref[...].reshape(seqs * frame_count, width),
                encoder_weight_ref[...],
                preferred_element_type=F32,
            )
            + encoder_bias_ref[...]
        )
        .astype(BF16)
        .astype(F32)
        .reshape(frame_ref.shape)
    )
    for load in loads[5:]:
        load.wait()

    counts = block_counts(lens_ref, tokens_ref, first_seq, first_frame)
    lanes = lane_ids(frame_count)
    vocab_ids = lax.broadcasted_iota(jnp.int32, (frame_count, vocab), 1)
    times = first_frame + lax.broadcasted_iota(jnp.int32, (frame_count, 1), 0)

    def one_block(i, _):
        seq = jnp.where(i >= counts[0], 1, 0)
        sub = i - seq * counts[0]
        first_unit = sub * SUB_UNITS
        seq_len = lens_ref[first_seq + seq]
        last_unit = tokens_ref[first_seq + seq]
        own_lanes = (lanes // GROUP) % 2 == seq
        frames = frame_ref[seq]
        hidden = jnp.concatenate(
            [
                jnp.tanh(frames + token_ref[pl.ds(seq * units + first_unit + j, 1), :])
                for j in range(SUB_UNITS)
            ],
            axis=0,
        ).astype(BF16)
        logits = jnp.dot(hidden, weight_ref[...], preferred_element_type=F32) + bias_ref[...]
        top = jnp.max(logits, axis=1, keepdims=True)
        weights = jnp.exp(logits - top)
        total = jnp.sum(weights, axis=1, keepdims=True)
        softmax_ref[seq * (units // SUB_UNITS) + sub] = weights * (1.0 / total)
        log_total = top + jnp.log(total)
        blanks = (logits[:, :1] - log_total) * LOG2E
        for j in range(SUB_UNITS):
            unit = first_unit + j
            rows = slice(j * frame_count, (j + 1) * frame_count)
            label = label_table_ref[pl.ds(seq * units + unit, 1), :]
            label = jnp.concatenate([label] * (vocab // 128), axis=1)
            picked = jnp.sum(
                jnp.where(vocab_ids == label, logits[rows], 0.0), axis=1, keepdims=True
            )
            blank = blanks[rows]
            blank = jnp.where((times == seq_len - 1) & (unit < last_unit), NEG, blank)
            blank = jnp.where((times >= seq_len) | (unit > last_unit), 0.0, blank)
            step = jnp.where(
                (times >= seq_len) | (unit >= last_unit),
                NEG,
                (picked - log_total[rows]) * LOG2E,
            )
            at = (pl.ds(unit * (units + 1), frame_count, stride=units), slice(None))
            blank_ref[at] = jnp.where(own_lanes, blank, blank_ref[at])
            label_ref[at] = jnp.where(own_lanes, step, label_ref[at])
        return 0

    lax.fori_loop(0, counts[0] + counts[1], one_block, 0)
    eye = jnp.where(
        lane_ids(units) % GROUP == lax.broadcasted_iota(jnp.int32, (units, 128), 0), 0.0, NEG
    ).astype(F32)
    ahead, behind = both_ways(blank_ref, label_ref, units, steps, eye, eye)
    matrix_ref[0, 0] = jnp.where(lane_ids(units) < 64, behind, ahead)


def tangent_kernel(
    layout,
    lens_ref,
    tokens_ref,
    offset_ref,
    scale_ref,
    softmax_ref,
    frame_ref,
    token_ref,
    label_table_ref,
    blank_ref,
    label_ref,
    encoder_ref,
    encoder_weight_ref,
    weight_ref,
    *refs,
):
    hops = layout["hops"]
    matrix_refs, refs = refs[: hops + 1], refs[hops + 1 :]
    (
        encoder_gradient_ref,
        kept_ref,
        sent_ref,
        sums_ref,
        matrices_ref,
        ahead_ref,
        behind_ref,
        blank_part_ref,
        label_part_ref,
        frame_sum_ref,
        token_sum_ref,
        output_bias_ref,
        kept_sem,
        sent_sem,
    ) = refs
    seqs, frame_count, width = frame_ref.shape
    units = token_ref.shape[0] // seqs
    steps = frame_count + units - 1
    here = lax.axis_index("frames")
    first_frame = here * frame_count
    first_seq = lax.axis_index("tokens") * layout["seqs_here"] + offset_ref[0]
    chunks = matrices_ref.shape[0]
    vocab = weight_ref.shape[1]
    sums_ref[...] = jnp.zeros_like(sums_ref)
    output_bias_ref[...] = jnp.zeros_like(output_bias_ref)
    token_sum_ref[...] = jnp.zeros_like(token_sum_ref)
    frame_sum_ref[...] = jnp.zeros_like(frame_sum_ref)
    at = 0
    for matrix_ref in matrix_refs:
        matrices_ref[at : at + matrix_ref.shape[0]] = matrix_ref[:, 0]
        at += matrix_ref.shape[0]
    starts = lax.broadcasted_iota(jnp.int32, (units, 128), 0)
    lanes = lane_ids(units)
    early = lanes < 64
    gather_ids = lanes // GROUP * GROUP + starts
    own_first = (lane_ids(1) // GROUP) % 2 == 0

    def one_chunk(i, carry):
        column, kept = carry
        other = chunks - 1 - i
        kept = jnp.where(jnp.where(early, i, other) == here, column, kept)
        joined = column + jnp.where(early, matrices_ref[here ^ i], matrices_ref[here ^ other])
        top = jnp.max(joined, axis=0, keepdims=True)
        row = top + jnp.log2(jnp.sum(jnp.exp2(joined - top), axis=0, keepdims=True))
        row = jnp.broadcast_to(row, (units, 128))
        return jnp.take_along_axis(row, gather_ids, axis=1, mode="promise_in_bounds"), kept

    start = jnp.where(early & (starts > 0), NEG, 0.0).astype(F32)
    last, kept = lax.fori_loop(0, chunks, one_chunk, (start, start))
    swapped_halves = pltpu.roll(kept, 64, 1)
    both_ways(
        blank_ref,
        label_ref,
        units,
        steps,
        jnp.where(early, kept, swapped_halves),
        jnp.where(early, swapped_halves, kept),
        (ahead_ref, behind_ref),
    )
    log_norm = jnp.max(jnp.where(early, last, pltpu.roll(last, 64, 1)), axis=0, keepdims=True)
    scale = jnp.where(own_first, scale_ref[first_seq], scale_ref[first_seq + 1])
    length = jnp.where(own_first, lens_ref[first_seq], lens_ref[first_seq + 1])
    bound = jnp.where(own_first, tokens_ref[first_seq], tokens_ref[first_seq + 1])
    time_limit = jnp.minimum(length - first_frame, frame_count)

    def one_diagonal(e, _):
        rows = pl.ds(pl.multiple_of(e * units, 8), units)
        time = e - starts
        behind = behind_ref[rows, :]
        base = ahead_ref[rows, :] - log_norm
        live = (starts <= bound) & (time >= 0) & (time < time_limit)
        blank_part_ref[rows, :] = jnp.where(
            live, -scale * jnp.exp2(base + blank_ref[rows, :] + behind), 0.0
        )
        label_part_ref[rows, :] = jnp.where(
            live & (starts < bound),
            -scale * jnp.exp2(base + label_ref[rows, :] + pltpu.roll(behind, units - 1, 0)),
            0.0,
        )
        return 0

    lax.fori_loop(0, steps, one_diagonal, 0, unroll=3)

    counts = block_counts(lens_ref, tokens_ref, first_seq, first_frame)
    block_lanes = lane_ids(frame_count)

    def one_block(i, _):
        seq = jnp.where(i >= counts[0], 1, 0)
        sub = i - seq * counts[0]
        first_unit = sub * SUB_UNITS
        own_lanes = (block_lanes // GROUP) % 2 == seq
        frames = frame_ref[seq]
        block = seq * (units // SUB_UNITS) + sub
        hiddens, tangents = [], []
        for j in range(SUB_UNITS):
            unit = first_unit + j
            rows = slice(j * frame_count, (j + 1) * frame_count)
            hiddens.append(jnp.tanh(frames + token_ref[pl.ds(seq * units + unit, 1), :]))
            at = (pl.ds(unit * (units + 1), frame_count, stride=units), slice(None))
            blank, step = blank_part_ref[at], label_part_ref[at]
            blank = jnp.where(own_lanes, blank, pltpu.roll(blank, GROUP, 1))
            step = jnp.where(own_lanes, step, pltpu.roll(step, GROUP, 1))
            label = label_table_ref[pl.ds(seq * units + unit, 1), :]
            both = -(blank + step)
            pieces = []
            for v in range(vocab // 128):
                piece = softmax_ref[block, rows, v * 128 : (v + 1) * 128] * both
                if v == 0:
                    piece = piece + jnp.where(block_lanes == 0, blank, 0.0)
                piece = piece + jnp.where(block_lanes + v * 128 == label, step, 0.0)
                pieces.append(piece.astype(BF16))
            tangents.append(jnp.concatenate(pieces, axis=1))
        hidden = jnp.concatenate(hiddens, axis=0)
        low = hidden.astype(BF16)
        tangent = jnp.concatenate(tangents, axis=0)
        product = lax.dot_general(
            low, tangent, (((0,), (0,)), ((), ())), preferred_element_type=F32
        )
        for v in range(vocab // 128):
            sums_ref[v * width : (v + 1) * width, :] += product[:, v * 128 : (v + 1) * 128]
        output_bias_ref[...] += jnp.sum(tangent.astype(F32), axis=0, keepdims=True)
        inner = lax.dot_general(
            tangent, weight_ref[...], (((1,), (1,)), ((), ())), preferred_element_type=F32
        ) * (1.0 - hidden * hidden)
        total = frame_sum_ref[seq]
        for j in range(SUB_UNITS):
            rows = slice(j * frame_count, (j + 1) * frame_count)
            total = total + inner[rows]
            token_sum_ref[pl.ds(seq * units + first_unit + j, 1), :] = jnp.sum(
                inner[rows], axis=0, keepdims=True
            )
        frame_sum_ref[seq] = total
        return 0

    lax.fori_loop(0, counts[0] + counts[1], one_block, 0)

    low = frame_sum_ref[...].reshape(seqs * frame_count, width).astype(BF16)
    encoder_gradient_ref[...] = lax.dot_general(
        low, encoder_weight_ref[...], (((1,), (1,)), ((), ())), preferred_element_type=F32
    ).reshape(encoder_gradient_ref.shape)
    product = lax.dot_general(
        encoder_ref[...].reshape(seqs * frame_count, width),
        low,
        (((0,), (0,)), ((), ())),
        preferred_element_type=F32,
    )
    encoder_bias = jnp.sum(low.astype(F32), axis=0, keepdims=True)
    for v in range(width // 128):
        cut = slice(v * 128, (v + 1) * 128)
        at = layout["encoder"] + v * width
        sums_ref[at : at + width, :] = product[:, cut]
        at = layout["token"] + v * layout["token_rows"] + first_seq * units
        sums_ref[pl.ds(pl.multiple_of(at, 8), seqs * units), :] = token_sum_ref[:, cut]
        at = layout["encoder_bias"] + v
        sums_ref[at : at + 1, :] = encoder_bias[:, cut]
    for v in range(vocab // 128):
        at = layout["output_bias"] + v
        sums_ref[at : at + 1, :] = output_bias_ref[:, v * 128 : (v + 1) * 128]
    wide = lane_ids(1)
    loss = jnp.where(here == 0, -log_norm * LN2, 0.0)
    spread = jnp.where(wide == first_seq, loss[:, :1], 0.0)
    spread = spread + jnp.where(wide == first_seq + 1, loss[:, GROUP : GROUP + 1], 0.0)
    for k in range(3):
        part = spread.astype(BF16).astype(F32)
        sums_ref[layout["loss"] + k : layout["loss"] + k + 1, :] = part
        spread = spread - part
    half = sums_ref.shape[0] // 2
    place = lax.axis_index("tokens") & 1
    keep = pltpu.make_async_copy(
        sums_ref.at[pl.ds(pl.multiple_of(place * half, 8), half), :], kept_ref, kept_sem
    )
    send = pltpu.make_async_copy(
        sums_ref.at[pl.ds(pl.multiple_of((1 - place) * half, 8), half), :], sent_ref, sent_sem
    )
    send.start()
    keep.start()
    send.wait()
    keep.wait()


def halve_kernel(stage, kept_ref, received_ref, next_ref, sent_ref):
    even, odd = stage
    f, k = lax.axis_index("frames"), lax.axis_index("tokens")
    upper = jnp.where((k & 1) == 0, (f & even[0]) | (k & even[1]), (f & odd[0]) | (k & odd[1]))
    half = next_ref.shape[0]
    own = pl.ds(pl.multiple_of(jnp.where(upper != 0, half, 0), 16), half)
    other = pl.ds(pl.multiple_of(jnp.where(upper != 0, 0, half), 16), half)
    sent_ref[...] = (kept_ref[other, :] + received_ref[other, :].astype(F32)).astype(sent_ref.dtype)
    next_ref[...] = kept_ref[own, :] + received_ref[own, :].astype(F32)


def finish_kernel(
    layout,
    own_ref,
    other_ref,
    packets_ref,
    predictor_weight_ref,
    output_weight_ref,
    output_bias_ref,
    encoder_weight_ref,
    encoder_bias_ref,
    weight_gradient_ref,
    bias_gradient_ref,
    predictor_gradient_ref,
    losses_ref,
    full_ref,
    tokens_ref,
    predictor_ref,
    own_sem,
    other_sem,
):
    half = own_ref.shape[0]
    width, vocab = output_weight_ref.shape
    place = lax.axis_index("tokens") & 1
    own = pltpu.make_async_copy(
        own_ref, full_ref.at[pl.ds(pl.multiple_of(place * half, 16), half), :], own_sem
    )
    other = pltpu.make_async_copy(
        other_ref, full_ref.at[pl.ds(pl.multiple_of((1 - place) * half, 16), half), :], other_sem
    )
    own.start()
    other.start()
    own.wait()
    other.wait()
    for v in range(vocab // 128):
        output_weight_ref[:, v * 128 : (v + 1) * 128] = full_ref[
            v * width : (v + 1) * width, :
        ].astype(F32)
    for v in range(width // 128):
        at = layout["encoder"] + v * width
        encoder_weight_ref[:, v * 128 : (v + 1) * 128] = full_ref[at : at + width, :].astype(F32)
    rest = full_ref[layout["misc"] :, :].astype(F32)

    def row(name, k):
        at = layout[name] - layout["misc"] + k
        return rest[at : at + 1, :]

    output_bias_ref[...] = jnp.concatenate(
        [row("output_bias", v) for v in range(vocab // 128)], axis=1
    )
    encoder_bias_ref[...] = jnp.concatenate(
        [row("encoder_bias", v) for v in range(width // 128)], axis=1
    )
    count = layout["token_rows"]
    tokens = jnp.concatenate(
        [
            full_ref[layout["token"] + v * count : layout["token"] + (v + 1) * count, :]
            for v in range(width // 128)
        ],
        axis=1,
    )
    held_rows = packets_ref.shape[1] - 2
    for d in range(packets_ref.shape[0]):
        predictor_ref[d * held_rows : (d + 1) * held_rows, :] = packets_ref[
            d, :held_rows, :
        ].astype(F32)
    weight_gradient_ref[...] = lax.dot_general(
        predictor_ref[...].astype(BF16), tokens, (((0,), (0,)), ((), ())), preferred_element_type=F32
    )
    wide = tokens.astype(F32)
    bias_gradient_ref[...] = jnp.sum(wide, axis=0, keepdims=True)
    tokens_ref[...] = wide
    device = lax.axis_index("frames") * lax.axis_size("tokens") + lax.axis_index("tokens")
    mine = jnp.concatenate(
        [tokens_ref[pl.ds(device * held_rows + r, 1), :] for r in range(held_rows)], axis=0
    )
    predictor_gradient_ref[...] = lax.dot_general(
        mine.astype(BF16),
        predictor_weight_ref[...],
        (((1,), (1,)), ((), ())),
        preferred_element_type=F32,
    )
    loss = row("loss", 0) + row("loss", 1) + row("loss", 2)
    losses_ref[...] = jnp.sum(
        jnp.where(lane_ids(1) == lax.axis_index("frames"), loss, 0.0), axis=1, keepdims=True
    )


def in_hbm(array):
    return pltpu.with_memory_space_constraint(array, pltpu.HBM)


def in_vmem(array):
    return pltpu.with_memory_space_constraint(array, pltpu.VMEM)


def permuted(array, partner):
    frames, tokens = lax.axis_size("frames"), lax.axis_size("tokens")
    pairs = []
    for f in range(frames):
        for k in range(tokens):
            g, h = partner(f, k)
            pairs.append((f * tokens + k, g * tokens + h))
    return lax.ppermute(array, AXES, pairs)


def doubled(array):
    blocks, bit = [array], 1
    while bit < lax.axis_size("frames"):
        joined = jnp.concatenate(blocks, axis=0) if len(blocks) > 1 else blocks[0]
        blocks.append(permuted(joined, lambda f, k: (f ^ bit, k)))
        bit *= 2
    return blocks


def stages():
    frame_bits = [(1 << i, 0) for i in range(lax.axis_size("frames").bit_length() - 1)]
    token_bits = [(0, 1 << i) for i in range(1, lax.axis_size("tokens").bit_length() - 1)]
    if len(frame_bits) < 2 or not token_bits:
        order = token_bits + frame_bits
        return list(zip(order, order))
    x, z, y = frame_bits[0], frame_bits[1], token_bits[0]
    rest = frame_bits[2:] + token_bits[1:]
    return list(zip([x, y, z] + rest, [z, x, y] + rest))


def is_upper(stage):
    f, k = lax.axis_index("frames"), lax.axis_index("tokens")
    even, odd = stage
    return jnp.where(
        (k & 1) == 0, (f & even[0]) | (k & even[1]), (f & odd[0]) | (k & odd[1])
    ) != 0


def across(stage):
    even, odd = stage
    return lambda f, k: (f ^ (odd if k & 1 else even)[0], k ^ (odd if k & 1 else even)[1])


def reduced_and_gathered(kept, sent):
    neighbour = lambda f, k: (f, k ^ 1)
    received = permuted(sent, neighbour)
    plan = stages()
    for number, stage in enumerate(plan):
        half = kept.shape[0] // 2
        kept, sent = pl.pallas_call(
            functools.partial(halve_kernel, stage),
            in_specs=[pl.BlockSpec(memory_space=pltpu.VMEM)] * 2,
            out_specs=[pl.BlockSpec(memory_space=pltpu.VMEM)] * 2,
            out_shape=[
                pltpu.VMEM((half, 128), F32),
                pltpu.VMEM((half, 128), BF16 if number < 2 else F32),
            ],
            compiler_params=pltpu.CompilerParams(vmem_limit_bytes=4 * 2**20),
        )(in_vmem(kept), in_vmem(received))
        received = permuted(sent, across(stage))
    array = (kept + received).astype(BF16)
    for stage in reversed(plan):
        upper = is_upper(stage)
        other = permuted(array, across(stage))
        array = jnp.where(
            upper, jnp.concatenate([other, array]), jnp.concatenate([array, other])
        )
    return array, permuted(array, neighbour)


def per_device(
    encoder_out,
    encoder_weight,
    encoder_bias,
    predictor_out,
    predictor_weight,
    predictor_bias,
    output_weight,
    output_bias,
    labels,
    frame_lens,
    token_lens,
    loss_scale,
):
    seq_count, frame_count, width = encoder_out.shape
    vocab = output_weight.shape[1]
    all_seqs = labels.shape[0]
    held_seqs, held_units = predictor_out.shape[:2]
    assert held_seqs == 1
    frame_axis, token_axis = lax.axis_size("frames"), lax.axis_size("tokens")
    device_count = frame_axis * token_axis
    units = held_units * token_axis
    calls = seq_count // 2
    steps = frame_count + units - 1
    diagonals = (steps + 1) * units
    smem = pl.BlockSpec(memory_space=pltpu.SMEM)
    vmem = pl.BlockSpec(memory_space=pltpu.VMEM)
    anywhere = pl.BlockSpec(memory_space=pl.ANY)
    params = pltpu.CompilerParams(vmem_limit_bytes=28 * 2**20)

    packets = pl.pallas_call(
        packet_kernel,
        in_specs=[vmem] * 2,
        out_specs=vmem,
        out_shape=jax.ShapeDtypeStruct((device_count, held_units + 2, width), BF16),
    )(predictor_out.reshape(held_units, width), labels)
    packets = lax.all_to_all(packets, AXES, 0, 0, tiled=True)

    score_shapes = [
        ((2 * units // SUB_UNITS, SUB_UNITS * frame_count, vocab), F32),
        ((2, frame_count, width), F32),
        ((2 * units, width), F32),
        ((2 * units, 128), jnp.int32),
        ((diagonals, 128), F32),
        ((diagonals, 128), F32),
        ((2, frame_count, width), BF16),
        ((width, width), BF16),
        ((width, width), BF16),
        ((width, vocab), BF16),
        ((1, 1, units, 128), F32),
    ]

    def scores(given):
        offset, encoder = given
        return pl.pallas_call(
            functools.partial(score_kernel, seq_count),
            in_specs=[smem, vmem] + [anywhere] * 9,
            out_specs=[vmem] * len(score_shapes),
            out_shape=[pltpu.VMEM(s, t) for s, t in score_shapes],
            scratch_shapes=[
                pltpu.VMEM((token_axis, width), F32),
                pltpu.VMEM((1, width), F32),
                pltpu.VMEM((1, width), F32),
                pltpu.VMEM((1, vocab), F32),
                pltpu.SMEM(frame_lens.shape, jnp.int32),
                pltpu.SMEM(token_lens.shape, jnp.int32),
                pltpu.SemaphoreType.DMA((9,)),
            ],
            compiler_params=params,
        )(
            offset,
            in_vmem(packets),
            *map(
                in_hbm,
                (
                    frame_lens,
                    token_lens,
                    encoder,
                    encoder_weight,
                    encoder_bias.reshape(1, width),
                    predictor_weight,
                    predictor_bias.reshape(1, width),
                    output_weight,
                    output_bias.reshape(1, vocab),
                ),
            ),
        )

    offsets = 2 * jnp.arange(calls, dtype=jnp.int32).reshape(calls, 1)
    encoders = encoder_out.reshape(calls, 2, frame_count, width)
    if calls == 1:
        scored = scores((offsets[0], encoder_out))
        matrix = scored[-1]
    else:
        scored = lax.map(scores, (offsets, encoders))
        matrix = scored[-1].reshape(1, calls, units, 128)

    for_tangents = lambda scored: [*scored[:8], scored[9]]
    matrices = doubled(matrix)
    layout = {"seqs_here": seq_count}
    at = vocab // 128 * width
    layout["encoder"] = at
    at += width // 128 * width
    layout["token"], layout["token_rows"] = at, all_seqs * units
    at += width // 128 * all_seqs * units
    layout["misc"] = layout["output_bias"] = at
    at += vocab // 128
    layout["encoder_bias"] = at
    at += width // 128
    layout["loss"] = at
    at += 3
    rows = at + (-at % (16 * device_count))

    def tangents(given):
        offset, scored, matrices = given
        return pl.pallas_call(
            functools.partial(tangent_kernel, dict(layout, hops=len(matrices) - 1)),
            in_specs=[smem] * 4 + [vmem] * (9 + len(matrices)),
            out_specs=[vmem] * 3,
            out_shape=[
                jax.ShapeDtypeStruct((2, frame_count, width), F32),
                pltpu.VMEM((rows // 2, 128), F32),
                pltpu.VMEM((rows // 2, 128), F32),
            ],
            scratch_shapes=[
                pltpu.VMEM((rows, 128), F32),
                pltpu.VMEM((frame_axis, units, 128), F32),
                pltpu.VMEM((diagonals, 128), F32),
                pltpu.VMEM((diagonals, 128), F32),
                pltpu.VMEM((diagonals, 128), F32),
                pltpu.VMEM((diagonals, 128), F32),
                pltpu.VMEM((2, frame_count, width), F32),
                pltpu.VMEM((2 * units, width), F32),
                pltpu.VMEM((1, vocab), F32),
                pltpu.SemaphoreType.DMA,
                pltpu.SemaphoreType.DMA,
            ],
            compiler_params=params,
        )(
            frame_lens,
            token_lens,
            offset,
            loss_scale,
            *map(in_vmem, (*scored, *matrices)),
        )

    if calls == 1:
        encoder_gradient, kept, sent = tangents((offsets[0], for_tangents(scored), matrices))
    else:

        def add_call(sums, given):
            offset, scored, call = given
            own = [lax.dynamic_slice_in_dim(m, call, 1, 1) for m in matrices]
            gradient, kept, sent = tangents((offset, scored, own))
            return (sums[0] + kept, sums[1] + sent), gradient

        nothing = jnp.zeros((rows // 2, 128), F32)
        (kept, sent), encoder_gradient = lax.scan(
            add_call, (nothing, nothing), (offsets, for_tangents(scored), jnp.arange(calls))
        )
        encoder_gradient = encoder_gradient.reshape(encoder_out.shape)

    own, other = reduced_and_gathered(kept, sent)
    finished = pl.pallas_call(
        functools.partial(finish_kernel, layout),
        in_specs=[anywhere, anywhere, vmem, vmem],
        out_specs=[vmem] * 8,
        out_shape=[
            jax.ShapeDtypeStruct((width, vocab), F32),
            jax.ShapeDtypeStruct((1, vocab), F32),
            jax.ShapeDtypeStruct((width, width), F32),
            jax.ShapeDtypeStruct((1, width), F32),
            jax.ShapeDtypeStruct((width, width), F32),
            jax.ShapeDtypeStruct((1, width), F32),
            jax.ShapeDtypeStruct((held_units, width), F32),
            jax.ShapeDtypeStruct((1, 1), F32),
        ],
        scratch_shapes=[
            pltpu.VMEM((rows, 128), BF16),
            pltpu.VMEM((all_seqs * units, width), F32),
            pltpu.VMEM((all_seqs * units, width), F32),
            pltpu.SemaphoreType.DMA,
            pltpu.SemaphoreType.DMA,
        ],
        compiler_params=params,
    )(own, other, packets, in_vmem(scored[8]) if calls == 1 else predictor_weight)
    return (
        finished[7].reshape(1),
        encoder_gradient,
        finished[6].reshape(1, held_units, width),
        finished[2],
        finished[3].reshape(width),
        finished[4],
        finished[5].reshape(width),
        finished[0],
        finished[1].reshape(vocab),
    )


def solution(mesh):
    placed = (
        P("tokens", "frames", None),
        P(),
        P(),
        P("frames", "tokens", None),
        P(),
        P(),
        P(),
        P(),
        P(None, "tokens"),
        P(),
        P(),
        P(),
    )
    return jax.shard_map(
        per_device,
        mesh=mesh,
        in_specs=placed,
        out_specs=(
            P("frames"),
            P("tokens", "frames", None),
            P("frames", "tokens", None),
            P(),
            P(),
            P(),
            P(),
            P(),
            P(),
        ),
        check_vma=False,
    )
```

time: 3630 us -> 121 us (0.03)
  waiting for transfers between devices: 1620 us -> 70.2 us
  blocking collectives: 844 us -> 17.9 us
  starting transfers between devices: 593 us -> 4.87 us
  other arithmetic: 369 us -> 0.48 us
  local copies, waits for them, and re-layouts: 134 us -> 0.63 us
  matrix products: 44.7 us -> 0 us
    ppermute x16 -> x13, waiting for transfers between devices: 1510 us -> 70.2 us  [permuted(): return lax.ppermute(array, AXES, pairs)]
    all_to_all x1, blocking collectives: 753 us -> 17.9 us  [per_device(): packets = lax.all_to_all(packets, AXES, 0, 0, tiled=True)]
    ppermute x16 -> x13, starting transfers between devices: 593 us -> 4.87 us  [permuted(): return lax.ppermute(array, AXES, pairs)]
    another operation x259 -> x0, other arithmetic: 121 us -> none  [the longest x64 60.1 us: backward_frame_step(): lax.cumlogsumexp(row_blank + after_row + running, axis=state_row.ndim - 1...]
    psum x1 -> x0, waiting for transfers between devices: 106 us -> none  [per_device(): lax.psum((encoder_weight_sum, encoder_bias_sum, predictor_weight_sum, pre...]
    dynamic_update_slice x128 -> x0, other arithmetic: 85.7 us -> none  [forward_rows(): return lax.scan(forward_frame_step, entry_row, (blank_rows, label_rows))]
    gather x24 -> x0, local copies, waits for them, and re-layouts: 53.7 us -> none  [label_logits(): return jnp.take_along_axis(logits, chosen, axis=3)[..., 0]]
    add x141 -> x0, other arithmetic: 52.1 us -> none  [the longest x64 44.2 us: forward_frame_step(): leaving = forward_log + row_blank]
  transfers between devices with their start and end apart: 18 -> 13, of which waited for: 18 -> 13; matrix products, arithmetic and copies ran while one was open for 0% -> 0% of each run, Pallas kernels for 0% -> 0%
where the time goes in v1:
time: 121 us; the launch traced here: 119 us
  waiting for transfers between devices  70.2 us (58%)
  Pallas kernels  24.3 us (20%)
  blocking collectives  17.9 us (15%)
  starting transfers between devices  4.87 us (4%)
    ppermute x13, waiting for transfers between devices, permuted(): return lax.ppermute(array, AXES, pairs)  70.2 us
    all_to_all x1, blocking collectives, per_device(): packets = lax.all_to_all(packets, AXES, 0, 0, tiled=True)  17.9 us
    pallas_call x1, Pallas kernels, tangents(): pl.pallas_call(functools.partial(tangent_kernel, dict(layout, hops=len(ma...  11.4 us
    pallas_call x1, Pallas kernels, scores(): pl.pallas_call(functools.partial(score_kernel, seq_count), in_specs=[smem...  8.08 us
    ppermute x13, starting transfers between devices, permuted(): return lax.ppermute(array, AXES, pairs)  4.87 us
    pallas_call x1, Pallas kernels, per_device(): pl.pallas_call(functools.partial(finish_kernel, layout), in_specs=[anywhe...  2.84 us
  transfers between devices with their start and end apart: 13, of which 13 were waited for; matrix products, arithmetic and copies ran while one was open for 0% of the time, Pallas kernels for 0%

profile of v1, /device:TPU:0, one launch (start us, length us, event | category | flops | bytes accessed | tf_op | source)
XLA Modules:
  0.0 119.2 jit_solution(1518918476034663018)
XLA Ops:
  0.7 1.5 %shard_map.187 = bf16[32,8,512]{2,1,0:T(8,128)(2,1)} custom-call(bf16[6,512]{1,0:T(8,128)(2,1)} %bitcast.10, s32[8,6]{1,0:T(8,128)} %labels_ref.1), custom_call_target="tpu_custom_call" | custom-call | tf_op jit(solution)/shard_map/pallas_call | solution.py:634
  2.2 17.9 %all_to_all.5.packets_ref = bf16[32,8,512]{2,1,0:T(8,128)(2,1)S(1)} all-to-all(bf16[32,8,512]{2,1,0:T(8,128)(2,1)} %shard_map.187), channel_id=1, replica_groups=mesh['frames'=8,'tokens'=4] {'frames','tokens'}, dimensions={0} | all-to-all | bytes 524288 | tf_op jit(solution)/shard_map/all_to_all | solution.py:640
  20.1 8.1 %shard_map.188 = (f32[12,256,1024]{2,1,0:T(8,128)S(1)}, f32[2,64,512]{2,1,0:T(8,128)S(1)}, f32[48,512]{1,0:T(8,128)S(1)}, s32[48,128]{1,0:T(8,128)S(1)}, f32[211...) custom-call(s32[1]{0:T(128)} %constant.18.clone.1.offset_ref, ...), custom_call_target="tpu_custom_call" | custom-call | tf_op jit(solution)/shard_map/pallas_call | solution.py:658
  28.2 1.0 collective-permute-start
  29.2 2.8 %collective-permute-done.refs_1_ = f32[1,1,24,128]{3,2,1,0:T(8,128)S(1)} collective-permute-done((f32[1,1,24,128]{3,2,1,0:T(8,128)S(1)}, f32[1,1,24,128]{3,2,1,0:T(8,128)S(1)}, u32[]{:S(2)}, u32[]{:S(2)}) %collective-permute-start) | collective-permute-done | bytes 12320 | tf_op jit(solution)/shard_map/ppermute | solution.py:541
  32.0 3.7 %collective-permute-done.1.refs_2_ = f32[2,1,24,128]{3,2,1,0:T(8,128)S(1)} collective-permute-done((f32[2,1,24,128]{3,2,1,0:T(8,128)S(1)}, f32[2,1,24,128]{3,2,1,0:T(8,128)S(1)}, u32[]{:S(2)}, u32[]{:S(2)}) %collective-permute-start.1) | collective-permute-done | bytes 24608 | tf_op jit(solution)/shard_map/ppermute | solution.py:541
  35.8 5.5 %collective-permute-done.2.refs_3_ = f32[4,1,24,128]{3,2,1,0:T(8,128)S(1)} collective-permute-done((f32[4,1,24,128]{3,2,1,0:T(8,128)S(1)}, f32[4,1,24,128]{3,2,1,0:T(8,128)S(1)}, u32[]{:S(2)}, u32[]{:S(2)}) %collective-permute-start.2) | collective-permute-done | bytes 49184 | tf_op jit(solution)/shard_map/ppermute | solution.py:541
  41.3 11.4 %shard_map.189 = (f32[2,64,512]{2,1,0:T(8,128)}, f32[3584,128]{1,0:T(8,128)S(1)}, f32[3584,128]{1,0:T(8,128)S(1)}) custom-call(s32[8]{0:T(128)S(1)} %copy-done, s32[8]{0:T(128)S(1)} %copy-done.1, s32[1]{0:T(128)} %constant.18.clone.1.offset_ref, f32[8]{0:T(128)S(1)} %copy-done.2, f32[12,256,1024]{2,1,0:T(8,128)S(1)} %get-tuple-element.39.softmax_ref, ...), custom_call_target="tpu_custom_call" | custom-call | tf_op jit(solution)/shard_map/pallas_call | solution.py:719
  52.7 3.2 %collective-permute-start.3 = (f32[3584,128]{1,0:T(8,128)S(1)}, f32[3584,128]{1,0:T(8,128)S(1)}, u32[]{:S(2)}, u32[]{:S(2)}) collective-permute-start(f32[3584,128]{1,0:T(8,128)S(1)} %get-tuple-element.50), channel_id=1, source_target_pairs={{0,1},{1,0},{2,3},{3,2},{4,5},{5,4},{6,7},{7,6},{8,9},{9,8},{10,11... | collective-permute-start | bytes 5505032 | tf_op jit(solution)/shard_map/ppermute | solution.py:541
  55.9 3.4 %collective-permute-done.3.received_ref = f32[3584,128]{1,0:T(8,128)S(1)} collective-permute-done((f32[3584,128]{1,0:T(8,128)S(1)}, f32[3584,128]{1,0:T(8,128)S(1)}, u32[]{:S(2)}, u32[]{:S(2)}) %collective-permute-start.3) | collective-permute-done | bytes 1835040 | tf_op jit(solution)/shard_map/ppermute | solution.py:541
  59.3 0.3 shard_map.190
  59.6 8.5 %collective-permute-done.4.received_ref = bf16[1792,128]{1,0:T(8,128)(2,1)S(1)} collective-permute-done((bf16[1792,128]{1,0:T(8,128)(2,1)S(1)}, bf16[1792,128]{1,0:T(8,128)(2,1)S(1)}, u32[]{:S(2)}, u32[]{:S(2)}) %collective-permute-start.4) | collective-permute-done | bytes 458784 | tf_op jit(solution)/shard_map/ppermute | solution.py:541
  68.3 6.0 %collective-permute-done.5.received_ref = bf16[896,128]{1,0:T(8,128)(2,1)S(1)} collective-permute-done((bf16[896,128]{1,0:T(8,128)(2,1)S(1)}, bf16[896,128]{1,0:T(8,128)(2,1)S(1)}, u32[]{:S(2)}, u32[]{:S(2)}) %collective-permute-start.5) | collective-permute-done | bytes 229408 | tf_op jit(solution)/shard_map/ppermute | solution.py:541
  74.4 6.0 %collective-permute-done.6.received_ref = f32[448,128]{1,0:T(8,128)S(1)} collective-permute-done((f32[448,128]{1,0:T(8,128)S(1)}, f32[448,128]{1,0:T(8,128)S(1)}, u32[]{:S(2)}, u32[]{:S(2)}) %collective-permute-start.6) | collective-permute-done | bytes 229408 | tf_op jit(solution)/shard_map/ppermute | solution.py:541
  80.5 7.6 %collective-permute-done.7 = f32[224,128]{1,0:T(8,128)S(1)} collective-permute-done((f32[224,128]{1,0:T(8,128)S(1)}, f32[224,128]{1,0:T(8,128)S(1)}, u32[]{:S(2)}, u32[]{:S(2)}) %collective-permute-start.7) | collective-permute-done | bytes 114720 | tf_op jit(solution)/shard_map/ppermute | solution.py:541
  88.2 5.1 %collective-permute-done.8 = bf16[224,128]{1,0:T(8,128)(2,1)S(1)} collective-permute-done((bf16[224,128]{1,0:T(8,128)(2,1)S(1)}, bf16[224,128]{1,0:T(8,128)(2,1)S(1)}, u32[]{:S(2)}, u32[]{:S(2)}) %collective-permute-start.8) | collective-permute-done | bytes 57376 | tf_op jit(solution)/shard_map/ppermute | solution.py:541
  93.4 4.8 %collective-permute-done.9 = bf16[448,128]{1,0:T(8,128)(2,1)S(1)} collective-permute-done((bf16[448,128]{1,0:T(8,128)(2,1)S(1)}, bf16[448,128]{1,0:T(8,128)(2,1)S(1)}, u32[]{:S(2)}, u32[]{:S(2)}) %collective-permute-start.9) | collective-permute-done | bytes 114720 | tf_op jit(solution)/shard_map/ppermute | solution.py:541
  98.3 6.0 %collective-permute-done.10 = bf16[896,128]{1,0:T(8,128)(2,1)S(1)} collective-permute-done((bf16[896,128]{1,0:T(8,128)(2,1)S(1)}, bf16[896,128]{1,0:T(8,128)(2,1)S(1)}, u32[]{:S(2)}, u32[]{:S(2)}) %collective-permute-start.10) | collective-permute-done | bytes 229408 | tf_op jit(solution)/shard_map/ppermute | solution.py:541
  104.3 0.1 maximum_select_fusion.1
  104.5 8.5 %collective-permute-done.11 = bf16[1792,128]{1,0:T(8,128)(2,1)S(1)} collective-permute-done((bf16[1792,128]{1,0:T(8,128)(2,1)S(1)}, bf16[1792,128]{1,0:T(8,128)(2,1)S(1)}, u32[]{:S(2)}, u32[]{:S(2)}) %collective-permute-start.11) | collective-permute-done | bytes 458784 | tf_op jit(solution)/shard_map/ppermute | solution.py:541
  113.0 0.2 maximum_select_fusion.own_ref
  113.3 2.5 %collective-permute-done.12.other_ref = bf16[3584,128]{1,0:T(8,128)(2,1)S(1)} collective-permute-done((bf16[3584,128]{1,0:T(8,128)(2,1)S(1)}, bf16[3584,128]{1,0:T(8,128)(2,1)S(1)}, u32[]{:S(2)}, u32[]{:S(2)}) %collective-permute-start.12) | collective-permute-done | bytes 917536 | tf_op jit(solution)/shard_map/ppermute | solution.py:541
  115.7 2.8 %shard_map.194 = (f32[512,1024]{1,0:T(8,128)}, f32[1,1024]{1,0:T(1,128)}, f32[512,512]{1,0:T(8,128)}, f32[1,512]{1,0:T(1,128)}, f32[512,512]{1,0:T(8,128)}, /*in...) custom-call(bf16[3584,128]{1,0:T(8,128)(2,1)S(1)} %maximum_select_fusion.own_ref, ...), custom_call_target="tpu_custom_call" | custom-call | tf_op jit(solution)/shard_map/pallas_call | solution.py:767
  118.6 0.6 copy.21
  (25 shorter events, 1.0 us)
Async XLA Ops:
  0.6 40.6 %copy-start = (s32[8]{0:T(128)S(1)}, s32[8]{0:T(128)}, u32[]{:S(2)}) copy-start(s32[8]{0:T(128)} %lens_ref.1) | copy-start | bytes 100
  0.7 40.6 %copy-start.1 = (s32[8]{0:T(128)S(1)}, s32[8]{0:T(128)}, u32[]{:S(2)}) copy-start(s32[8]{0:T(128)} %tokens_ref.1) | copy-start | bytes 100
  0.7 40.6 %copy-start.2 = (f32[8]{0:T(128)S(1)}, f32[8]{0:T(128)}, u32[]{:S(2)}) copy-start(f32[8]{0:T(128)} %scale_ref.1) | copy-start | bytes 100
  28.2 3.8 %collective-permute-start = (f32[1,1,24,128]{3,2,1,0:T(8,128)S(1)}, f32[1,1,24,128]{3,2,1,0:T(8,128)S(1)}, u32[]{:S(2)}, u32[]{:S(2)}) collective-permute-start(f32[1,1,24,128]{3,2,1,0:T(8,128)S(1)} %get-tuple-element.48.refs_0_), channel_id=1, source_target_pairs={{0,4},{1,5},{2,6},{3,7},{4,0},{5,1},{6,2},{7,3},{8,12},{9,13},{10,... | collective-permute-start | bytes 36872 | tf_op jit(solution)/shard_map/ppermute | solution.py:541
  32.0 3.8 %collective-permute-start.1 = (f32[2,1,24,128]{3,2,1,0:T(8,128)S(1)}, f32[2,1,24,128]{3,2,1,0:T(8,128)S(1)}, u32[]{:S(2)}, u32[]{:S(2)}) collective-permute-start(f32[2,1,24,128]{3,2,1,0:T(8,128)S(1)} %pad_maximum_fusion.1), channel_id=1, source_target_pairs={{0,8},{1,9},{2,10},{3,11},{4,12},{5,13},{6,14},{7,15},{8,0},{9,1},... | collective-permute-start | bytes 73736 | tf_op jit(solution)/shard_map/ppermute | solution.py:541
  35.8 5.5 %collective-permute-start.2 = (f32[4,1,24,128]{3,2,1,0:T(8,128)S(1)}, f32[4,1,24,128]{3,2,1,0:T(8,128)S(1)}, u32[]{:S(2)}, u32[]{:S(2)}) collective-permute-start(f32[4,1,24,128]{3,2,1,0:T(8,128)S(1)} %pad_maximum_fusion), channel_id=1, source_target_pairs={{0,16},{1,17},{2,18},{3,19},{4,20},{5,21},{6,22},{7,23},{8,24},{9,... | collective-permute-start | bytes 147464 | tf_op jit(solution)/shard_map/ppermute | solution.py:541
  52.7 6.6 %collective-permute-start.3 = (f32[3584,128]{1,0:T(8,128)S(1)}, f32[3584,128]{1,0:T(8,128)S(1)}, u32[]{:S(2)}, u32[]{:S(2)}) collective-permute-start(f32[3584,128]{1,0:T(8,128)S(1)} %get-tuple-element.50), channel_id=1, source_target_pairs={{0,1},{1,0},{2,3},{3,2},{4,5},{5,4},{6,7},{7,6},{8,9},{9,8},{10,11... | collective-permute-start | bytes 5505032 | tf_op jit(solution)/shard_map/ppermute | solution.py:541
  59.6 8.5 %collective-permute-start.4 = (bf16[1792,128]{1,0:T(8,128)(2,1)S(1)}, bf16[1792,128]{1,0:T(8,128)(2,1)S(1)}, u32[]{:S(2)}, u32[]{:S(2)}) collective-permute-start(bf16[1792,128]{1,0:T(8,128)(2,1)S(1)} %get-tuple-element.52), channel_id=1, source_target_pairs={{0,4},{1,9},{2,6},{3,11},{4,0},{5,13},{6,2},{7,15},{8,12},{9,1},{1... | collective-permute-start | bytes 1376264 | tf_op jit(solution)/shard_map/ppermute | solution.py:541
  68.2 6.1 %collective-permute-start.5 = (bf16[896,128]{1,0:T(8,128)(2,1)S(1)}, bf16[896,128]{1,0:T(8,128)(2,1)S(1)}, u32[]{:S(2)}, u32[]{:S(2)}) collective-permute-start(bf16[896,128]{1,0:T(8,128)(2,1)S(1)} %get-tuple-element.54), channel_id=1, source_target_pairs={{0,2},{1,5},{2,0},{3,7},{4,6},{5,1},{6,4},{7,3},{8,10},{9,13},{10,... | collective-permute-start | bytes 688136 | tf_op jit(solution)/shard_map/ppermute | solution.py:541
  74.3 6.1 %collective-permute-start.6 = (f32[448,128]{1,0:T(8,128)S(1)}, f32[448,128]{1,0:T(8,128)S(1)}, u32[]{:S(2)}, u32[]{:S(2)}) collective-permute-start(f32[448,128]{1,0:T(8,128)S(1)} %get-tuple-element.56), channel_id=1, source_target_pairs={{0,8},{1,3},{2,10},{3,1},{4,12},{5,7},{6,14},{7,5},{8,0},{9,11},{1... | collective-permute-start | bytes 688136 | tf_op jit(solution)/shard_map/ppermute | solution.py:541
  80.4 7.7 %collective-permute-start.7 = (f32[224,128]{1,0:T(8,128)S(1)}, f32[224,128]{1,0:T(8,128)S(1)}, u32[]{:S(2)}, u32[]{:S(2)}) collective-permute-start(f32[224,128]{1,0:T(8,128)S(1)} %get-tuple-element.58), channel_id=1, source_target_pairs={{0,16},{1,17},{2,18},{3,19},{4,20},{5,21},{6,22},{7,23},{8,24},{9,... | collective-permute-start | bytes 344072 | tf_op jit(solution)/shard_map/ppermute | solution.py:541
  88.1 5.1 %collective-permute-start.8 = (bf16[224,128]{1,0:T(8,128)(2,1)S(1)}, bf16[224,128]{1,0:T(8,128)(2,1)S(1)}, u32[]{:S(2)}, u32[]{:S(2)}) collective-permute-start(bf16[224,128]{1,0:T(8,128)(2,1)S(1)} %add_convert_fusion), channel_id=1, source_target_pairs={{0,16},{1,17},{2,18},{3,19},{4,20},{5,21},{6,22},{7,23},{8,24},{9,... | collective-permute-start | bytes 172040 | tf_op jit(solution)/shard_map/ppermute | solution.py:541
  93.3 4.9 %collective-permute-start.9 = (bf16[448,128]{1,0:T(8,128)(2,1)S(1)}, bf16[448,128]{1,0:T(8,128)(2,1)S(1)}, u32[]{:S(2)}, u32[]{:S(2)}) collective-permute-start(bf16[448,128]{1,0:T(8,128)(2,1)S(1)} %maximum_select_fusion.3), channel_id=1, source_target_pairs={{0,8},{1,3},{2,10},{3,1},{4,12},{5,7},{6,14},{7,5},{8,0},{9,11},{1... | collective-permute-start | bytes 344072 | tf_op jit(solution)/shard_map/ppermute | solution.py:541
  98.2 6.1 %collective-permute-start.10 = (bf16[896,128]{1,0:T(8,128)(2,1)S(1)}, bf16[896,128]{1,0:T(8,128)(2,1)S(1)}, u32[]{:S(2)}, u32[]{:S(2)}) collective-permute-start(bf16[896,128]{1,0:T(8,128)(2,1)S(1)} %maximum_select_fusion.2), channel_id=1, source_target_pairs={{0,2},{1,5},{2,0},{3,7},{4,6},{5,1},{6,4},{7,3},{8,10},{9,13},{10,... | collective-permute-start | bytes 688136 | tf_op jit(solution)/shard_map/ppermute | solution.py:541
  104.4 8.5 %collective-permute-start.11 = (bf16[1792,128]{1,0:T(8,128)(2,1)S(1)}, bf16[1792,128]{1,0:T(8,128)(2,1)S(1)}, u32[]{:S(2)}, u32[]{:S(2)}) collective-permute-start(bf16[1792,128]{1,0:T(8,128)(2,1)S(1)} %maximum_select_fusion.1), channel_id=1, source_target_pairs={{0,4},{1,9},{2,6},{3,11},{4,0},{5,13},{6,2},{7,15},{8,12},{9,1},{1... | collective-permute-start | bytes 1376264 | tf_op jit(solution)/shard_map/ppermute | solution.py:541
  113.2 2.5 %collective-permute-start.12 = (bf16[3584,128]{1,0:T(8,128)(2,1)S(1)}, bf16[3584,128]{1,0:T(8,128)(2,1)S(1)}, u32[]{:S(2)}, u32[]{:S(2)}) collective-permute-start(bf16[3584,128]{1,0:T(8,128)(2,1)S(1)} %maximum_select_fusion.own_ref), channel_id=1, source_target_pairs={{0,1},{1,0},{2,3},{3,2},{4,5},{5,4},{6,7},{7,6},{8,9},{9,8},{10,11... | collective-permute-start | bytes 2752520 | tf_op jit(solution)/shard_map/ppermute | solution.py:541

commit v2 on v1

v2 whole, which is shorter than its diff:
```python
import functools

import jax
import jax.numpy as jnp
from jax import lax
from jax.experimental import pallas as pl
from jax.experimental.pallas import tpu as pltpu
from jax.sharding import PartitionSpec as P

NEG = -1e30
LOG2E = 1.4426950408889634
LN2 = 0.6931471805599453
BF16 = jnp.bfloat16
F32 = jnp.float32
GROUP = 32
SUB_UNITS = 4
AXES = ("frames", "tokens")


def lane_ids(rows):
    return lax.broadcasted_iota(jnp.int32, (rows, 128), 1)


def log2_add(a, b):
    return jnp.maximum(a, b) + jnp.log2(1.0 + jnp.exp2(-jnp.abs(a - b)))


def both_ways(blank_ref, label_ref, units, steps, ahead, behind, keep=None):
    def one_step(i, state):
        ahead, behind = state
        back = steps - 1 - i
        here = pl.ds(pl.multiple_of(i * units, 8), units)
        there = pl.ds(pl.multiple_of(back * units, 8), units)
        if keep is not None:
            keep[0][here, :] = ahead
            keep[1][there, :] = behind
        from_left = pltpu.roll(ahead + label_ref[here, :], 1, 0)
        to_right = pltpu.roll(behind, units - 1, 0) + label_ref[there, :]
        ahead = log2_add(ahead + blank_ref[here, :], from_left)
        behind = log2_add(behind + blank_ref[there, :], to_right)
        return ahead, behind

    return lax.fori_loop(0, steps, one_step, (ahead, behind))


def in_two_stages(count, first, second, even, odd, between=None):
    def two_blocks(n, _):
        first(2 * n + 1, odd)
        second(2 * n, even)
        first(jnp.minimum(2 * n + 2, count - 1), even)
        second(2 * n + 1, odd)
        return 0

    @pl.when(count > 0)
    def _():
        first(0, even)

    if between is not None:
        between()

    @pl.when(count > 0)
    def _():
        lax.fori_loop(0, count // 2, two_blocks, 0)

        @pl.when(count % 2 == 1)
        def _():
            second(count - 1, even)


def packet_kernel(predictor_hbm, labels_hbm, *refs):
    *refs, predictor_ref, labels_ref, sems = refs
    count = len(refs) // 2
    packets_ref = refs[count]
    targets = (predictor_ref, labels_ref, *refs[count + 1 :])
    loads = [
        pltpu.make_async_copy(source, target, sems.at[n])
        for n, (source, target) in enumerate(
            zip((predictor_hbm, labels_hbm, *refs[:count]), targets)
        )
    ]
    for load in loads:
        load.start()
    loads[0].wait()
    loads[1].wait()
    seqs, units = labels_ref.shape
    width = packets_ref.shape[2]
    flat = jnp.zeros((1, width), F32)
    for s in range(seqs):
        row = labels_ref[s : s + 1, :].astype(F32)
        row = jnp.concatenate([row, jnp.zeros((1, width - units), F32)], axis=1)
        flat = flat + (pltpu.roll(row, s * units, 1) if s else row)
    high = jnp.floor(flat * (1.0 / 32.0))
    packet = jnp.concatenate(
        [predictor_ref[...].astype(F32), high, flat - high * 32.0], axis=0
    ).astype(BF16)
    for d in range(packets_ref.shape[0]):
        packets_ref[d] = packet
    for load in loads[2:]:
        load.wait()


def block_counts(lens_ref, tokens_ref, first_seq, first_frame):
    counts = []
    for s in range(2):
        inside = first_frame < lens_ref[first_seq + s]
        counts.append(jnp.where(inside, tokens_ref[first_seq + s] // SUB_UNITS + 1, 0))
    return counts


def score_kernel(
    seqs_here,
    offset_ref,
    packets_ref,
    lens_hbm,
    tokens_hbm,
    encoder_ref,
    encoder_weight_ref,
    encoder_bias_ref,
    predictor_weight_ref,
    predictor_bias_ref,
    weight_ref,
    bias_ref,
    softmax_ref,
    frame_ref,
    token_ref,
    label_table_ref,
    blank_ref,
    label_ref,
    hidden_ref,
    turned_ref,
    inverse_ref,
    matrix_ref,
    even_ref,
    odd_ref,
    labels_smem,
    label_rows_ref,
    lens_ref,
    tokens_ref,
    load_sems,
    label_sem,
):
    loads = [
        pltpu.make_async_copy(lens_hbm, lens_ref, load_sems.at[0]),
        pltpu.make_async_copy(tokens_hbm, tokens_ref, load_sems.at[1]),
    ]
    for load in loads:
        load.start()
    seqs, frame_count, width = encoder_ref.shape
    units = token_ref.shape[0] // seqs
    shards = label_rows_ref.shape[0]
    shard_units = units // shards
    steps = frame_count + units - 1
    first_frame = lax.axis_index("frames") * frame_count
    first_seq = lax.axis_index("tokens") * seqs_here + offset_ref[0]
    vocab = weight_ref.shape[1]
    blank_ref[...] = jnp.zeros_like(blank_ref)
    label_ref[...] = jnp.full(label_ref.shape, NEG, F32)
    for s in range(seqs):
        for k in range(shards):
            rows = packets_ref[(first_seq + s) * shards + k]
            at = s * units + k * shard_units
            token_ref[at : at + shard_units, :] = rows[:shard_units].astype(F32)
    for k in range(shards):
        halves = packets_ref[k, shard_units:, :].astype(F32)
        label_rows_ref[k : k + 1, :] = halves[:1] * 32.0 + halves[1:2]
    wide = lane_ids(1)
    table = jnp.zeros((1, 128), F32)
    for s in range(seqs):
        for k in range(shards):
            target = s * units + k * shard_units
            shift = (target - (first_seq + s) * shard_units) % width
            row = pltpu.roll(label_rows_ref[k : k + 1, :], shift, 1)[:, :128]
            table = jnp.where((wide >= target) & (wide < target + shard_units), row, table)
    label_table_ref[...] = table.astype(jnp.int32)
    label_copy = pltpu.make_async_copy(label_table_ref, labels_smem, label_sem)
    label_copy.start()
    token_ref[...] = (
        jnp.dot(token_ref[...].astype(BF16), predictor_weight_ref[...], preferred_element_type=F32)
        + predictor_bias_ref[...]
    ).astype(BF16).astype(F32)
    frame_ref[...] = (
        (
            jnp.dot(
                encoder_ref[...].reshape(seqs * frame_count, width),
                encoder_weight_ref[...],
                preferred_element_type=F32,
            )
            + encoder_bias_ref[...]
        )
        .astype(BF16)
        .astype(F32)
        .reshape(frame_ref.shape)
    )
    for load in loads:
        load.wait()

    counts = block_counts(lens_ref, tokens_ref, first_seq, first_frame)
    blocks = counts[0] + counts[1]
    lanes = lane_ids(frame_count)
    times = first_frame + lax.broadcasted_iota(jnp.int32, (frame_count, 1), 0)

    def place_of(i):
        seq = jnp.where(i >= counts[0], 1, 0)
        sub = i - seq * counts[0]
        return seq, sub, seq * (units // SUB_UNITS) + sub

    def multiply(i, logits_ref):
        seq, sub, block = place_of(i)
        frames = frame_ref[seq]
        hidden = jnp.concatenate(
            [
                jnp.tanh(frames + token_ref[pl.ds(seq * units + sub * SUB_UNITS + j, 1), :])
                for j in range(SUB_UNITS)
            ],
            axis=0,
        )
        hidden_ref[block] = hidden
        low = hidden.astype(BF16)
        turned_ref[block, :width, :] = low.T
        turned_ref[block, width:, :] = jnp.ones(
            (turned_ref.shape[1] - width, turned_ref.shape[2]), BF16
        )
        logits_ref[...] = (
            jnp.dot(low, weight_ref[...], preferred_element_type=F32) + bias_ref[...]
        )

    def score(i, logits_ref):
        seq, sub, block = place_of(i)
        first_unit = sub * SUB_UNITS
        seq_len = lens_ref[first_seq + seq]
        last_unit = tokens_ref[first_seq + seq]
        own_lanes = (lanes // GROUP) % 2 == seq
        logits = logits_ref[...]
        top = jnp.max(logits, axis=1, keepdims=True)
        weights = jnp.exp(logits - top)
        total = jnp.sum(weights, axis=1, keepdims=True)
        softmax_ref[block] = weights
        inverse_ref[block] = jnp.broadcast_to(1.0 / total, (weights.shape[0], 128))
        log_total = top + jnp.log(total)
        blanks = (logits[:, :1] - log_total) * LOG2E
        for j in range(SUB_UNITS):
            unit = first_unit + j
            rows = slice(j * frame_count, (j + 1) * frame_count)
            label = labels_smem[0, seq * units + unit]
            tile = logits_ref[rows, pl.ds(pl.multiple_of(label // 128 * 128, 128), 128)]
            picked = jnp.sum(
                jnp.where(lanes == label % 128, tile, 0.0), axis=1, keepdims=True
            )
            blank = blanks[rows]
            blank = jnp.where((times == seq_len - 1) & (unit < last_unit), NEG, blank)
            blank = jnp.where((times >= seq_len) | (unit > last_unit), 0.0, blank)
            step = jnp.where(
                (times >= seq_len) | (unit >= last_unit),
                NEG,
                (picked - log_total[rows]) * LOG2E,
            )
            at = (pl.ds(unit * (units + 1), frame_count, stride=units), slice(None))
            blank_ref[at] = jnp.where(own_lanes, blank, blank_ref[at])
            label_ref[at] = jnp.where(own_lanes, step, label_ref[at])

    in_two_stages(blocks, multiply, score, even_ref, odd_ref, label_copy.wait)
    eye = jnp.where(
        lane_ids(units) % GROUP == lax.broadcasted_iota(jnp.int32, (units, 128), 0), 0.0, NEG
    ).astype(F32)
    ahead, behind = both_ways(blank_ref, label_ref, units, steps, eye, eye)
    matrix_ref[0, 0] = jnp.where(lane_ids(units) < 64, behind, ahead)


def tangent_kernel(
    layout,
    lens_ref,
    tokens_ref,
    offset_ref,
    scale_ref,
    softmax_ref,
    label_table_ref,
    blank_ref,
    label_ref,
    turned_ref,
    inverse_ref,
    *refs,
):
    hops = layout["hops"]
    matrix_refs, refs = refs[: hops + 1], refs[hops + 1 :]
    (
        tangents_ref,
        output_bias_ref,
        loss_ref,
        *kept_refs,
        sums_ref,
        matrices_ref,
        ahead_ref,
        behind_ref,
        blank_part_ref,
        label_part_ref,
        even_ref,
        odd_ref,
        labels_smem,
        label_sem,
        sems,
    ) = refs
    label_copy = pltpu.make_async_copy(label_table_ref, labels_smem, label_sem)
    label_copy.start()
    sums_ref[...] = jnp.zeros_like(sums_ref)
    output_bias_ref[...] = jnp.zeros_like(output_bias_ref)
    frame_count = layout["frame_count"]
    width = turned_ref.shape[1] - 16
    units = layout["units"]
    steps = frame_count + units - 1
    here = lax.axis_index("frames")
    first_frame = here * frame_count
    first_seq = lax.axis_index("tokens") * layout["seqs_here"] + offset_ref[0]
    chunks = matrices_ref.shape[0]
    vocab = softmax_ref.shape[2]
    at = 0
    for matrix_ref in matrix_refs:
        matrices_ref[at : at + matrix_ref.shape[0]] = matrix_ref[:, 0]
        at += matrix_ref.shape[0]
    starts = lax.broadcasted_iota(jnp.int32, (units, 128), 0)
    lanes = lane_ids(units)
    early = lanes < 64
    gather_ids = lanes // GROUP * GROUP + starts
    own_first = (lane_ids(1) // GROUP) % 2 == 0

    def one_chunk(i, carry):
        column, kept = carry
        other = chunks - 1 - i
        kept = jnp.where(jnp.where(early, i, other) == here, column, kept)
        joined = column + jnp.where(early, matrices_ref[here ^ i], matrices_ref[here ^ other])
        top = jnp.max(joined, axis=0, keepdims=True)
        row = top + jnp.log2(jnp.sum(jnp.exp2(joined - top), axis=0, keepdims=True))
        row = jnp.broadcast_to(row, (units, 128))
        return jnp.take_along_axis(row, gather_ids, axis=1, mode="promise_in_bounds"), kept

    start = jnp.where(early & (starts > 0), NEG, 0.0).astype(F32)
    last, kept = lax.fori_loop(0, chunks, one_chunk, (start, start))
    swapped_halves = pltpu.roll(kept, 64, 1)
    both_ways(
        blank_ref,
        label_ref,
        units,
        steps,
        jnp.where(early, kept, swapped_halves),
        jnp.where(early, swapped_halves, kept),
        (ahead_ref, behind_ref),
    )
    log_norm = jnp.max(jnp.where(early, last, pltpu.roll(last, 64, 1)), axis=0, keepdims=True)
    scale = jnp.where(own_first, scale_ref[first_seq], scale_ref[first_seq + 1])
    length = jnp.where(own_first, lens_ref[first_seq], lens_ref[first_seq + 1])
    bound = jnp.where(own_first, tokens_ref[first_seq], tokens_ref[first_seq + 1])
    time_limit = jnp.minimum(length - first_frame, frame_count)

    def one_diagonal(e, _):
        rows = pl.ds(pl.multiple_of(e * units, 8), units)
        time = e - starts
        behind = behind_ref[rows, :]
        base = ahead_ref[rows, :] - log_norm
        live = (starts <= bound) & (time >= 0) & (time < time_limit)
        blank_part_ref[rows, :] = jnp.where(
            live, -scale * jnp.exp2(base + blank_ref[rows, :] + behind), 0.0
        )
        label_part_ref[rows, :] = jnp.where(
            live & (starts < bound),
            -scale * jnp.exp2(base + label_ref[rows, :] + pltpu.roll(behind, units - 1, 0)),
            0.0,
        )
        return 0

    lax.fori_loop(0, steps, one_diagonal, 0, unroll=3)

    counts = block_counts(lens_ref, tokens_ref, first_seq, first_frame)
    block_lanes = lane_ids(frame_count)

    def place_of(i):
        seq = jnp.where(i >= counts[0], 1, 0)
        sub = i - seq * counts[0]
        return seq, sub, seq * (units // SUB_UNITS) + sub

    wide = lane_ids(1)
    loss = jnp.where(here == 0, -log_norm * LN2, 0.0)
    spread = jnp.where(wide == first_seq, loss[:, :1], 0.0)
    loss_ref[...] = spread + jnp.where(wide == first_seq + 1, loss[:, GROUP : GROUP + 1], 0.0)
    label_copy.wait()

    def prepare(i, tangent_ref):
        seq, sub, block = place_of(i)
        own_lanes = (block_lanes // GROUP) % 2 == seq
        for j in range(SUB_UNITS):
            unit = sub * SUB_UNITS + j
            rows = slice(j * frame_count, (j + 1) * frame_count)
            at = (pl.ds(unit * (units + 1), frame_count, stride=units), slice(None))
            blank, step = blank_part_ref[at], label_part_ref[at]
            blank = jnp.where(own_lanes, blank, pltpu.roll(blank, GROUP, 1))
            step = jnp.where(own_lanes, step, pltpu.roll(step, GROUP, 1))
            both = -(blank + step) * inverse_ref[block, rows, :]
            for v in range(vocab // 128):
                cut = slice(v * 128, (v + 1) * 128)
                piece = softmax_ref[block, rows, cut] * both
                if v == 0:
                    piece = piece + jnp.where(block_lanes == 0, blank, 0.0)
                piece = piece.astype(BF16)
                tangent_ref[rows, cut] = piece
                tangents_ref[block, rows, cut] = piece
            label = labels_smem[0, seq * units + unit]
            cut = pl.ds(pl.multiple_of(label // 128 * 128, 128), 128)
            piece = softmax_ref[block, rows, cut] * both
            piece = piece + jnp.where((block_lanes == 0) & (label < 128), blank, 0.0)
            piece = (piece + jnp.where(block_lanes == label % 128, step, 0.0)).astype(BF16)
            tangent_ref[rows, cut] = piece
            tangents_ref[block, rows, cut] = piece

    def multiply(i, tangent_ref):
        _, _, block = place_of(i)
        product = jnp.dot(turned_ref[block], tangent_ref[...], preferred_element_type=F32)
        for v in range(vocab // 128):
            sums_ref[v * width : (v + 1) * width, :] += product[:width, v * 128 : (v + 1) * 128]
        output_bias_ref[...] += product[width : width + 1, :]

    in_two_stages(counts[0] + counts[1], prepare, multiply, even_ref, odd_ref)
    part_halves(sums_ref, kept_refs, sems)


def part_halves(sums_ref, piece_refs, sems):
    place = lax.axis_index("tokens") & 1
    copies, start = [], 0
    for kept_ref, sent_ref in zip(piece_refs[::2], piece_refs[1::2]):
        half = kept_ref.shape[0]
        for part, target in ((1 - place, sent_ref), (place, kept_ref)):
            source = sums_ref.at[pl.ds(pl.multiple_of(start + part * half, 8), half), :]
            copies.append(pltpu.make_async_copy(source, target, sems.at[len(copies)]))
        start += 2 * half
    for copy in copies:
        copy.start()
    for copy in copies:
        copy.wait()


def inner_kernel(
    layout,
    lens_ref,
    tokens_ref,
    offset_ref,
    tangents_ref,
    hidden_ref,
    weight_ref,
    encoder_ref,
    output_bias_ref,
    loss_ref,
    frame_tangent_ref,
    kept_ref,
    sent_ref,
    sums_ref,
    frame_sum_ref,
    token_sum_ref,
    even_ref,
    odd_ref,
    sems,
):
    seqs, frame_count, width = encoder_ref.shape
    units = token_sum_ref.shape[0] // seqs
    vocab = weight_ref.shape[1]
    first_frame = lax.axis_index("frames") * frame_count
    first_seq = lax.axis_index("tokens") * layout["seqs_here"] + offset_ref[0]
    frame_sum_ref[...] = jnp.zeros_like(frame_sum_ref)
    token_sum_ref[...] = jnp.zeros_like(token_sum_ref)
    unset = slice(layout["token"], sums_ref.shape[0])
    sums_ref[unset, :] = jnp.zeros_like(sums_ref[unset, :])
    counts = block_counts(lens_ref, tokens_ref, first_seq, first_frame)

    def place_of(i):
        seq = jnp.where(i >= counts[0], 1, 0)
        sub = i - seq * counts[0]
        return seq, sub, seq * (units // SUB_UNITS) + sub

    def multiply(i, product_ref):
        _, _, block = place_of(i)
        product_ref[...] = lax.dot_general(
            tangents_ref[block],
            weight_ref[...],
            (((1,), (1,)), ((), ())),
            preferred_element_type=F32,
        )

    def add_up(i, product_ref):
        seq, sub, block = place_of(i)
        hidden = hidden_ref[block]
        inner = product_ref[...] * (1.0 - hidden * hidden)
        total = frame_sum_ref[seq]
        for j in range(SUB_UNITS):
            rows = slice(j * frame_count, (j + 1) * frame_count)
            total = total + inner[rows]
            token_sum_ref[pl.ds(seq * units + sub * SUB_UNITS + j, 1), :] = jnp.sum(
                inner[rows], axis=0, keepdims=True
            )
        frame_sum_ref[seq] = total

    in_two_stages(counts[0] + counts[1], multiply, add_up, even_ref, odd_ref)
    low = frame_sum_ref[...].reshape(seqs * frame_count, width).astype(BF16)
    frame_tangent_ref[...] = low
    product = lax.dot_general(
        encoder_ref[...].reshape(seqs * frame_count, width),
        low,
        (((0,), (0,)), ((), ())),
        preferred_element_type=F32,
    )
    encoder_bias = jnp.sum(low.astype(F32), axis=0, keepdims=True)
    for v in range(width // 128):
        cut = slice(v * 128, (v + 1) * 128)
        at = layout["encoder"] + v * width
        sums_ref[at : at + width, :] = product[:, cut]
        at = layout["token"] + v * layout["token_rows"] + first_seq * units
        sums_ref[pl.ds(pl.multiple_of(at, 8), seqs * units), :] = token_sum_ref[:, cut]
        at = layout["encoder_bias"] + v
        sums_ref[at : at + 1, :] = encoder_bias[:, cut]
    for v in range(vocab // 128):
        at = layout["output_bias"] + v
        sums_ref[at : at + 1, :] = output_bias_ref[:, v * 128 : (v + 1) * 128]
    spread = loss_ref[...]
    for k in range(3):
        part = spread.astype(BF16).astype(F32)
        sums_ref[layout["loss"] + k : layout["loss"] + k + 1, :] = part
        spread = spread - part
    part_halves(sums_ref, (kept_ref, sent_ref), sems)


def encoder_kernel(frame_tangent_ref, encoder_weight_ref, encoder_gradient_ref):
    encoder_gradient_ref[...] = lax.dot_general(
        frame_tangent_ref[...],
        encoder_weight_ref[...],
        (((1,), (1,)), ((), ())),
        preferred_element_type=F32,
    ).reshape(encoder_gradient_ref.shape)


def two_halves(stage, half):
    upper = upper_of(stage)
    own = pl.ds(pl.multiple_of(jnp.where(upper != 0, half, 0), 16), half)
    other = pl.ds(pl.multiple_of(jnp.where(upper != 0, 0, half), 16), half)
    return own, other


def halve_kernel(stages, merge, *refs):
    count, at = len(stages), 0
    for n, stage in enumerate(stages):
        kept_ref, received_ref = refs[2 * n : 2 * n + 2]
        half = kept_ref.shape[0] // 2
        own, other = two_halves(stage, half)
        if merge:
            next_ref, sent_ref = (ref.at[at : at + half, :] for ref in refs[2 * count :])
            at += half
        else:
            next_ref, sent_ref = refs[2 * count + 2 * n : 2 * count + 2 * n + 2]
        sent_ref[...] = (kept_ref[other, :] + received_ref[other, :].astype(F32)).astype(
            sent_ref.dtype
        )
        next_ref[...] = kept_ref[own, :] + received_ref[own, :].astype(F32)


def last_kernel(kept_ref, received_ref, sum_ref):
    sum_ref[...] = (kept_ref[...] + received_ref[...].astype(F32)).astype(BF16)


def join_kernel(stages, merged, *refs):
    count, at = len(stages), 0
    joined_refs = refs[2:] if merged else refs[2 * count :]
    for n, (stage, joined_ref) in enumerate(zip(stages, joined_refs)):
        half = joined_ref.shape[0] // 2
        own, other = two_halves(stage, half)
        if merged:
            own_ref, other_ref = (ref.at[at : at + half, :] for ref in refs[:2])
            at += half
        else:
            own_ref, other_ref = refs[2 * n : 2 * n + 2]
        joined_ref[own, :] = own_ref[...]
        joined_ref[other, :] = other_ref[...]


def put_together(halves, full_refs, sems):
    place = lax.axis_index("tokens") & 1
    copies = []
    for n, (full_ref, start) in enumerate(full_refs):
        own_ref, other_ref = halves[2 * n : 2 * n + 2]
        half = own_ref.shape[0]
        for part, source in ((place, own_ref), (1 - place, other_ref)):
            target = full_ref.at[pl.ds(pl.multiple_of(start + part * half, 16), half), :]
            copies.append(pltpu.make_async_copy(source, target, sems.at[len(copies)]))
    for copy in copies:
        copy.start()
    for copy in copies:
        copy.wait()


def finish_kernel(
    layout,
    *refs,
):
    halves, refs = refs[:4], refs[4:]
    (
        packets_ref,
        predictor_weight_ref,
        output_weight_ref,
        output_bias_ref,
        encoder_weight_ref,
        encoder_bias_ref,
        weight_gradient_ref,
        bias_gradient_ref,
        predictor_gradient_ref,
        losses_ref,
        output_ref,
        full_ref,
        tokens_ref,
        predictor_ref,
        sems,
    ) = refs
    put_together(halves, ((output_ref, 0), (full_ref, 0)), sems)
    width, vocab = output_weight_ref.shape
    for v in range(vocab // 128):
        output_weight_ref[:, v * 128 : (v + 1) * 128] = output_ref[
            v * width : (v + 1) * width, :
        ].astype(F32)
    for v in range(width // 128):
        at = layout["encoder"] + v * width
        encoder_weight_ref[:, v * 128 : (v + 1) * 128] = full_ref[at : at + width, :].astype(F32)
    rest = full_ref[layout["misc"] :, :].astype(F32)

    def row(name, k):
        at = layout[name] - layout["misc"] + k
        return rest[at : at + 1, :]

    output_bias_ref[...] = jnp.concatenate(
        [row("output_bias", v) for v in range(vocab // 128)], axis=1
    )
    encoder_bias_ref[...] = jnp.concatenate(
        [row("encoder_bias", v) for v in range(width // 128)], axis=1
    )
    count = layout["token_rows"]
    tokens = jnp.concatenate(
        [
            full_ref[layout["token"] + v * count : layout["token"] + (v + 1) * count, :]
            for v in range(width // 128)
        ],
        axis=1,
    )
    held_rows = packets_ref.shape[1] - 2
    for d in range(packets_ref.shape[0]):
        predictor_ref[d * held_rows : (d + 1) * held_rows, :] = packets_ref[
            d, :held_rows, :
        ].astype(F32)
    weight_gradient_ref[...] = lax.dot_general(
        predictor_ref[...].astype(BF16),
        tokens,
        (((0,), (0,)), ((), ())),
        preferred_element_type=F32,
    )
    wide = tokens.astype(F32)
    bias_gradient_ref[...] = jnp.sum(wide, axis=0, keepdims=True)
    tokens_ref[...] = wide
    device = lax.axis_index("frames") * lax.axis_size("tokens") + lax.axis_index("tokens")
    mine = jnp.concatenate(
        [tokens_ref[pl.ds(device * held_rows + r, 1), :] for r in range(held_rows)], axis=0
    )
    predictor_gradient_ref[:, 0, :] = lax.dot_general(
        mine.astype(BF16),
        predictor_weight_ref[...],
        (((1,), (1,)), ((), ())),
        preferred_element_type=F32,
    )
    loss = row("loss", 0) + row("loss", 1) + row("loss", 2)
    losses_ref[...] = jnp.sum(
        jnp.where(lane_ids(1) == lax.axis_index("frames"), loss, 0.0), axis=1, keepdims=True
    )


def in_hbm(array):
    return pltpu.with_memory_space_constraint(array, pltpu.HBM)


def in_vmem(array):
    return pltpu.with_memory_space_constraint(array, pltpu.VMEM)


def permuted(array, partner):
    frames, tokens = lax.axis_size("frames"), lax.axis_size("tokens")
    pairs = []
    for f in range(frames):
        for k in range(tokens):
            g, h = partner(f, k)
            pairs.append((f * tokens + k, g * tokens + h))
    return lax.ppermute(array, AXES, pairs)


def doubled(array):
    blocks, bit = [array], 1
    while bit < lax.axis_size("frames"):
        joined = jnp.concatenate(blocks, axis=0) if len(blocks) > 1 else blocks[0]
        blocks.append(permuted(joined, lambda f, k: (f ^ bit, k)))
        bit *= 2
    return blocks


def stages(shift):
    frame_bits = [(1 << i, 0) for i in range(lax.axis_size("frames").bit_length() - 1)]
    token_bits = [(0, 1 << i) for i in range(1, lax.axis_size("tokens").bit_length() - 1)]
    first = frame_bits[:1] + token_bits + frame_bits[1:2]
    return first[shift:] + first[:shift] + frame_bits[2:]


def upper_of(stage):
    return (lax.axis_index("frames") & stage[0]) | (lax.axis_index("tokens") & stage[1])


def across(stage):
    return lambda f, k: (f ^ stage[0], k ^ stage[1])


def neighbour(f, k):
    return f, k ^ 1


def call(body, ins, outs, smem=(), scratch=(), limit=4):
    vmem = pl.BlockSpec(memory_space=pltpu.VMEM)
    return pl.pallas_call(
        body,
        in_specs=[pl.BlockSpec(memory_space=pltpu.SMEM)] * len(smem) + [vmem] * len(ins),
        out_specs=[vmem] * len(outs),
        out_shape=[
            pltpu.VMEM(shape, kind) if inside else jax.ShapeDtypeStruct(shape, kind)
            for shape, kind, inside in outs
        ],
        scratch_shapes=list(scratch),
        compiler_params=pltpu.CompilerParams(vmem_limit_bytes=limit * 2**20),
    )(*smem, *map(in_vmem, ins))


def reduced_and_gathered(pieces):
    plans = list(zip(*(stages(n) for n in range(len(pieces)))))
    flat = [a for kept, sent in pieces for a in (kept, permuted(sent, neighbour))]
    way_back = []
    for number, plan in enumerate(plans):
        plan = plan[: len(flat) // 2]
        merge = len(plan) > 1 and len(set(plan)) == 1
        halves = [kept.shape[0] // 2 for kept in flat[::2]]
        way_back.append((plan, merge, [2 * half for half in halves]))
        if merge:
            halves = [sum(halves)]
        sent_type = BF16 if number < 2 else F32
        flat = call(
            functools.partial(halve_kernel, plan, merge),
            flat,
            [out for half in halves for out in (((half, 128), F32, True), ((half, 128), sent_type, True))],
        )
        flat = [
            permuted(a, across(plan[n // 2])) if n % 2 else a for n, a in enumerate(flat)
        ]
    arrays = [
        call(last_kernel, flat[n : n + 2], [(flat[n].shape, BF16, True)])[0]
        for n in range(0, len(flat), 2)
    ]
    for plan, merged, sizes in reversed(way_back):
        flat = [a for array, stage in zip(arrays, plan) for a in (array, permuted(array, across(stage)))]
        arrays = call(
            functools.partial(join_kernel, plan, merged),
            flat,
            [((size, 128), BF16, True) for size in sizes],
        )
    return [(array, permuted(array, neighbour)) for array in arrays]


def per_device(
    encoder_out,
    encoder_weight,
    encoder_bias,
    predictor_out,
    predictor_weight,
    predictor_bias,
    output_weight,
    output_bias,
    labels,
    frame_lens,
    token_lens,
    loss_scale,
):
    seq_count, frame_count, width = encoder_out.shape
    vocab = output_weight.shape[1]
    all_seqs = labels.shape[0]
    held_seqs, held_units = predictor_out.shape[:2]
    assert held_seqs == 1
    frame_axis, token_axis = lax.axis_size("frames"), lax.axis_size("tokens")
    device_count = frame_axis * token_axis
    units = held_units * token_axis
    calls = seq_count // 2
    steps = frame_count + units - 1
    diagonals = (steps + 1) * units
    smem = pl.BlockSpec(memory_space=pltpu.SMEM)
    vmem = pl.BlockSpec(memory_space=pltpu.VMEM)
    anywhere = pl.BlockSpec(memory_space=pl.ANY)

    weights = (
        encoder_out,
        encoder_weight,
        encoder_bias.reshape(1, width),
        predictor_weight,
        predictor_bias.reshape(1, width),
        output_weight,
        output_bias.reshape(1, vocab),
    )
    packets, *weights = pl.pallas_call(
        packet_kernel,
        in_specs=[anywhere] * (2 + len(weights)),
        out_specs=[vmem] * (1 + len(weights)),
        out_shape=[jax.ShapeDtypeStruct((device_count, held_units + 2, width), BF16)]
        + [pltpu.VMEM(w.shape, w.dtype) for w in weights],
        scratch_shapes=[
            pltpu.VMEM((held_units, width), BF16),
            pltpu.VMEM(labels.shape, jnp.int32),
            pltpu.SemaphoreType.DMA((2 + len(weights),)),
        ],
        compiler_params=pltpu.CompilerParams(vmem_limit_bytes=4 * 2**20),
    )(*map(in_hbm, (predictor_out.reshape(held_units, width), labels, *weights)))
    packets = lax.all_to_all(packets, AXES, 0, 0, tiled=True)

    score_shapes = [
        ((2 * units // SUB_UNITS, SUB_UNITS * frame_count, vocab), F32),
        ((2, frame_count, width), F32),
        ((2 * units, width), F32),
        ((1, 128), jnp.int32),
        ((diagonals, 128), F32),
        ((diagonals, 128), F32),
        ((2 * units // SUB_UNITS, SUB_UNITS * frame_count, width), F32),
        ((2 * units // SUB_UNITS, width + 16, SUB_UNITS * frame_count), BF16),
        ((2 * units // SUB_UNITS, SUB_UNITS * frame_count, 128), F32),
        ((1, 1, units, 128), F32),
    ]

    def scores(given):
        offset, encoder = given
        return pl.pallas_call(
            functools.partial(score_kernel, seq_count),
            in_specs=[smem, vmem] + [anywhere] * 2 + [vmem] * len(weights),
            out_specs=[vmem] * len(score_shapes),
            out_shape=[pltpu.VMEM(s, t) for s, t in score_shapes],
            scratch_shapes=[
                pltpu.VMEM((SUB_UNITS * frame_count, vocab), F32),
                pltpu.VMEM((SUB_UNITS * frame_count, vocab), F32),
                pltpu.SMEM((1, 128), jnp.int32),
                pltpu.VMEM((token_axis, width), F32),
                pltpu.SMEM(frame_lens.shape, jnp.int32),
                pltpu.SMEM(token_lens.shape, jnp.int32),
                pltpu.SemaphoreType.DMA((2,)),
                pltpu.SemaphoreType.DMA,
            ],
            compiler_params=pltpu.CompilerParams(vmem_limit_bytes=8 * 2**20),
        )(
            offset,
            in_vmem(packets),
            in_hbm(frame_lens),
            in_hbm(token_lens),
            *map(in_vmem, (encoder, *weights[1:])),
        )

    offsets = 2 * jnp.arange(calls, dtype=jnp.int32).reshape(calls, 1)
    encoders = weights[0].reshape(calls, 2, frame_count, width)
    if calls == 1:
        scored = scores((offsets[0], weights[0]))
        matrix = scored[-1]
    else:
        scored = lax.map(scores, (offsets, encoders))
        matrix = scored[-1].reshape(1, calls, units, 128)

    matrices = doubled(matrix)
    layout = {"seqs_here": seq_count, "frame_count": frame_count, "units": units}
    layout["encoder"] = 0
    at = width // 128 * width
    layout["token"], layout["token_rows"] = at, all_seqs * units
    at += width // 128 * all_seqs * units
    layout["misc"] = layout["output_bias"] = at
    at += vocab // 128
    layout["encoder_bias"] = at
    at += width // 128
    layout["loss"] = at
    at += 3
    align = 16 * device_count
    output_rows = vocab // 128 * width
    output_rows += -output_rows % align
    rest_rows = at + (-at % align)

    blocks = 2 * units // SUB_UNITS
    block_rows = SUB_UNITS * frame_count

    def tangents(offset, scored, matrices):
        softmax, _, _, table, blank, label, _, turned, inverse = scored
        given = (softmax, table, blank, label, turned, inverse, *matrices)
        return pl.pallas_call(
            functools.partial(tangent_kernel, dict(layout, hops=len(matrices) - 1)),
            in_specs=[smem] * 4 + [vmem] * len(given),
            out_specs=[vmem] * 5,
            out_shape=[
                pltpu.VMEM((blocks, block_rows, vocab), BF16),
                pltpu.VMEM((1, vocab), F32),
                pltpu.VMEM((1, 128), F32),
            ]
            + [pltpu.VMEM((output_rows // 2, 128), F32)] * 2,
            scratch_shapes=[
                pltpu.VMEM((output_rows, 128), F32),
                pltpu.VMEM((frame_axis, units, 128), F32),
                pltpu.VMEM((diagonals, 128), F32),
                pltpu.VMEM((diagonals, 128), F32),
                pltpu.VMEM((diagonals, 128), F32),
                pltpu.VMEM((diagonals, 128), F32),
                pltpu.VMEM((block_rows, vocab), BF16),
                pltpu.VMEM((block_rows, vocab), BF16),
                pltpu.SMEM((1, 128), jnp.int32),
                pltpu.SemaphoreType.DMA,
                pltpu.SemaphoreType.DMA((4,)),
            ],
            compiler_params=pltpu.CompilerParams(vmem_limit_bytes=12 * 2**20),
        )(frame_lens, token_lens, offset, loss_scale, *map(in_vmem, given))

    def inners(offset, encoder, scored, tangent, output_bias_sum, loss):
        given = (tangent, scored[6], weights[5], encoder, output_bias_sum, loss)
        return call(
            functools.partial(inner_kernel, layout),
            given,
            [
                ((2 * frame_count, width), BF16, True),
                ((rest_rows // 2, 128), F32, True),
                ((rest_rows // 2, 128), F32, True),
            ],
            smem=(frame_lens, token_lens, offset),
            scratch=[
                pltpu.VMEM((rest_rows, 128), F32),
                pltpu.VMEM((2, frame_count, width), F32),
                pltpu.VMEM((2 * units, width), F32),
                pltpu.VMEM((block_rows, width), F32),
                pltpu.VMEM((block_rows, width), F32),
                pltpu.SemaphoreType.DMA((2,)),
            ],
            limit=10,
        )

    def encoder_gradient_of(frame_tangent):
        return call(
            encoder_kernel,
            (frame_tangent, weights[1]),
            [((2, frame_count, width), F32, False)],
        )[0]

    if calls == 1:
        scored = scored[:-1]
        tangent, output_bias_sum, loss, *output_sums = tangents(offsets[0], scored, matrices)

        frame_tangent, *rest = inners(
            offsets[0], weights[0], scored, tangent, output_bias_sum, loss
        )
        sums = [*output_sums, *rest]
        encoder_gradient = encoder_gradient_of(frame_tangent)
    else:

        def add_call(sums, given):
            offset, encoder, scored, call = given
            own = [lax.dynamic_slice_in_dim(m, call, 1, 1) for m in matrices]
            tangent, output_bias_sum, loss, *more = tangents(offset, scored, own)
            frame_tangent, *rest = inners(
                offset, encoder, scored, tangent, output_bias_sum, loss
            )
            return [a + b for a, b in zip(sums, more + rest)], encoder_gradient_of(frame_tangent)

        nothing = [jnp.zeros((r, 128), F32) for r in (output_rows // 2, rest_rows // 2)]
        sums, encoder_gradient = lax.scan(
            add_call,
            [nothing[0]] * 2 + [nothing[1]] * 2,
            (offsets, encoders, scored[:-1], jnp.arange(calls)),
        )
        encoder_gradient = encoder_gradient.reshape(encoder_out.shape)

    halves = reduced_and_gathered(list(zip(sums[::2], sums[1::2])))
    finished = call(
        functools.partial(finish_kernel, layout),
        [*(a for pair in halves for a in pair), packets, weights[3]],
        [
            ((width, vocab), F32, False),
            ((1, vocab), F32, False),
            ((width, width), F32, False),
            ((1, width), F32, False),
            ((width, width), F32, False),
            ((1, width), F32, False),
            ((held_units, 1, width), F32, False),
            ((1, 1), F32, False),
        ],
        scratch=[
            pltpu.VMEM((output_rows, 128), BF16),
            pltpu.VMEM((rest_rows, 128), BF16),
            pltpu.VMEM((all_seqs * units, width), F32),
            pltpu.VMEM((all_seqs * units, width), F32),
            pltpu.SemaphoreType.DMA((6,)),
        ],
        limit=20,
    )
    return (
        finished[7].reshape(1),
        encoder_gradient,
        finished[6].transpose(1, 0, 2),
        finished[2],
        finished[3].reshape(width),
        finished[4],
        finished[5].reshape(width),
        finished[0],
        finished[1].reshape(vocab),
    )


def solution(mesh):
    placed = (
        P("tokens", "frames", None),
        P(),
        P(),
        P("frames", "tokens", None),
        P(),
        P(),
        P(),
        P(),
        P(None, "tokens"),
        P(),
        P(),
        P(),
    )
    return jax.shard_map(
        per_device,
        mesh=mesh,
        in_specs=placed,
        out_specs=(
            P("frames"),
            P("tokens", "frames", None),
            P("frames", "tokens", None),
            P(),
            P(),
            P(),
            P(),
            P(),
            P(),
        ),
        check_vma=False,
    )
```

time: 121 us -> 117 us (0.967)
  waiting for transfers between devices: 70.2 us -> 52.4 us
  starting transfers between devices: 4.87 us -> 17.1 us
  Pallas kernels: 24.3 us -> 26.8 us
    ppermute x13 -> x21, waiting for transfers between devices: 70.2 us -> 52.4 us  [permuted(): return lax.ppermute(array, AXES, pairs)]
    ppermute x13 -> x21, starting transfers between devices: 4.87 us -> 17.1 us  [permuted(): return lax.ppermute(array, AXES, pairs)]
    pallas_call x6 -> x13, Pallas kernels: 4.78 us -> 10.5 us  [the longest x12 8.74 us: call(): pl.pallas_call(body, in_specs=[pl.BlockSpec(memory_space=pltpu.SMEM)] * l...]
    pallas_call x1, Pallas kernels: 11.4 us -> 8.27 us  [tangents(): pl.pallas_call(functools.partial(tangent_kernel, dict(layout, hops=len(ma...]
  transfers between devices with their start and end apart: 13 -> 21, of which waited for: 13 -> 16; matrix products, arithmetic and copies ran while one was open for 0% -> 0% of each run, Pallas kernels for 0% -> 5%
where the time goes in v2:
time: 117 us; the launch traced here: 115 us
  waiting for transfers between devices  52.4 us (45%)
  Pallas kernels  26.8 us (23%)
  blocking collectives  17.7 us (15%)
  starting transfers between devices  17.1 us (15%)
    ppermute x21, waiting for transfers between devices, permuted(): return lax.ppermute(array, AXES, pairs)  52.4 us
    all_to_all x1, blocking collectives, per_device(): packets = lax.all_to_all(packets, AXES, 0, 0, tiled=True)  17.7 us
    ppermute x21, starting transfers between devices, permuted(): return lax.ppermute(array, AXES, pairs)  17.1 us
    pallas_call x12, Pallas kernels, call(): pl.pallas_call(body, in_specs=[pl.BlockSpec(memory_space=pltpu.SMEM)] * l...  8.74 us
    pallas_call x1, Pallas kernels, tangents(): pl.pallas_call(functools.partial(tangent_kernel, dict(layout, hops=len(ma...  8.27 us
    pallas_call x1, Pallas kernels, scores(): pl.pallas_call(functools.partial(score_kernel, seq_count), in_specs=[smem...  8.05 us
  transfers between devices with their start and end apart: 21, of which 16 were waited for; matrix products, arithmetic and copies ran while one was open for 0% of the time, Pallas kernels for 5%

profile of v2, /device:TPU:0, one launch (start us, length us, event | category | flops | bytes accessed | tf_op | source)
XLA Modules:
  0.0 114.8 jit_solution(11454975543315053840)
XLA Ops:
  0.7 1.8 %shard_map.187 = (bf16[32,8,512]{2,1,0:T(8,128)(2,1)S(1)}, bf16[2,64,512]{2,1,0:T(8,128)(2,1)S(1)}, bf16[512,512]{1,0:T(8,128)(2,1)S(1)}, f32[1,512]{1,0:T(1,128...) custom-call(bf16[6,512]{1,0:T(8,128)(2,1)} %bitcast.9, ...), custom_call_target="tpu_custom_call" | custom-call | tf_op jit(solution)/shard_map/pallas_call | solution.py:807
  2.5 17.7 %all_to_all.5.packets_ref.refs_4_ = bf16[32,8,512]{2,1,0:T(8,128)(2,1)S(1)} all-to-all(bf16[32,8,512]{2,1,0:T(8,128)(2,1)S(1)} %get-tuple-element.63), channel_id=1, replica_groups=mesh['frames'=8,'tokens'=4] {'frames','tokens'}, dimensions={0} | all-to-all | bytes 524288 | tf_op jit(solution)/shard_map/all_to_all | solution.py:820
  20.2 8.1 %shard_map.188 = (f32[12,256,1024]{2,1,0:T(8,128)S(1)}, f32[2,64,512]{2,1,0:T(8,128)}, f32[48,512]{1,0:T(8,128)}, s32[1,128]{1,0:T(1,128)S(1)}, f32[2112,128]{1,...) custom-call(s32[1]{0:T(128)} %constant.0.clone.1.offset_ref, ...), custom_call_target="tpu_custom_call" | custom-call | tf_op jit(solution)/shard_map/pallas_call | solution.py:837
  29.2 2.8 %collective-permute-done.refs_1_ = f32[1,1,24,128]{3,2,1,0:T(8,128)S(1)} collective-permute-done((f32[1,1,24,128]{3,2,1,0:T(8,128)S(1)}, f32[1,1,24,128]{3,2,1,0:T(8,128)S(1)}, u32[]{:S(2)}, u32[]{:S(2)}) %collective-permute-start) | collective-permute-done | bytes 12320 | tf_op jit(solution)/shard_map/ppermute | solution.py:689
  32.9 2.9 %collective-permute-done.1.refs_2_ = f32[2,1,24,128]{3,2,1,0:T(8,128)S(1)} collective-permute-done((f32[2,1,24,128]{3,2,1,0:T(8,128)S(1)}, f32[2,1,24,128]{3,2,1,0:T(8,128)S(1)}, u32[]{:S(2)}, u32[]{:S(2)}) %collective-permute-start.1) | collective-permute-done | bytes 24608 | tf_op jit(solution)/shard_map/ppermute | solution.py:689
  35.9 5.5 %collective-permute-done.2.refs_3_ = f32[4,1,24,128]{3,2,1,0:T(8,128)S(1)} collective-permute-done((f32[4,1,24,128]{3,2,1,0:T(8,128)S(1)}, f32[4,1,24,128]{3,2,1,0:T(8,128)S(1)}, u32[]{:S(2)}, u32[]{:S(2)}) %collective-permute-start.2) | collective-permute-done | bytes 49184 | tf_op jit(solution)/shard_map/ppermute | solution.py:689
  41.4 8.3 %shard_map.189 = (bf16[12,256,1024]{2,1,0:T(8,128)(2,1)S(1)}, f32[1,1024]{1,0:T(1,128)S(1)}, f32[1,128]{1,0:T(1,128)S(1)}, f32[2048,128]{1,0:T(8,128)S(1)}, f32[2048,128]{1,0:T(8,128)S(1)}) custom-call(s32[8]{0:T(128)S(1)} %copy-done, s32[8]{0:T(128)S(1)} %copy-done.1, s32[1]{0:T(128)} %constant.0.clone.1.offset_ref, f32[8]{0:T(128)S(1)} %copy-done.2, ...), custom_call_target="tpu_custom_call" | custom-call | tf_op jit(solution)/shard_map/pallas_call | solution.py:893
  50.4 4.3 %shard_map.190 = (bf16[128,512]{1,0:T(8,128)(2,1)S(1)}, f32[1536,128]{1,0:T(8,128)S(1)}, f32[1536,128]{1,0:T(8,128)S(1)}) custom-call(s32[8]{0:T(128)S(1)} %copy-done, s32[8]{0:T(128)S(1)} %copy-done.1, s32[1]{0:T(128)} %constant.0.clone.1.offset_ref, bf16[12,256,1024]{2,1,0:T(8,128)(2,1)S(1)} %get-tuple-element.80.tangents_ref, ...), custom_call_target="tpu_custom_call" | custom-call | tf_op jit(solution)/shard_map/pallas_call | solution.py:722
  54.7 1.9 %collective-permute-start.4 = (f32[1536,128]{1,0:T(8,128)S(1)}, f32[1536,128]{1,0:T(8,128)S(1)}, u32[]{:S(2)}, u32[]{:S(2)}) collective-permute-start(f32[1536,128]{1,0:T(8,128)S(1)} %get-tuple-element.85), channel_id=1, source_target_pairs={{0,1},{1,0},{2,3},{3,2},{4,5},{5,4},{6,7},{7,6},{8,9},{9,8},{10,11... | collective-permute-start | bytes 2359304 | tf_op jit(solution)/shard_map/ppermute | solution.py:689
  56.6 1.9 %collective-permute-done.4.refs_3_ = f32[1536,128]{1,0:T(8,128)S(1)} collective-permute-done((f32[1536,128]{1,0:T(8,128)S(1)}, f32[1536,128]{1,0:T(8,128)S(1)}, u32[]{:S(2)}, u32[]{:S(2)}) %collective-permute-start.4) | collective-permute-done | bytes 786464 | tf_op jit(solution)/shard_map/ppermute | solution.py:689
  59.3 6.9 %collective-permute-done.6.refs_3_ = bf16[768,128]{1,0:T(8,128)(2,1)S(1)} collective-permute-done((bf16[768,128]{1,0:T(8,128)(2,1)S(1)}, bf16[768,128]{1,0:T(8,128)(2,1)S(1)}, u32[]{:S(2)}, u32[]{:S(2)}) %collective-permute-start.6) | collective-permute-done | bytes 196640 | tf_op jit(solution)/shard_map/ppermute | solution.py:689
  68.1 4.2 %collective-permute-done.8.refs_3_ = bf16[384,128]{1,0:T(8,128)(2,1)S(1)} collective-permute-done((bf16[384,128]{1,0:T(8,128)(2,1)S(1)}, bf16[384,128]{1,0:T(8,128)(2,1)S(1)}, u32[]{:S(2)}, u32[]{:S(2)}) %collective-permute-start.8) | collective-permute-done | bytes 98336 | tf_op jit(solution)/shard_map/ppermute | solution.py:689
  72.9 1.6 %collective-permute-start.10 = (f32[192,128]{1,0:T(8,128)S(1)}, f32[192,128]{1,0:T(8,128)S(1)}, u32[]{:S(2)}, u32[]{:S(2)}) collective-permute-start(f32[192,128]{1,0:T(8,128)S(1)} %get-tuple-element.97), channel_id=1, source_target_pairs={{0,4},{1,5},{2,6},{3,7},{4,0},{5,1},{6,2},{7,3},{8,12},{9,13},{10,... | collective-permute-start | bytes 294920 | tf_op jit(solution)/shard_map/ppermute | solution.py:689
  74.5 3.0 %collective-permute-done.10.refs_3_ = f32[192,128]{1,0:T(8,128)S(1)} collective-permute-done((f32[192,128]{1,0:T(8,128)S(1)}, f32[192,128]{1,0:T(8,128)S(1)}, u32[]{:S(2)}, u32[]{:S(2)}) %collective-permute-start.10) | collective-permute-done | bytes 98336 | tf_op jit(solution)/shard_map/ppermute | solution.py:689
  77.6 1.6 %collective-permute-start.11 = (f32[224,128]{1,0:T(8,128)S(1)}, f32[224,128]{1,0:T(8,128)S(1)}, u32[]{:S(2)}, u32[]{:S(2)}) collective-permute-start(f32[224,128]{1,0:T(8,128)S(1)} %get-tuple-element.99), channel_id=1, source_target_pairs={{0,16},{1,17},{2,18},{3,19},{4,20},{5,21},{6,22},{7,23},{8,24},{9,... | collective-permute-start | bytes 344072 | tf_op jit(solution)/shard_map/ppermute | solution.py:689
  79.2 6.0 %collective-permute-done.11.received_ref = f32[224,128]{1,0:T(8,128)S(1)} collective-permute-done((f32[224,128]{1,0:T(8,128)S(1)}, f32[224,128]{1,0:T(8,128)S(1)}, u32[]{:S(2)}, u32[]{:S(2)}) %collective-permute-start.11) | collective-permute-done | bytes 114720 | tf_op jit(solution)/shard_map/ppermute | solution.py:689
  85.3 5.7 %collective-permute-done.12.refs_1_ = bf16[224,128]{1,0:T(8,128)(2,1)S(1)} collective-permute-done((bf16[224,128]{1,0:T(8,128)(2,1)S(1)}, bf16[224,128]{1,0:T(8,128)(2,1)S(1)}, u32[]{:S(2)}, u32[]{:S(2)}) %collective-permute-start.12) | collective-permute-done | bytes 57376 | tf_op jit(solution)/shard_map/ppermute | solution.py:689
  92.7 2.6 %collective-permute-done.14.refs_3_ = bf16[192,128]{1,0:T(8,128)(2,1)S(1)} collective-permute-done((bf16[192,128]{1,0:T(8,128)(2,1)S(1)}, bf16[192,128]{1,0:T(8,128)(2,1)S(1)}, u32[]{:S(2)}, u32[]{:S(2)}) %collective-permute-start.14) | collective-permute-done | bytes 49184 | tf_op jit(solution)/shard_map/ppermute | solution.py:689
  95.4 1.7 %collective-permute-start.15 = (bf16[512,128]{1,0:T(8,128)(2,1)S(1)}, bf16[512,128]{1,0:T(8,128)(2,1)S(1)}, u32[]{:S(2)}, u32[]{:S(2)}) collective-permute-start(bf16[512,128]{1,0:T(8,128)(2,1)S(1)} %get-tuple-element.102.refs_0_), channel_id=1, source_target_pairs={{0,2},{1,3},{2,0},{3,1},{4,6},{5,7},{6,4},{7,5},{8,10},{9,11},{10,... | collective-permute-start | bytes 393224 | tf_op jit(solution)/shard_map/ppermute | solution.py:689
  97.1 1.9 %collective-permute-start.16 = (bf16[384,128]{1,0:T(8,128)(2,1)S(1)}, bf16[384,128]{1,0:T(8,128)(2,1)S(1)}, u32[]{:S(2)}, u32[]{:S(2)}) collective-permute-start(bf16[384,128]{1,0:T(8,128)(2,1)S(1)} %get-tuple-element.103.refs_2_), channel_id=1, source_target_pairs={{0,8},{1,9},{2,10},{3,11},{4,12},{5,13},{6,14},{7,15},{8,0},{9,1},... | collective-permute-start | bytes 294920 | tf_op jit(solution)/shard_map/ppermute | solution.py:689
  99.0 2.8 %collective-permute-done.16.refs_3_ = bf16[384,128]{1,0:T(8,128)(2,1)S(1)} collective-permute-done((bf16[384,128]{1,0:T(8,128)(2,1)S(1)}, bf16[384,128]{1,0:T(8,128)(2,1)S(1)}, u32[]{:S(2)}, u32[]{:S(2)}) %collective-permute-start.16) | collective-permute-done | bytes 98336 | tf_op jit(solution)/shard_map/ppermute | solution.py:689
  101.8 1.8 %collective-permute-start.17 = (bf16[1024,128]{1,0:T(8,128)(2,1)S(1)}, bf16[1024,128]{1,0:T(8,128)(2,1)S(1)}, u32[]{:S(2)}, u32[]{:S(2)}) collective-permute-start(bf16[1024,128]{1,0:T(8,128)(2,1)S(1)} %get-tuple-element.104.refs_0_), channel_id=1, source_target_pairs={{0,4},{1,5},{2,6},{3,7},{4,0},{5,1},{6,2},{7,3},{8,12},{9,13},{10,... | collective-permute-start | bytes 786440 | tf_op jit(solution)/shard_map/ppermute | solution.py:689
  103.7 5.5 %collective-permute-done.18.refs_3_ = bf16[768,128]{1,0:T(8,128)(2,1)S(1)} collective-permute-done((bf16[768,128]{1,0:T(8,128)(2,1)S(1)}, bf16[768,128]{1,0:T(8,128)(2,1)S(1)}, u32[]{:S(2)}, u32[]{:S(2)}) %collective-permute-start.18) | collective-permute-done | bytes 196640 | tf_op jit(solution)/shard_map/ppermute | solution.py:689
  111.9 2.9 %shard_map.200 = (f32[512,1024]{1,0:T(8,128)}, f32[1,1024]{1,0:T(1,128)}, f32[512,512]{1,0:T(8,128)}, f32[1,512]{1,0:T(1,128)}, f32[512,512]{1,0:T(8,128)}, /*in...) custom-call(bf16[2048,128]{1,0:T(8,128)(2,1)S(1)} %get-tuple-element.106.refs_0_, ...), custom_call_target="tpu_custom_call" | custom-call | tf_op jit(solution)/shard_map/pallas_call | solution.py:722
  (42 shorter events, 10.7 us)
Async XLA Ops:
  0.6 40.7 %copy-start.1 = (s32[8]{0:T(128)S(1)}, s32[8]{0:T(128)}, u32[]{:S(2)}) copy-start(s32[8]{0:T(128)} %tokens_ref.3) | copy-start | bytes 100
  0.7 40.7 %copy-start = (s32[8]{0:T(128)S(1)}, s32[8]{0:T(128)}, u32[]{:S(2)}) copy-start(s32[8]{0:T(128)} %lens_ref.3) | copy-start | bytes 100
  0.7 40.7 %copy-start.2 = (f32[8]{0:T(128)S(1)}, f32[8]{0:T(128)}, u32[]{:S(2)}) copy-start(f32[8]{0:T(128)} %scale_ref.1) | copy-start | bytes 100
  28.2 3.8 %collective-permute-start = (f32[1,1,24,128]{3,2,1,0:T(8,128)S(1)}, f32[1,1,24,128]{3,2,1,0:T(8,128)S(1)}, u32[]{:S(2)}, u32[]{:S(2)}) collective-permute-start(f32[1,1,24,128]{3,2,1,0:T(8,128)S(1)} %get-tuple-element.77.refs_0_), channel_id=1, source_target_pairs={{0,4},{1,5},{2,6},{3,7},{4,0},{5,1},{6,2},{7,3},{8,12},{9,13},{10,... | collective-permute-start | bytes 36872 | tf_op jit(solution)/shard_map/ppermute | solution.py:689
  32.0 3.9 %collective-permute-start.1 = (f32[2,1,24,128]{3,2,1,0:T(8,128)S(1)}, f32[2,1,24,128]{3,2,1,0:T(8,128)S(1)}, u32[]{:S(2)}, u32[]{:S(2)}) collective-permute-start(f32[2,1,24,128]{3,2,1,0:T(8,128)S(1)} %pad_maximum_fusion.1), channel_id=1, source_target_pairs={{0,8},{1,9},{2,10},{3,11},{4,12},{5,13},{6,14},{7,15},{8,0},{9,1},... | collective-permute-start | bytes 73736 | tf_op jit(solution)/shard_map/ppermute | solution.py:689
  35.9 5.5 %collective-permute-start.2 = (f32[4,1,24,128]{3,2,1,0:T(8,128)S(1)}, f32[4,1,24,128]{3,2,1,0:T(8,128)S(1)}, u32[]{:S(2)}, u32[]{:S(2)}) collective-permute-start(f32[4,1,24,128]{3,2,1,0:T(8,128)S(1)} %pad_maximum_fusion), channel_id=1, source_target_pairs={{0,16},{1,17},{2,18},{3,19},{4,20},{5,21},{6,22},{7,23},{8,24},{9,... | collective-permute-start | bytes 147464 | tf_op jit(solution)/shard_map/ppermute | solution.py:689
  49.7 8.8 %collective-permute-start.3 = (f32[2048,128]{1,0:T(8,128)S(1)}, f32[2048,128]{1,0:T(8,128)S(1)}, u32[]{:S(2)}, u32[]{:S(2)}) collective-permute-start(f32[2048,128]{1,0:T(8,128)S(1)} %get-tuple-element.79), channel_id=1, source_target_pairs={{0,1},{1,0},{2,3},{3,2},{4,5},{5,4},{6,7},{7,6},{8,9},{9,8},{10,11... | collective-permute-start | bytes 3145736 | tf_op jit(solution)/shard_map/ppermute | solution.py:689
  54.7 3.8 %collective-permute-start.4 = (f32[1536,128]{1,0:T(8,128)S(1)}, f32[1536,128]{1,0:T(8,128)S(1)}, u32[]{:S(2)}, u32[]{:S(2)}) collective-permute-start(f32[1536,128]{1,0:T(8,128)S(1)} %get-tuple-element.85), channel_id=1, source_target_pairs={{0,1},{1,0},{2,3},{3,2},{4,5},{5,4},{6,7},{7,6},{8,9},{9,8},{10,11... | collective-permute-start | bytes 2359304 | tf_op jit(solution)/shard_map/ppermute | solution.py:689
  58.7 8.7 %collective-permute-start.5 = (bf16[1024,128]{1,0:T(8,128)(2,1)S(1)}, bf16[1024,128]{1,0:T(8,128)(2,1)S(1)}, u32[]{:S(2)}, u32[]{:S(2)}) collective-permute-start(bf16[1024,128]{1,0:T(8,128)(2,1)S(1)} %get-tuple-element.87), channel_id=1, source_target_pairs={{0,4},{1,5},{2,6},{3,7},{4,0},{5,1},{6,2},{7,3},{8,12},{9,13},{10,... | collective-permute-start | bytes 786440 | tf_op jit(solution)/shard_map/ppermute | solution.py:689
  59.3 6.9 %collective-permute-start.6 = (bf16[768,128]{1,0:T(8,128)(2,1)S(1)}, bf16[768,128]{1,0:T(8,128)(2,1)S(1)}, u32[]{:S(2)}, u32[]{:S(2)}) collective-permute-start(bf16[768,128]{1,0:T(8,128)(2,1)S(1)} %get-tuple-element.89), channel_id=1, source_target_pairs={{0,2},{1,3},{2,0},{3,1},{4,6},{5,7},{6,4},{7,5},{8,10},{9,11},{10,... | collective-permute-start | bytes 589832 | tf_op jit(solution)/shard_map/ppermute | solution.py:689
  67.5 5.0 %collective-permute-start.7 = (bf16[512,128]{1,0:T(8,128)(2,1)S(1)}, bf16[512,128]{1,0:T(8,128)(2,1)S(1)}, u32[]{:S(2)}, u32[]{:S(2)}) collective-permute-start(bf16[512,128]{1,0:T(8,128)(2,1)S(1)} %get-tuple-element.91), channel_id=1, source_target_pairs={{0,2},{1,3},{2,0},{3,1},{4,6},{5,7},{6,4},{7,5},{8,10},{9,11},{10,... | collective-permute-start | bytes 393224 | tf_op jit(solution)/shard_map/ppermute | solution.py:689
  67.6 4.7 %collective-permute-start.8 = (bf16[384,128]{1,0:T(8,128)(2,1)S(1)}, bf16[384,128]{1,0:T(8,128)(2,1)S(1)}, u32[]{:S(2)}, u32[]{:S(2)}) collective-permute-start(bf16[384,128]{1,0:T(8,128)(2,1)S(1)} %get-tuple-element.93), channel_id=1, source_target_pairs={{0,8},{1,9},{2,10},{3,11},{4,12},{5,13},{6,14},{7,15},{8,0},{9,1},... | collective-permute-start | bytes 294920 | tf_op jit(solution)/shard_map/ppermute | solution.py:689
  72.5 5.0 %collective-permute-start.9 = (f32[256,128]{1,0:T(8,128)S(1)}, f32[256,128]{1,0:T(8,128)S(1)}, u32[]{:S(2)}, u32[]{:S(2)}) collective-permute-start(f32[256,128]{1,0:T(8,128)S(1)} %get-tuple-element.95), channel_id=1, source_target_pairs={{0,8},{1,9},{2,10},{3,11},{4,12},{5,13},{6,14},{7,15},{8,0},{9,1},... | collective-permute-start | bytes 393224 | tf_op jit(solution)/shard_map/ppermute | solution.py:689
  72.9 4.6 %collective-permute-start.10 = (f32[192,128]{1,0:T(8,128)S(1)}, f32[192,128]{1,0:T(8,128)S(1)}, u32[]{:S(2)}, u32[]{:S(2)}) collective-permute-start(f32[192,128]{1,0:T(8,128)S(1)} %get-tuple-element.97), channel_id=1, source_target_pairs={{0,4},{1,5},{2,6},{3,7},{4,0},{5,1},{6,2},{7,3},{8,12},{9,13},{10,... | collective-permute-start | bytes 294920 | tf_op jit(solution)/shard_map/ppermute | solution.py:689
  77.6 7.6 %collective-permute-start.11 = (f32[224,128]{1,0:T(8,128)S(1)}, f32[224,128]{1,0:T(8,128)S(1)}, u32[]{:S(2)}, u32[]{:S(2)}) collective-permute-start(f32[224,128]{1,0:T(8,128)S(1)} %get-tuple-element.99), channel_id=1, source_target_pairs={{0,16},{1,17},{2,18},{3,19},{4,20},{5,21},{6,22},{7,23},{8,24},{9,... | collective-permute-start | bytes 344072 | tf_op jit(solution)/shard_map/ppermute | solution.py:689
  85.2 5.8 %collective-permute-start.12 = (bf16[224,128]{1,0:T(8,128)(2,1)S(1)}, bf16[224,128]{1,0:T(8,128)(2,1)S(1)}, u32[]{:S(2)}, u32[]{:S(2)}) collective-permute-start(bf16[224,128]{1,0:T(8,128)(2,1)S(1)} %shard_map.195.refs_0_), channel_id=1, source_target_pairs={{0,16},{1,17},{2,18},{3,19},{4,20},{5,21},{6,22},{7,23},{8,24},{9,... | collective-permute-start | bytes 172040 | tf_op jit(solution)/shard_map/ppermute | solution.py:689
  91.0 4.3 %collective-permute-start.13 = (bf16[256,128]{1,0:T(8,128)(2,1)S(1)}, bf16[256,128]{1,0:T(8,128)(2,1)S(1)}, u32[]{:S(2)}, u32[]{:S(2)}) collective-permute-start(bf16[256,128]{1,0:T(8,128)(2,1)S(1)} %get-tuple-element.100.refs_0_), channel_id=1, source_target_pairs={{0,8},{1,9},{2,10},{3,11},{4,12},{5,13},{6,14},{7,15},{8,0},{9,1},... | collective-permute-start | bytes 196616 | tf_op jit(solution)/shard_map/ppermute | solution.py:689
  91.2 4.1 %collective-permute-start.14 = (bf16[192,128]{1,0:T(8,128)(2,1)S(1)}, bf16[192,128]{1,0:T(8,128)(2,1)S(1)}, u32[]{:S(2)}, u32[]{:S(2)}) collective-permute-start(bf16[192,128]{1,0:T(8,128)(2,1)S(1)} %get-tuple-element.101.refs_2_), channel_id=1, source_target_pairs={{0,4},{1,5},{2,6},{3,7},{4,0},{5,1},{6,2},{7,3},{8,12},{9,13},{10,... | collective-permute-start | bytes 147464 | tf_op jit(solution)/shard_map/ppermute | solution.py:689
  95.4 6.4 %collective-permute-start.15 = (bf16[512,128]{1,0:T(8,128)(2,1)S(1)}, bf16[512,128]{1,0:T(8,128)(2,1)S(1)}, u32[]{:S(2)}, u32[]{:S(2)}) collective-permute-start(bf16[512,128]{1,0:T(8,128)(2,1)S(1)} %get-tuple-element.102.refs_0_), channel_id=1, source_target_pairs={{0,2},{1,3},{2,0},{3,1},{4,6},{5,7},{6,4},{7,5},{8,10},{9,11},{10,... | collective-permute-start | bytes 393224 | tf_op jit(solution)/shard_map/ppermute | solution.py:689
  97.1 4.6 %collective-permute-start.16 = (bf16[384,128]{1,0:T(8,128)(2,1)S(1)}, bf16[384,128]{1,0:T(8,128)(2,1)S(1)}, u32[]{:S(2)}, u32[]{:S(2)}) collective-permute-start(bf16[384,128]{1,0:T(8,128)(2,1)S(1)} %get-tuple-element.103.refs_2_), channel_id=1, source_target_pairs={{0,8},{1,9},{2,10},{3,11},{4,12},{5,13},{6,14},{7,15},{8,0},{9,1},... | collective-permute-start | bytes 294920 | tf_op jit(solution)/shard_map/ppermute | solution.py:689
  101.8 7.5 %collective-permute-start.17 = (bf16[1024,128]{1,0:T(8,128)(2,1)S(1)}, bf16[1024,128]{1,0:T(8,128)(2,1)S(1)}, u32[]{:S(2)}, u32[]{:S(2)}) collective-permute-start(bf16[1024,128]{1,0:T(8,128)(2,1)S(1)} %get-tuple-element.104.refs_0_), channel_id=1, source_target_pairs={{0,4},{1,5},{2,6},{3,7},{4,0},{5,1},{6,2},{7,3},{8,12},{9,13},{10,... | collective-permute-start | bytes 786440 | tf_op jit(solution)/shard_map/ppermute | solution.py:689
  103.6 5.7 %collective-permute-start.18 = (bf16[768,128]{1,0:T(8,128)(2,1)S(1)}, bf16[768,128]{1,0:T(8,128)(2,1)S(1)}, u32[]{:S(2)}, u32[]{:S(2)}) collective-permute-start(bf16[768,128]{1,0:T(8,128)(2,1)S(1)} %get-tuple-element.105.refs_2_), channel_id=1, source_target_pairs={{0,2},{1,3},{2,0},{3,1},{4,6},{5,7},{6,4},{7,5},{8,10},{9,11},{10,... | collective-permute-start | bytes 589832 | tf_op jit(solution)/shard_map/ppermute | solution.py:689
  109.3 2.5 %collective-permute-start.19 = (bf16[2048,128]{1,0:T(8,128)(2,1)S(1)}, bf16[2048,128]{1,0:T(8,128)(2,1)S(1)}, u32[]{:S(2)}, u32[]{:S(2)}) collective-permute-start(bf16[2048,128]{1,0:T(8,128)(2,1)S(1)} %get-tuple-element.106.refs_0_), channel_id=1, source_target_pairs={{0,1},{1,0},{2,3},{3,2},{4,5},{5,4},{6,7},{7,6},{8,9},{9,8},{10,11... | collective-permute-start | bytes 1572872 | tf_op jit(solution)/shard_map/ppermute | solution.py:689
  109.4 2.5 %collective-permute-start.20 = (bf16[1536,128]{1,0:T(8,128)(2,1)S(1)}, bf16[1536,128]{1,0:T(8,128)(2,1)S(1)}, u32[]{:S(2)}, u32[]{:S(2)}) collective-permute-start(bf16[1536,128]{1,0:T(8,128)(2,1)S(1)} %get-tuple-element.107.refs_2_), channel_id=1, source_target_pairs={{0,1},{1,0},{2,3},{3,2},{4,5},{5,4},{6,7},{7,6},{8,9},{9,8},{10,11... | collective-permute-start | bytes 1179656 | tf_op jit(solution)/shard_map/ppermute | solution.py:689

commit v3 on v2

--- a/solution.py
+++ b/solution.py
@@ -14,6 +14,7 @@
 F32 = jnp.float32
 GROUP = 32
 SUB_UNITS = 4
+ORDERS = ((0, 1), (2, 1))
 AXES = ("frames", "tokens")
 
 
@@ -99,11 +100,27 @@
         load.wait()
 
 
+def entry(row_ref, place):
+    row = row_ref[...].astype(F32)
+    ids = lax.broadcasted_iota(jnp.int32, row.shape, 1)
+    return jnp.sum(jnp.where(ids == place, row, 0.0), axis=1, keepdims=True)
+
+
+def whole_number(row_ref, place):
+    return entry(row_ref, place).astype(jnp.int32)[0, 0]
+
+
+def first_of(seqs_here, offset_ref):
+    first_seq = lax.axis_index("tokens") * seqs_here
+    return first_seq if offset_ref is None else first_seq + whole_number(offset_ref, 0)
+
+
 def block_counts(lens_ref, tokens_ref, first_seq, first_frame):
     counts = []
     for s in range(2):
-        inside = first_frame < lens_ref[first_seq + s]
-        counts.append(jnp.where(inside, tokens_ref[first_seq + s] // SUB_UNITS + 1, 0))
+        inside = first_frame < whole_number(lens_ref, first_seq + s)
+        units = whole_number(tokens_ref, first_seq + s)
+        counts.append(jnp.where(inside, units // SUB_UNITS + 1, 0))
     return counts
 
 
@@ -111,8 +128,8 @@
     seqs_here,
     offset_ref,
     packets_ref,
-    lens_hbm,
-    tokens_hbm,
+    lens_ref,
+    tokens_ref,
     encoder_ref,
     encoder_weight_ref,
     encoder_bias_ref,
@@ -127,31 +144,23 @@
     blank_ref,
     label_ref,
     hidden_ref,
-    turned_ref,
     inverse_ref,
+    parts_ref,
     matrix_ref,
     even_ref,
     odd_ref,
     labels_smem,
     label_rows_ref,
-    lens_ref,
-    tokens_ref,
-    load_sems,
     label_sem,
 ):
-    loads = [
-        pltpu.make_async_copy(lens_hbm, lens_ref, load_sems.at[0]),
-        pltpu.make_async_copy(tokens_hbm, tokens_ref, load_sems.at[1]),
-    ]
-    for load in loads:
-        load.start()
     seqs, frame_count, width = encoder_ref.shape
     units = token_ref.shape[0] // seqs
     shards = label_rows_ref.shape[0]
     shard_units = units // shards
-    steps = frame_count + units - 1
+    part = frame_count // 2
+    steps = part + units - 1
     first_frame = lax.axis_index("frames") * frame_count
-    first_seq = lax.axis_index("tokens") * seqs_here + offset_ref[0]
+    first_seq = first_of(seqs_here, offset_ref)
     vocab = weight_ref.shape[1]
     blank_ref[...] = jnp.zeros_like(blank_ref)
     label_ref[...] = jnp.full(label_ref.shape, NEG, F32)
@@ -191,12 +200,13 @@
         .astype(F32)
         .reshape(frame_ref.shape)
     )
-    for load in loads:
-        load.wait()
 
     counts = block_counts(lens_ref, tokens_ref, first_seq, first_frame)
     blocks = counts[0] + counts[1]
+    lens = [whole_number(lens_ref, first_seq + s) for s in range(2)]
+    last_units = [whole_number(tokens_ref, first_seq + s) for s in range(2)]
     lanes = lane_ids(frame_count)
+    part_lanes = lane_ids(part)
     times = first_frame + lax.broadcasted_iota(jnp.int32, (frame_count, 1), 0)
 
     def place_of(i):
@@ -216,10 +226,6 @@
         )
         hidden_ref[block] = hidden
         low = hidden.astype(BF16)
-        turned_ref[block, :width, :] = low.T
-        turned_ref[block, width:, :] = jnp.ones(
-            (turned_ref.shape[1] - width, turned_ref.shape[2]), BF16
-        )
         logits_ref[...] = (
             jnp.dot(low, weight_ref[...], preferred_element_type=F32) + bias_ref[...]
         )
@@ -227,9 +233,9 @@
     def score(i, logits_ref):
         seq, sub, block = place_of(i)
         first_unit = sub * SUB_UNITS
-        seq_len = lens_ref[first_seq + seq]
-        last_unit = tokens_ref[first_seq + seq]
-        own_lanes = (lanes // GROUP) % 2 == seq
+        seq_len = jnp.where(seq == 0, lens[0], lens[1])
+        last_unit = jnp.where(seq == 0, last_units[0], last_units[1])
+        own_lanes = (part_lanes // GROUP) % 2 == seq
         logits = logits_ref[...]
         top = jnp.max(logits, axis=1, keepdims=True)
         weights = jnp.exp(logits - top)
@@ -254,7 +260,9 @@
                 NEG,
                 (picked - log_total[rows]) * LOG2E,
             )
-            at = (pl.ds(unit * (units + 1), frame_count, stride=units), slice(None))
+            at = (pl.ds(unit * (units + 1), part, stride=units), slice(None))
+            blank = jnp.where(part_lanes < 64, blank[:part], blank[part:])
+            step = jnp.where(part_lanes < 64, step[:part], step[part:])
             blank_ref[at] = jnp.where(own_lanes, blank, blank_ref[at])
             label_ref[at] = jnp.where(own_lanes, step, label_ref[at])
 
@@ -263,14 +271,44 @@
         lane_ids(units) % GROUP == lax.broadcasted_iota(jnp.int32, (units, 128), 0), 0.0, NEG
     ).astype(F32)
     ahead, behind = both_ways(blank_ref, label_ref, units, steps, eye, eye)
-    matrix_ref[0, 0] = jnp.where(lane_ids(units) < 64, behind, ahead)
+    lanes = lane_ids(units)
+    early = lanes < 64
+    columns = jnp.where(early, behind, ahead)
+    parts_ref[...] = columns
+    others = pltpu.roll(jnp.where(early, ahead, behind), 64, 1)
+    ways = [
+        jnp.take_along_axis(
+            columns, lanes // GROUP * GROUP + k, axis=1, mode="promise_in_bounds"
+        )
+        + others[k : k + 1, :]
+        for k in range(units)
+    ]
+    top = functools.reduce(jnp.maximum, ways)
+    total = functools.reduce(jnp.add, [jnp.exp2(way - top) for way in ways])
+    matrix_ref[0, 0] = top + jnp.log2(total)
+
+
+def turn_kernel(layout, offset_ref, lens_ref, tokens_ref, hidden_ref, turned_ref):
+    width = hidden_ref.shape[2]
+    first_frame = lax.axis_index("frames") * layout["frame_count"]
+    first_seq = first_of(layout["seqs_here"], offset_ref)
+    counts = block_counts(lens_ref, tokens_ref, first_seq, first_frame)
+
+    def one_block(i, _):
+        seq = jnp.where(i >= counts[0], 1, 0)
+        block = i + seq * (layout["units"] // SUB_UNITS - counts[0])
+        turned_ref[block, :width, :] = hidden_ref[block].astype(BF16).T
+        turned_ref[block, width:, :] = jnp.ones((16, turned_ref.shape[2]), BF16)
+        return 0
+
+    lax.fori_loop(0, counts[0] + counts[1], one_block, 0)
 
 
 def tangent_kernel(
     layout,
+    offset_ref,
     lens_ref,
     tokens_ref,
-    offset_ref,
     scale_ref,
     softmax_ref,
     label_table_ref,
@@ -278,6 +316,7 @@
     label_ref,
     turned_ref,
     inverse_ref,
+    parts_ref,
     *refs,
 ):
     hops = layout["hops"]
@@ -301,15 +340,14 @@
     ) = refs
     label_copy = pltpu.make_async_copy(label_table_ref, labels_smem, label_sem)
     label_copy.start()
-    sums_ref[...] = jnp.zeros_like(sums_ref)
-    output_bias_ref[...] = jnp.zeros_like(output_bias_ref)
     frame_count = layout["frame_count"]
     width = turned_ref.shape[1] - 16
     units = layout["units"]
-    steps = frame_count + units - 1
+    part = frame_count // 2
+    steps = part + units - 1
     here = lax.axis_index("frames")
     first_frame = here * frame_count
-    first_seq = lax.axis_index("tokens") * layout["seqs_here"] + offset_ref[0]
+    first_seq = first_of(layout["seqs_here"], offset_ref)
     chunks = matrices_ref.shape[0]
     vocab = softmax_ref.shape[2]
     at = 0
@@ -322,54 +360,64 @@
     gather_ids = lanes // GROUP * GROUP + starts
     own_first = (lane_ids(1) // GROUP) % 2 == 0
 
+    def through(column, matrix):
+        ways = column + matrix
+        top = jnp.max(ways, axis=0, keepdims=True)
+        row = top + jnp.log2(jnp.sum(jnp.exp2(ways - top), axis=0, keepdims=True))
+        row = jnp.broadcast_to(row, (units, 128))
+        return jnp.take_along_axis(row, gather_ids, axis=1, mode="promise_in_bounds")
+
     def one_chunk(i, carry):
         column, kept = carry
         other = chunks - 1 - i
         kept = jnp.where(jnp.where(early, i, other) == here, column, kept)
-        joined = column + jnp.where(early, matrices_ref[here ^ i], matrices_ref[here ^ other])
-        top = jnp.max(joined, axis=0, keepdims=True)
-        row = top + jnp.log2(jnp.sum(jnp.exp2(joined - top), axis=0, keepdims=True))
-        row = jnp.broadcast_to(row, (units, 128))
-        return jnp.take_along_axis(row, gather_ids, axis=1, mode="promise_in_bounds"), kept
+        matrix = jnp.where(early, matrices_ref[here ^ i], matrices_ref[here ^ other])
+        return through(column, matrix), kept
 
     start = jnp.where(early & (starts > 0), NEG, 0.0).astype(F32)
     last, kept = lax.fori_loop(0, chunks, one_chunk, (start, start))
-    swapped_halves = pltpu.roll(kept, 64, 1)
+    middle = pltpu.roll(through(kept, parts_ref[...]), 64, 1)
     both_ways(
         blank_ref,
         label_ref,
         units,
         steps,
-        jnp.where(early, kept, swapped_halves),
-        jnp.where(early, swapped_halves, kept),
+        jnp.where(early, kept, middle),
+        jnp.where(early, middle, kept),
         (ahead_ref, behind_ref),
     )
     log_norm = jnp.max(jnp.where(early, last, pltpu.roll(last, 64, 1)), axis=0, keepdims=True)
-    scale = jnp.where(own_first, scale_ref[first_seq], scale_ref[first_seq + 1])
-    length = jnp.where(own_first, lens_ref[first_seq], lens_ref[first_seq + 1])
-    bound = jnp.where(own_first, tokens_ref[first_seq], tokens_ref[first_seq + 1])
-    time_limit = jnp.minimum(length - first_frame, frame_count)
+    scale, length, bound = (
+        jnp.where(own_first, entry(ref, first_seq), entry(ref, first_seq + 1))
+        for ref in (scale_ref, lens_ref, tokens_ref)
+    )
+    length, bound = length.astype(jnp.int32), bound.astype(jnp.int32)
+    part_start = first_frame + jnp.where(lane_ids(1) < 64, 0, part)
+    last_diagonal = starts + jnp.minimum(length - part_start, part)
+    first_blank = jnp.where(starts <= bound, starts, steps)
+    first_label = jnp.where(starts < bound, starts, steps)
+    norm = log_norm - jnp.log2(scale)
 
     def one_diagonal(e, _):
         rows = pl.ds(pl.multiple_of(e * units, 8), units)
-        time = e - starts
         behind = behind_ref[rows, :]
-        base = ahead_ref[rows, :] - log_norm
-        live = (starts <= bound) & (time >= 0) & (time < time_limit)
+        base = ahead_ref[rows, :] - norm
+        before_end = last_diagonal > e
         blank_part_ref[rows, :] = jnp.where(
-            live, -scale * jnp.exp2(base + blank_ref[rows, :] + behind), 0.0
+            before_end & (first_blank <= e), jnp.exp2(base + blank_ref[rows, :] + behind), 0.0
         )
         label_part_ref[rows, :] = jnp.where(
-            live & (starts < bound),
-            -scale * jnp.exp2(base + label_ref[rows, :] + pltpu.roll(behind, units - 1, 0)),
+            before_end & (first_label <= e),
+            jnp.exp2(base + label_ref[rows, :] + pltpu.roll(behind, units - 1, 0)),
             0.0,
         )
         return 0
 
-    lax.fori_loop(0, steps, one_diagonal, 0, unroll=3)
+    lax.fori_loop(0, steps, one_diagonal, 0, unroll=5)
 
     counts = block_counts(lens_ref, tokens_ref, first_seq, first_frame)
     block_lanes = lane_ids(frame_count)
+    part_lanes = lane_ids(part)
 
     def place_of(i):
         seq = jnp.where(i >= counts[0], 1, 0)
@@ -382,30 +430,41 @@
     loss_ref[...] = spread + jnp.where(wide == first_seq + 1, loss[:, GROUP : GROUP + 1], 0.0)
     label_copy.wait()
 
+    counts_all = counts[0] + counts[1]
+    sums_ref[...] = jnp.zeros_like(sums_ref)
+    output_bias_ref[...] = jnp.zeros_like(output_bias_ref)
+
     def prepare(i, tangent_ref):
         seq, sub, block = place_of(i)
-        own_lanes = (block_lanes // GROUP) % 2 == seq
+        own_lanes = [part_lanes % GROUP + GROUP * (seq + 2 * half) for half in (0, 1)]
         for j in range(SUB_UNITS):
             unit = sub * SUB_UNITS + j
             rows = slice(j * frame_count, (j + 1) * frame_count)
-            at = (pl.ds(unit * (units + 1), frame_count, stride=units), slice(None))
-            blank, step = blank_part_ref[at], label_part_ref[at]
-            blank = jnp.where(own_lanes, blank, pltpu.roll(blank, GROUP, 1))
-            step = jnp.where(own_lanes, step, pltpu.roll(step, GROUP, 1))
-            both = -(blank + step) * inverse_ref[block, rows, :]
+            at = (pl.ds(unit * (units + 1), part, stride=units), slice(None))
+            blank, step = (
+                jnp.concatenate(
+                    [
+                        jnp.take_along_axis(ref[at], ids, axis=1, mode="promise_in_bounds")
+                        for ids in own_lanes
+                    ],
+                    axis=0,
+                )
+                for ref in (blank_part_ref, label_part_ref)
+            )
+            both = (blank + step) * inverse_ref[block, rows, :]
             for v in range(vocab // 128):
                 cut = slice(v * 128, (v + 1) * 128)
                 piece = softmax_ref[block, rows, cut] * both
                 if v == 0:
-                    piece = piece + jnp.where(block_lanes == 0, blank, 0.0)
+                    piece = piece - jnp.where(block_lanes == 0, blank, 0.0)
                 piece = piece.astype(BF16)
                 tangent_ref[rows, cut] = piece
                 tangents_ref[block, rows, cut] = piece
             label = labels_smem[0, seq * units + unit]
             cut = pl.ds(pl.multiple_of(label // 128 * 128, 128), 128)
             piece = softmax_ref[block, rows, cut] * both
-            piece = piece + jnp.where((block_lanes == 0) & (label < 128), blank, 0.0)
-            piece = (piece + jnp.where(block_lanes == label % 128, step, 0.0)).astype(BF16)
+            piece = piece - jnp.where((block_lanes == 0) & (label < 128), blank, 0.0)
+            piece = (piece - jnp.where(block_lanes == label % 128, step, 0.0)).astype(BF16)
             tangent_ref[rows, cut] = piece
             tangents_ref[block, rows, cut] = piece
 
@@ -416,7 +475,7 @@
             sums_ref[v * width : (v + 1) * width, :] += product[:width, v * 128 : (v + 1) * 128]
         output_bias_ref[...] += product[width : width + 1, :]
 
-    in_two_stages(counts[0] + counts[1], prepare, multiply, even_ref, odd_ref)
+    in_two_stages(counts_all, prepare, multiply, even_ref, odd_ref)
     part_halves(sums_ref, kept_refs, sems)
 
 
@@ -437,9 +496,9 @@
 
 def inner_kernel(
     layout,
+    offset_ref,
     lens_ref,
     tokens_ref,
-    offset_ref,
     tangents_ref,
     hidden_ref,
     weight_ref,
@@ -460,7 +519,7 @@
     units = token_sum_ref.shape[0] // seqs
     vocab = weight_ref.shape[1]
     first_frame = lax.axis_index("frames") * frame_count
-    first_seq = lax.axis_index("tokens") * layout["seqs_here"] + offset_ref[0]
+    first_seq = first_of(layout["seqs_here"], offset_ref)
     frame_sum_ref[...] = jnp.zeros_like(frame_sum_ref)
     token_sum_ref[...] = jnp.zeros_like(token_sum_ref)
     unset = slice(layout["token"], sums_ref.shape[0])
@@ -472,19 +531,15 @@
         sub = i - seq * counts[0]
         return seq, sub, seq * (units // SUB_UNITS) + sub
 
-    def multiply(i, product_ref):
-        _, _, block = place_of(i)
-        product_ref[...] = lax.dot_general(
-            tangents_ref[block],
-            weight_ref[...],
-            (((1,), (1,)), ((), ())),
-            preferred_element_type=F32,
-        )
-
-    def add_up(i, product_ref):
+    def product_of(tangents):
+        return lax.dot_general(
+            tangents, weight_ref[...], (((1,), (1,)), ((), ())), preferred_element_type=F32
+        )
+
+    def add_up(i, product):
         seq, sub, block = place_of(i)
         hidden = hidden_ref[block]
-        inner = product_ref[...] * (1.0 - hidden * hidden)
+        inner = product * (1.0 - hidden * hidden)
         total = frame_sum_ref[seq]
         for j in range(SUB_UNITS):
             rows = slice(j * frame_count, (j + 1) * frame_count)
@@ -494,7 +549,22 @@
             )
         frame_sum_ref[seq] = total
 
-    in_two_stages(counts[0] + counts[1], multiply, add_up, even_ref, odd_ref)
+    def multiply_two(n, product_ref):
+        both = [tangents_ref[place_of(2 * n + m)[2]] for m in (0, 1)]
+        product_ref[...] = product_of(jnp.concatenate(both, axis=0))
+
+    def add_up_two(n, product_ref):
+        half = product_ref.shape[0] // 2
+        add_up(2 * n, product_ref[:half])
+        add_up(2 * n + 1, product_ref[half:])
+
+    blocks = counts[0] + counts[1]
+    in_two_stages(blocks // 2, multiply_two, add_up_two, even_ref, odd_ref)
+
+    @pl.when(blocks % 2 == 1)
+    def _():
+        add_up(blocks - 1, product_of(tangents_ref[place_of(blocks - 1)[2]]))
+
     low = frame_sum_ref[...].reshape(seqs * frame_count, width).astype(BF16)
     frame_tangent_ref[...] = low
     product = lax.dot_general(
@@ -575,72 +645,92 @@
         joined_ref[other, :] = other_ref[...]
 
 
-def put_together(halves, full_refs, sems):
+def finish_kernel(
+    layout,
+    output_own_ref,
+    output_other_ref,
+    rest_own_ref,
+    rest_other_ref,
+    packets_ref,
+    predictor_weight_ref,
+    output_weight_hbm,
+    encoder_weight_hbm,
+    weight_gradient_hbm,
+    output_bias_ref,
+    encoder_bias_ref,
+    bias_gradient_ref,
+    predictor_gradient_ref,
+    losses_ref,
+    output_weight_ref,
+    encoder_weight_ref,
+    weight_gradient_ref,
+    tail_ref,
+    tokens_ref,
+    predictor_ref,
+    sems,
+):
+    width, vocab = output_weight_ref.shape
     place = lax.axis_index("tokens") & 1
     copies = []
-    for n, (full_ref, start) in enumerate(full_refs):
-        own_ref, other_ref = halves[2 * n : 2 * n + 2]
-        half = own_ref.shape[0]
-        for part, source in ((place, own_ref), (1 - place, other_ref)):
-            target = full_ref.at[pl.ds(pl.multiple_of(start + part * half, 16), half), :]
-            copies.append(pltpu.make_async_copy(source, target, sems.at[len(copies)]))
-    for copy in copies:
-        copy.start()
-    for copy in copies:
-        copy.wait()
-
-
-def finish_kernel(
-    layout,
-    *refs,
-):
-    halves, refs = refs[:4], refs[4:]
-    (
-        packets_ref,
-        predictor_weight_ref,
-        output_weight_ref,
-        output_bias_ref,
-        encoder_weight_ref,
-        encoder_bias_ref,
-        weight_gradient_ref,
-        bias_gradient_ref,
-        predictor_gradient_ref,
-        losses_ref,
-        output_ref,
-        full_ref,
-        tokens_ref,
-        predictor_ref,
-        sems,
-    ) = refs
-    put_together(halves, ((output_ref, 0), (full_ref, 0)), sems)
-    width, vocab = output_weight_ref.shape
-    for v in range(vocab // 128):
-        output_weight_ref[:, v * 128 : (v + 1) * 128] = output_ref[
-            v * width : (v + 1) * width, :
-        ].astype(F32)
+
+    def send(source, target):
+        copies.append(pltpu.make_async_copy(source, target, sems.at[len(copies)]))
+        copies[-1].start()
+
+    def in_order(own_ref, other_ref, body):
+        def reader(low_ref, high_ref):
+            def rows(start, stop):
+                half = low_ref.shape[0]
+                if stop <= half:
+                    return low_ref[start:stop, :]
+                if start >= half:
+                    return high_ref[start - half : stop - half, :]
+                return jnp.concatenate([low_ref[start:, :], high_ref[: stop - half, :]], axis=0)
+
+            return rows
+
+        @pl.when(place == 0)
+        def _():
+            body(reader(own_ref, other_ref))
+
+        @pl.when(place == 1)
+        def _():
+            body(reader(other_ref, own_ref))
+
+    chunk = width // 4
+
+    def unpack(target, start):
+        def body(rows):
+            for v in range(target.shape[1] // 128):
+                at = start + v * width
+                for r in range(0, width, chunk):
+                    target[r : r + chunk, v * 128 : (v + 1) * 128] = rows(
+                        at + r, at + r + chunk
+                    ).astype(F32)
+
+        return body
+
+    half = vocab // 2
+    for n in (0, 1):
+        columns = slice(n * half, (n + 1) * half)
+        in_order(
+            output_own_ref,
+            output_other_ref,
+            unpack(output_weight_ref.at[:, columns], n * half // 128 * width),
+        )
+        send(output_weight_ref.at[:, columns], output_weight_hbm.at[:, columns])
+    in_order(rest_own_ref, rest_other_ref, unpack(encoder_weight_ref, layout["encoder"]))
+    send(encoder_weight_ref, encoder_weight_hbm)
+    tail_start = layout["token"]
+
+    def keep_tail(rows):
+        tail_ref[...] = rows(tail_start, tail_start + tail_ref.shape[0]).astype(F32)
+
+    in_order(rest_own_ref, rest_other_ref, keep_tail)
+    count = layout["token_rows"]
     for v in range(width // 128):
-        at = layout["encoder"] + v * width
-        encoder_weight_ref[:, v * 128 : (v + 1) * 128] = full_ref[at : at + width, :].astype(F32)
-    rest = full_ref[layout["misc"] :, :].astype(F32)
-
-    def row(name, k):
-        at = layout[name] - layout["misc"] + k
-        return rest[at : at + 1, :]
-
-    output_bias_ref[...] = jnp.concatenate(
-        [row("output_bias", v) for v in range(vocab // 128)], axis=1
-    )
-    encoder_bias_ref[...] = jnp.concatenate(
-        [row("encoder_bias", v) for v in range(width // 128)], axis=1
-    )
-    count = layout["token_rows"]
-    tokens = jnp.concatenate(
-        [
-            full_ref[layout["token"] + v * count : layout["token"] + (v + 1) * count, :]
-            for v in range(width // 128)
-        ],
-        axis=1,
-    )
+        tokens_ref[:, v * 128 : (v + 1) * 128] = tail_ref[v * count : (v + 1) * count, :]
+    tokens = tokens_ref[...]
     held_rows = packets_ref.shape[1] - 2
     for d in range(packets_ref.shape[0]):
         predictor_ref[d * held_rows : (d + 1) * held_rows, :] = packets_ref[
@@ -648,13 +738,23 @@
         ].astype(F32)
     weight_gradient_ref[...] = lax.dot_general(
         predictor_ref[...].astype(BF16),
-        tokens,
+        tokens.astype(BF16),
         (((0,), (0,)), ((), ())),
         preferred_element_type=F32,
     )
-    wide = tokens.astype(F32)
-    bias_gradient_ref[...] = jnp.sum(wide, axis=0, keepdims=True)
-    tokens_ref[...] = wide
+    send(weight_gradient_ref, weight_gradient_hbm)
+
+    def row(name, k):
+        at = layout[name] - tail_start + k
+        return tail_ref[at : at + 1, :]
+
+    output_bias_ref[...] = jnp.concatenate(
+        [row("output_bias", v) for v in range(vocab // 128)], axis=1
+    )
+    encoder_bias_ref[...] = jnp.concatenate(
+        [row("encoder_bias", v) for v in range(width // 128)], axis=1
+    )
+    bias_gradient_ref[...] = jnp.sum(tokens, axis=0, keepdims=True)
     device = lax.axis_index("frames") * lax.axis_size("tokens") + lax.axis_index("tokens")
     mine = jnp.concatenate(
         [tokens_ref[pl.ds(device * held_rows + r, 1), :] for r in range(held_rows)], axis=0
@@ -669,6 +769,8 @@
     losses_ref[...] = jnp.sum(
         jnp.where(lane_ids(1) == lax.axis_index("frames"), loss, 0.0), axis=1, keepdims=True
     )
+    for copy in copies:
+        copy.wait()
 
 
 def in_hbm(array):
@@ -698,42 +800,53 @@
     return blocks
 
 
-def stages(shift):
+def stages(even, odd):
     frame_bits = [(1 << i, 0) for i in range(lax.axis_size("frames").bit_length() - 1)]
     token_bits = [(0, 1 << i) for i in range(1, lax.axis_size("tokens").bit_length() - 1)]
     first = frame_bits[:1] + token_bits + frame_bits[1:2]
-    return first[shift:] + first[:shift] + frame_bits[2:]
+    orders = [first[shift:] + first[:shift] + frame_bits[2:] for shift in (even, odd)]
+    return list(zip(*orders))
 
 
 def upper_of(stage):
-    return (lax.axis_index("frames") & stage[0]) | (lax.axis_index("tokens") & stage[1])
+    f, k = lax.axis_index("frames"), lax.axis_index("tokens")
+    even, odd = ((f & frame_bit) | (k & token_bit) for frame_bit, token_bit in stage)
+    return jnp.where((k & 1) == 0, even, odd)
 
 
 def across(stage):
-    return lambda f, k: (f ^ stage[0], k ^ stage[1])
+    return lambda f, k: (f ^ stage[k & 1][0], k ^ stage[k & 1][1])
 
 
 def neighbour(f, k):
     return f, k ^ 1
 
 
-def call(body, ins, outs, smem=(), scratch=(), limit=4):
+def call(body, ins, outs, scratch=(), limit=4):
     vmem = pl.BlockSpec(memory_space=pltpu.VMEM)
+    there = [array is not None for array in ins]
+
+    def kernel(*refs):
+        given = iter(refs)
+        body(*(next(given) if here else None for here in there), *given)
+
     return pl.pallas_call(
-        body,
-        in_specs=[pl.BlockSpec(memory_space=pltpu.SMEM)] * len(smem) + [vmem] * len(ins),
-        out_specs=[vmem] * len(outs),
+        kernel,
+        in_specs=[vmem] * sum(there),
+        out_specs=[
+            pl.BlockSpec(memory_space=pl.ANY) if inside is None else vmem for _, _, inside in outs
+        ],
         out_shape=[
             pltpu.VMEM(shape, kind) if inside else jax.ShapeDtypeStruct(shape, kind)
             for shape, kind, inside in outs
         ],
         scratch_shapes=list(scratch),
         compiler_params=pltpu.CompilerParams(vmem_limit_bytes=limit * 2**20),
-    )(*smem, *map(in_vmem, ins))
+    )(*(in_vmem(array) for array in ins if array is not None))
 
 
 def reduced_and_gathered(pieces):
-    plans = list(zip(*(stages(n) for n in range(len(pieces)))))
+    plans = list(zip(*(stages(*shifts) for shifts in ORDERS)))
     flat = [a for kept, sent in pieces for a in (kept, permuted(sent, neighbour))]
     way_back = []
     for number, plan in enumerate(plans):
@@ -744,11 +857,23 @@
         if merge:
             halves = [sum(halves)]
         sent_type = BF16 if number < 2 else F32
-        flat = call(
-            functools.partial(halve_kernel, plan, merge),
-            flat,
-            [out for half in halves for out in (((half, 128), F32, True), ((half, 128), sent_type, True))],
-        )
+        outs = [
+            out
+            for half in halves
+            for out in (((half, 128), F32, True), ((half, 128), sent_type, True))
+        ]
+        if number in (0, 1):
+            flat = [
+                a
+                for n, stage in enumerate(plan)
+                for a in call(
+                    functools.partial(halve_kernel, [stage], False),
+                    flat[2 * n : 2 * n + 2],
+                    outs[2 * n : 2 * n + 2],
+                )
+            ]
+        else:
+            flat = call(functools.partial(halve_kernel, plan, merge), flat, outs)
         flat = [
             permuted(a, across(plan[n // 2])) if n % 2 else a for n, a in enumerate(flat)
         ]
@@ -756,13 +881,20 @@
         call(last_kernel, flat[n : n + 2], [(flat[n].shape, BF16, True)])[0]
         for n in range(0, len(flat), 2)
     ]
-    for plan, merged, sizes in reversed(way_back):
+    for number, (plan, merged, sizes) in reversed(list(enumerate(way_back))):
         flat = [a for array, stage in zip(arrays, plan) for a in (array, permuted(array, across(stage)))]
-        arrays = call(
-            functools.partial(join_kernel, plan, merged),
-            flat,
-            [((size, 128), BF16, True) for size in sizes],
-        )
+        outs = [((size, 128), BF16, True) for size in sizes]
+        if number in (0,):
+            arrays = [
+                call(
+                    functools.partial(join_kernel, [stage], False),
+                    flat[2 * n : 2 * n + 2],
+                    outs[n : n + 1],
+                )[0]
+                for n, stage in enumerate(plan)
+            ]
+        else:
+            arrays = call(functools.partial(join_kernel, plan, merged), flat, outs)
     return [(array, permuted(array, neighbour)) for array in arrays]
 
 
@@ -789,9 +921,7 @@
     device_count = frame_axis * token_axis
     units = held_units * token_axis
     calls = seq_count // 2
-    steps = frame_count + units - 1
-    diagonals = (steps + 1) * units
-    smem = pl.BlockSpec(memory_space=pltpu.SMEM)
+    diagonals = (frame_count // 2 + units) * units
     vmem = pl.BlockSpec(memory_space=pltpu.VMEM)
     anywhere = pl.BlockSpec(memory_space=pl.ANY)
 
@@ -803,6 +933,9 @@
         predictor_bias.reshape(1, width),
         output_weight,
         output_bias.reshape(1, vocab),
+        frame_lens.reshape(1, all_seqs),
+        token_lens.reshape(1, all_seqs),
+        loss_scale.reshape(1, all_seqs),
     )
     packets, *weights = pl.pallas_call(
         packet_kernel,
@@ -817,6 +950,8 @@
         ],
         compiler_params=pltpu.CompilerParams(vmem_limit_bytes=4 * 2**20),
     )(*map(in_hbm, (predictor_out.reshape(held_units, width), labels, *weights)))
+    *weights, frame_lens, token_lens, loss_scale = weights
+    lens = frame_lens, token_lens
     packets = lax.all_to_all(packets, AXES, 0, 0, tiled=True)
 
     score_shapes = [
@@ -827,44 +962,33 @@
         ((diagonals, 128), F32),
         ((diagonals, 128), F32),
         ((2 * units // SUB_UNITS, SUB_UNITS * frame_count, width), F32),
-        ((2 * units // SUB_UNITS, width + 16, SUB_UNITS * frame_count), BF16),
         ((2 * units // SUB_UNITS, SUB_UNITS * frame_count, 128), F32),
+        ((units, 128), F32),
         ((1, 1, units, 128), F32),
     ]
 
-    def scores(given):
-        offset, encoder = given
-        return pl.pallas_call(
+    def scores(offset, encoder):
+        return call(
             functools.partial(score_kernel, seq_count),
-            in_specs=[smem, vmem] + [anywhere] * 2 + [vmem] * len(weights),
-            out_specs=[vmem] * len(score_shapes),
-            out_shape=[pltpu.VMEM(s, t) for s, t in score_shapes],
-            scratch_shapes=[
+            (offset, packets, *lens, encoder, *weights[1:]),
+            [(shape, kind, True) for shape, kind in score_shapes],
+            scratch=[
                 pltpu.VMEM((SUB_UNITS * frame_count, vocab), F32),
                 pltpu.VMEM((SUB_UNITS * frame_count, vocab), F32),
                 pltpu.SMEM((1, 128), jnp.int32),
                 pltpu.VMEM((token_axis, width), F32),
-                pltpu.SMEM(frame_lens.shape, jnp.int32),
-                pltpu.SMEM(token_lens.shape, jnp.int32),
-                pltpu.SemaphoreType.DMA((2,)),
                 pltpu.SemaphoreType.DMA,
             ],
-            compiler_params=pltpu.CompilerParams(vmem_limit_bytes=8 * 2**20),
-        )(
-            offset,
-            in_vmem(packets),
-            in_hbm(frame_lens),
-            in_hbm(token_lens),
-            *map(in_vmem, (encoder, *weights[1:])),
-        )
-
-    offsets = 2 * jnp.arange(calls, dtype=jnp.int32).reshape(calls, 1)
+            limit=8,
+        )
+
+    offsets = 2 * jnp.arange(calls, dtype=jnp.int32).reshape(calls, 1, 1)
     encoders = weights[0].reshape(calls, 2, frame_count, width)
     if calls == 1:
-        scored = scores((offsets[0], weights[0]))
+        scored = scores(None, weights[0])
         matrix = scored[-1]
     else:
-        scored = lax.map(scores, (offsets, encoders))
+        scored = lax.map(lambda given: scores(*given), (offsets, encoders))
         matrix = scored[-1].reshape(1, calls, units, 128)
 
     matrices = doubled(matrix)
@@ -887,20 +1011,31 @@
     blocks = 2 * units // SUB_UNITS
     block_rows = SUB_UNITS * frame_count
 
-    def tangents(offset, scored, matrices):
-        softmax, _, _, table, blank, label, _, turned, inverse = scored
-        given = (softmax, table, blank, label, turned, inverse, *matrices)
-        return pl.pallas_call(
+    def turns(offset, scored):
+        hidden = scored[6]
+        (turned,) = call(
+            functools.partial(turn_kernel, layout),
+            (offset, *lens, hidden),
+            [((hidden.shape[0], width + 16, hidden.shape[1]), BF16, True)],
+        )
+        return turned
+
+    def tangents(offset, scored, turned, matrices):
+        softmax, _, _, table, blank, label, _, inverse, parts = scored
+        return call(
             functools.partial(tangent_kernel, dict(layout, hops=len(matrices) - 1)),
-            in_specs=[smem] * 4 + [vmem] * len(given),
-            out_specs=[vmem] * 5,
-            out_shape=[
-                pltpu.VMEM((blocks, block_rows, vocab), BF16),
-                pltpu.VMEM((1, vocab), F32),
-                pltpu.VMEM((1, 128), F32),
-            ]
-            + [pltpu.VMEM((output_rows // 2, 128), F32)] * 2,
-            scratch_shapes=[
+            (
+                *(offset, *lens, loss_scale, softmax, table, blank, label),
+                *(turned, inverse, parts, *matrices),
+            ),
+            [
+                ((blocks, block_rows, vocab), BF16, True),
+                ((1, vocab), F32, True),
+                ((1, 128), F32, True),
+                ((output_rows // 2, 128), F32, True),
+                ((output_rows // 2, 128), F32, True),
+            ],
+            scratch=[
                 pltpu.VMEM((output_rows, 128), F32),
                 pltpu.VMEM((frame_axis, units, 128), F32),
                 pltpu.VMEM((diagonals, 128), F32),
@@ -913,26 +1048,24 @@
                 pltpu.SemaphoreType.DMA,
                 pltpu.SemaphoreType.DMA((4,)),
             ],
-            compiler_params=pltpu.CompilerParams(vmem_limit_bytes=12 * 2**20),
-        )(frame_lens, token_lens, offset, loss_scale, *map(in_vmem, given))
+            limit=12,
+        )
 
     def inners(offset, encoder, scored, tangent, output_bias_sum, loss):
-        given = (tangent, scored[6], weights[5], encoder, output_bias_sum, loss)
         return call(
             functools.partial(inner_kernel, layout),
-            given,
+            (offset, *lens, tangent, scored[6], weights[5], encoder, output_bias_sum, loss),
             [
                 ((2 * frame_count, width), BF16, True),
                 ((rest_rows // 2, 128), F32, True),
                 ((rest_rows // 2, 128), F32, True),
             ],
-            smem=(frame_lens, token_lens, offset),
             scratch=[
                 pltpu.VMEM((rest_rows, 128), F32),
                 pltpu.VMEM((2, frame_count, width), F32),
                 pltpu.VMEM((2 * units, width), F32),
-                pltpu.VMEM((block_rows, width), F32),
-                pltpu.VMEM((block_rows, width), F32),
+                pltpu.VMEM((2 * block_rows, width), F32),
+                pltpu.VMEM((2 * block_rows, width), F32),
                 pltpu.SemaphoreType.DMA((2,)),
             ],
             limit=10,
@@ -947,10 +1080,11 @@
 
     if calls == 1:
         scored = scored[:-1]
-        tangent, output_bias_sum, loss, *output_sums = tangents(offsets[0], scored, matrices)
+        turned = turns(None, scored)
+        tangent, output_bias_sum, loss, *output_sums = tangents(None, scored, turned, matrices)
 
         frame_tangent, *rest = inners(
-            offsets[0], weights[0], scored, tangent, output_bias_sum, loss
+            None, weights[0], scored, tangent, output_bias_sum, loss
         )
         sums = [*output_sums, *rest]
         encoder_gradient = encoder_gradient_of(frame_tangent)
@@ -959,7 +1093,8 @@
         def add_call(sums, given):
             offset, encoder, scored, call = given
             own = [lax.dynamic_slice_in_dim(m, call, 1, 1) for m in matrices]
-            tangent, output_bias_sum, loss, *more = tangents(offset, scored, own)
+            turned = turns(offset, scored)
+            tangent, output_bias_sum, loss, *more = tangents(offset, scored, turned, own)
             frame_tangent, *rest = inners(
                 offset, encoder, scored, tangent, output_bias_sum, loss
             )
@@ -974,25 +1109,29 @@
         encoder_gradient = encoder_gradient.reshape(encoder_out.shape)
 
     halves = reduced_and_gathered(list(zip(sums[::2], sums[1::2])))
+    tail_rows = width // 128 * all_seqs * units + vocab // 128 + width // 128 + 3
+    tail_rows += -tail_rows % 16
     finished = call(
         functools.partial(finish_kernel, layout),
         [*(a for pair in halves for a in pair), packets, weights[3]],
         [
-            ((width, vocab), F32, False),
+            ((width, vocab), F32, None),
+            ((width, width), F32, None),
+            ((width, width), F32, None),
             ((1, vocab), F32, False),
-            ((width, width), F32, False),
             ((1, width), F32, False),
-            ((width, width), F32, False),
             ((1, width), F32, False),
             ((held_units, 1, width), F32, False),
             ((1, 1), F32, False),
         ],
         scratch=[
-            pltpu.VMEM((output_rows, 128), BF16),
-            pltpu.VMEM((rest_rows, 128), BF16),
+            pltpu.VMEM((width, vocab), F32),
+            pltpu.VMEM((width, width), F32),
+            pltpu.VMEM((width, width), F32),
+            pltpu.VMEM((tail_rows, 128), F32),
             pltpu.VMEM((all_seqs * units, width), F32),
             pltpu.VMEM((all_seqs * units, width), F32),
-            pltpu.SemaphoreType.DMA((6,)),
+            pltpu.SemaphoreType.DMA((4,)),
         ],
         limit=20,
     )
@@ -1000,12 +1139,12 @@
         finished[7].reshape(1),
         encoder_gradient,
         finished[6].transpose(1, 0, 2),
+        finished[1],
+        finished[4].reshape(width),
         finished[2],
-        finished[3].reshape(width),
-        finished[4],
         finished[5].reshape(width),
         finished[0],
-        finished[1].reshape(vocab),
+        finished[3].reshape(vocab),
     )
 
 

time: 117 us -> 108 us (0.923)
  starting transfers between devices: 17.1 us -> 9.11 us
    ppermute x21, starting transfers between devices: 17.1 us -> 9.11 us  [permuted(): return lax.ppermute(array, AXES, pairs)]
    pallas_call x14 -> x18, Pallas kernels: 25.1 us -> 24.7 us  [call(): pl.pallas_call(kernel, in_specs=[vmem] * sum(there), out_specs=[pl.BlockS...]
  transfers between devices with their start and end apart: 21 -> 21, of which waited for: 16 -> 18; matrix products, arithmetic and copies ran while one was open for 0% -> 0% of each run, Pallas kernels for 5% -> 7%
where the time goes in v3:
time: 108 us; the launch traced here: 106 us
  waiting for transfers between devices  51.4 us (48%)
  Pallas kernels  26.5 us (25%)
  blocking collectives  17.7 us (16%)
  starting transfers between devices  9.11 us (8%)
    ppermute x21, waiting for transfers between devices, permuted(): return lax.ppermute(array, AXES, pairs)  51.4 us
    pallas_call x18, Pallas kernels, call(): pl.pallas_call(kernel, in_specs=[vmem] * sum(there), out_specs=[pl.BlockS...  24.7 us
    all_to_all x1, blocking collectives, per_device(): packets = lax.all_to_all(packets, AXES, 0, 0, tiled=True)  17.7 us
    ppermute x21, starting transfers between devices, permuted(): return lax.ppermute(array, AXES, pairs)  9.11 us
  transfers between devices with their start and end apart: 21, of which 18 were waited for; matrix products, arithmetic and copies ran while one was open for 0% of the time, Pallas kernels for 7%

profile of v3, /device:TPU:0, one launch (start us, length us, event | category | flops | bytes accessed | tf_op | source)
XLA Modules:
  0.0 105.5 jit_solution(351964335904822529)
XLA Ops:
  0.6 1.8 %shard_map.187 = (bf16[32,8,512]{2,1,0:T(8,128)(2,1)S(1)}, bf16[2,64,512]{2,1,0:T(8,128)(2,1)S(1)}, bf16[512,512]{1,0:T(8,128)(2,1)S(1)}, f32[1,512]{1,0:T(1,128...) custom-call(bf16[6,512]{1,0:T(8,128)(2,1)} %bitcast.12, ...), custom_call_target="tpu_custom_call" | custom-call | tf_op jit(solution)/shard_map/pallas_call | solution.py:940
  2.5 17.7 %all_to_all.5.refs_0_.refs_4_ = bf16[32,8,512]{2,1,0:T(8,128)(2,1)S(1)} all-to-all(bf16[32,8,512]{2,1,0:T(8,128)(2,1)S(1)} %get-tuple-element.67), channel_id=1, replica_groups=mesh['frames'=8,'tokens'=4] {'frames','tokens'}, dimensions={0} | all-to-all | bytes 524288 | tf_op jit(solution)/shard_map/all_to_all | solution.py:955
  20.2 7.4 %shard_map.188 = (f32[12,256,1024]{2,1,0:T(8,128)S(1)}, f32[2,64,512]{2,1,0:T(8,128)}, f32[48,512]{1,0:T(8,128)}, s32[1,128]{1,0:T(1,128)S(1)}, f32[1344,128]{1,...) custom-call(bf16[32,8,512]{2,1,0:T(8,128)(2,1)S(1)} %all_to_all.5.re, ...), custom_call_target="tpu_custom_call" | custom-call | tf_op jit(solution)/shard_map/pallas_call | solution.py:833
  27.6 1.0 collective-permute-start
  28.5 2.8 %collective-permute-done.refs_11_ = f32[1,1,24,128]{3,2,1,0:T(8,128)S(1)} collective-permute-done((f32[1,1,24,128]{3,2,1,0:T(8,128)S(1)}, f32[1,1,24,128]{3,2,1,0:T(8,128)S(1)}, u32[]{:S(2)}, u32[]{:S(2)}) %collective-permute-start) | collective-permute-done | bytes 12320 | tf_op jit(solution)/shard_map/ppermute | solution.py:791
  31.3 3.8 %collective-permute-done.1.refs_12_ = f32[2,1,24,128]{3,2,1,0:T(8,128)S(1)} collective-permute-done((f32[2,1,24,128]{3,2,1,0:T(8,128)S(1)}, f32[2,1,24,128]{3,2,1,0:T(8,128)S(1)}, u32[]{:S(2)}, u32[]{:S(2)}) %collective-permute-start.1) | collective-permute-done | bytes 24608 | tf_op jit(solution)/shard_map/ppermute | solution.py:791
  35.2 1.1 %shard_map.189.refs_7_ = bf16[12,528,256]{2,1,0:T(8,128)(2,1)S(1)} custom-call(s32[1,8]{1,0:T(1,128)S(1)} %get-tuple-element.64.refs_1_.refs_0_, s32[1,8]{1,0:T(1,128)S(1)} %get-tuple-element.65.refs_2_.refs_1_, f32[12,256,512]{2,1,0:T(8,128)S(1)} %get-tuple-element.79.refs_2_.refs_3_), custom_call_target="tpu_custom_call" | custom-call | tf_op jit(solution)/shard_map/pallas_call | solution.py:833
  36.3 4.0 %collective-permute-done.2.refs_13_ = f32[4,1,24,128]{3,2,1,0:T(8,128)S(1)} collective-permute-done((f32[4,1,24,128]{3,2,1,0:T(8,128)S(1)}, f32[4,1,24,128]{3,2,1,0:T(8,128)S(1)}, u32[]{:S(2)}, u32[]{:S(2)}) %collective-permute-start.2) | collective-permute-done | bytes 49184 | tf_op jit(solution)/shard_map/ppermute | solution.py:791
  40.3 7.4 %shard_map.190 = (bf16[12,256,1024]{2,1,0:T(8,128)(2,1)S(1)}, f32[1,1024]{1,0:T(1,128)S(1)}, f32[1,128]{1,0:T(1,128)S(1)}, f32[2048,128]{1,0:T(8,128)S(1)}, f32[2048,128]{1,0:T(8,128)S(1)}) custom-call(s32[1,8]{1,0:T(1,128)S(1)} %get-tuple-element.64.refs_1_.refs_0_, s32[1,8]{1,0:T(1,128)S(1)} %get-tuple-element.65.refs_2_.refs_1_, ...), custom_call_target="tpu_custom_call" | custom-call | tf_op jit(solution)/shard_map/pallas_call | solution.py:833
  47.8 4.4 %shard_map.193 = (bf16[128,512]{1,0:T(8,128)(2,1)S(1)}, f32[1536,128]{1,0:T(8,128)S(1)}, f32[1536,128]{1,0:T(8,128)S(1)}) custom-call(s32[1,8]{1,0:T(1,128)S(1)} %get-tuple-element.64.refs_1_.refs_0_, s32[1,8]{1,0:T(1,128)S(1)} %get-tuple-element.65.refs_2_.refs_1_, bf16[12,256,1024]{2,1,0:T(8,128)(2,1)S(1)} %get-tuple-element.89.refs_2_, ...), custom_call_target="tpu_custom_call" | custom-call | tf_op jit(solution)/shard_map/pallas_call | solution.py:833
  53.3 1.3 %collective-permute-done.6.refs_1_ = f32[1536,128]{1,0:T(8,128)S(1)} collective-permute-done((f32[1536,128]{1,0:T(8,128)S(1)}, f32[1536,128]{1,0:T(8,128)S(1)}, u32[]{:S(2)}, u32[]{:S(2)}) %collective-permute-start.6) | collective-permute-done | bytes 786464 | tf_op jit(solution)/shard_map/ppermute | solution.py:791
  54.7 4.1 %collective-permute-done.4.refs_1_ = bf16[1024,128]{1,0:T(8,128)(2,1)S(1)} collective-permute-done((bf16[1024,128]{1,0:T(8,128)(2,1)S(1)}, bf16[1024,128]{1,0:T(8,128)(2,1)S(1)}, u32[]{:S(2)}, u32[]{:S(2)}) %collective-permute-start.4) | collective-permute-done | bytes 262176 | tf_op jit(solution)/shard_map/ppermute | solution.py:791
  59.0 1.4 %collective-permute-done.7.refs_1_ = bf16[768,128]{1,0:T(8,128)(2,1)S(1)} collective-permute-done((bf16[768,128]{1,0:T(8,128)(2,1)S(1)}, bf16[768,128]{1,0:T(8,128)(2,1)S(1)}, u32[]{:S(2)}, u32[]{:S(2)}) %collective-permute-start.7) | collective-permute-done | bytes 196640 | tf_op jit(solution)/shard_map/ppermute | solution.py:791
  61.3 3.8 %collective-permute-done.8.refs_3_ = bf16[384,128]{1,0:T(8,128)(2,1)S(1)} collective-permute-done((bf16[384,128]{1,0:T(8,128)(2,1)S(1)}, bf16[384,128]{1,0:T(8,128)(2,1)S(1)}, u32[]{:S(2)}, u32[]{:S(2)}) %collective-permute-start.8) | collective-permute-done | bytes 98336 | tf_op jit(solution)/shard_map/ppermute | solution.py:791
  65.9 4.0 %collective-permute-done.10.refs_3_ = f32[192,128]{1,0:T(8,128)S(1)} collective-permute-done((f32[192,128]{1,0:T(8,128)S(1)}, f32[192,128]{1,0:T(8,128)S(1)}, u32[]{:S(2)}, u32[]{:S(2)}) %collective-permute-start.10) | collective-permute-done | bytes 98336 | tf_op jit(solution)/shard_map/ppermute | solution.py:791
  70.3 8.2 %collective-permute-done.11.refs_1_ = f32[224,128]{1,0:T(8,128)S(1)} collective-permute-done((f32[224,128]{1,0:T(8,128)S(1)}, f32[224,128]{1,0:T(8,128)S(1)}, u32[]{:S(2)}, u32[]{:S(2)}) %collective-permute-start.11) | collective-permute-done | bytes 114720 | tf_op jit(solution)/shard_map/ppermute | solution.py:791
  78.6 5.1 %collective-permute-done.12.refs_1_ = bf16[224,128]{1,0:T(8,128)(2,1)S(1)} collective-permute-done((bf16[224,128]{1,0:T(8,128)(2,1)S(1)}, bf16[224,128]{1,0:T(8,128)(2,1)S(1)}, u32[]{:S(2)}, u32[]{:S(2)}) %collective-permute-start.12) | collective-permute-done | bytes 57376 | tf_op jit(solution)/shard_map/ppermute | solution.py:791
  84.0 3.9 %collective-permute-done.14.refs_3_ = bf16[192,128]{1,0:T(8,128)(2,1)S(1)} collective-permute-done((bf16[192,128]{1,0:T(8,128)(2,1)S(1)}, bf16[192,128]{1,0:T(8,128)(2,1)S(1)}, u32[]{:S(2)}, u32[]{:S(2)}) %collective-permute-start.14) | collective-permute-done | bytes 49184 | tf_op jit(solution)/shard_map/ppermute | solution.py:791
  88.7 0.9 collective-permute-start.16
  89.6 3.7 %collective-permute-done.16.refs_3_ = bf16[384,128]{1,0:T(8,128)(2,1)S(1)} collective-permute-done((bf16[384,128]{1,0:T(8,128)(2,1)S(1)}, bf16[384,128]{1,0:T(8,128)(2,1)S(1)}, u32[]{:S(2)}, u32[]{:S(2)}) %collective-permute-start.16) | collective-permute-done | bytes 98336 | tf_op jit(solution)/shard_map/ppermute | solution.py:791
  94.3 2.9 %collective-permute-start.19 = (bf16[768,128]{1,0:T(8,128)(2,1)S(1)}, bf16[768,128]{1,0:T(8,128)(2,1)S(1)}, u32[]{:S(2)}, u32[]{:S(2)}) collective-permute-start(bf16[768,128]{1,0:T(8,128)(2,1)S(1)} %get-tuple-element.109.refs_0_), channel_id=1, source_target_pairs={{0,8},{1,3},{2,10},{3,1},{4,12},{5,7},{6,14},{7,5},{8,0},{9,11},{1... | collective-permute-start | bytes 589832 | tf_op jit(solution)/shard_map/ppermute | solution.py:791
  97.2 2.9 %collective-permute-done.17.refs_1_ = bf16[1024,128]{1,0:T(8,128)(2,1)S(1)} collective-permute-done((bf16[1024,128]{1,0:T(8,128)(2,1)S(1)}, bf16[1024,128]{1,0:T(8,128)(2,1)S(1)}, u32[]{:S(2)}, u32[]{:S(2)}) %collective-permute-start.17) | collective-permute-done | bytes 262176 | tf_op jit(solution)/shard_map/ppermute | solution.py:791
  101.0 1.0 shard_map.205
  102.8 2.8 %shard_map.204 = (f32[512,1024]{1,0:T(8,128)}, f32[512,512]{1,0:T(8,128)}, f32[512,512]{1,0:T(8,128)}, f32[1,1024]{1,0:T(1,128)}, f32[1,512]{1,0:T(1,128)}, /*in...) custom-call(bf16[2048,128]{1,0:T(8,128)(2,1)S(1)} %shard_map.202.refs_0_, ...), custom_call_target="tpu_custom_call" | custom-call | tf_op jit(solution)/shard_map/pallas_call | solution.py:833
  (40 shorter events, 7.2 us)
Async XLA Ops:
  27.6 3.8 %collective-permute-start = (f32[1,1,24,128]{3,2,1,0:T(8,128)S(1)}, f32[1,1,24,128]{3,2,1,0:T(8,128)S(1)}, u32[]{:S(2)}, u32[]{:S(2)}) collective-permute-start(f32[1,1,24,128]{3,2,1,0:T(8,128)S(1)} %get-tuple-element.82.refs_10_), channel_id=1, source_target_pairs={{0,4},{1,5},{2,6},{3,7},{4,0},{5,1},{6,2},{7,3},{8,12},{9,13},{10,... | collective-permute-start | bytes 36872 | tf_op jit(solution)/shard_map/ppermute | solution.py:791
  31.3 3.8 %collective-permute-start.1 = (f32[2,1,24,128]{3,2,1,0:T(8,128)S(1)}, f32[2,1,24,128]{3,2,1,0:T(8,128)S(1)}, u32[]{:S(2)}, u32[]{:S(2)}) collective-permute-start(f32[2,1,24,128]{3,2,1,0:T(8,128)S(1)} %pad_maximum_fusion.1), channel_id=1, source_target_pairs={{0,8},{1,9},{2,10},{3,11},{4,12},{5,13},{6,14},{7,15},{8,0},{9,1},... | collective-permute-start | bytes 73736 | tf_op jit(solution)/shard_map/ppermute | solution.py:791
  35.2 5.1 %collective-permute-start.2 = (f32[4,1,24,128]{3,2,1,0:T(8,128)S(1)}, f32[4,1,24,128]{3,2,1,0:T(8,128)S(1)}, u32[]{:S(2)}, u32[]{:S(2)}) collective-permute-start(f32[4,1,24,128]{3,2,1,0:T(8,128)S(1)} %pad_maximum_fusion), channel_id=1, source_target_pairs={{0,16},{1,17},{2,18},{3,19},{4,20},{5,21},{6,22},{7,23},{8,24},{9,... | collective-permute-start | bytes 147464 | tf_op jit(solution)/shard_map/ppermute | solution.py:791
  47.7 4.6 %collective-permute-start.3 = (f32[2048,128]{1,0:T(8,128)S(1)}, f32[2048,128]{1,0:T(8,128)S(1)}, u32[]{:S(2)}, u32[]{:S(2)}) collective-permute-start(f32[2048,128]{1,0:T(8,128)S(1)} %get-tuple-element.84), channel_id=1, source_target_pairs={{0,1},{1,0},{2,3},{3,2},{4,5},{5,4},{6,7},{7,6},{8,9},{9,8},{10,11... | collective-permute-start | bytes 3145736 | tf_op jit(solution)/shard_map/ppermute | solution.py:791
  52.2 2.4 %collective-permute-start.6 = (f32[1536,128]{1,0:T(8,128)S(1)}, f32[1536,128]{1,0:T(8,128)S(1)}, u32[]{:S(2)}, u32[]{:S(2)}) collective-permute-start(f32[1536,128]{1,0:T(8,128)S(1)} %get-tuple-element.93), channel_id=1, source_target_pairs={{0,1},{1,0},{2,3},{3,2},{4,5},{5,4},{6,7},{7,6},{8,9},{9,8},{10,11... | collective-permute-start | bytes 2359304 | tf_op jit(solution)/shard_map/ppermute | solution.py:791
  52.4 6.4 %collective-permute-start.4 = (bf16[1024,128]{1,0:T(8,128)(2,1)S(1)}, bf16[1024,128]{1,0:T(8,128)(2,1)S(1)}, u32[]{:S(2)}, u32[]{:S(2)}) collective-permute-start(bf16[1024,128]{1,0:T(8,128)(2,1)S(1)} %get-tuple-element.86), channel_id=1, source_target_pairs={{0,4},{1,3},{2,6},{3,1},{4,0},{5,7},{6,2},{7,5},{8,12},{9,11},{10,... | collective-permute-start | bytes 786440 | tf_op jit(solution)/shard_map/ppermute | solution.py:791
  54.7 5.7 %collective-permute-start.7 = (bf16[768,128]{1,0:T(8,128)(2,1)S(1)}, bf16[768,128]{1,0:T(8,128)(2,1)S(1)}, u32[]{:S(2)}, u32[]{:S(2)}) collective-permute-start(bf16[768,128]{1,0:T(8,128)(2,1)S(1)} %get-tuple-element.95), channel_id=1, source_target_pairs={{0,8},{1,3},{2,10},{3,1},{4,12},{5,7},{6,14},{7,5},{8,0},{9,11},{1... | collective-permute-start | bytes 589832 | tf_op jit(solution)/shard_map/ppermute | solution.py:791
  58.9 6.2 %collective-permute-start.5 = (bf16[512,128]{1,0:T(8,128)(2,1)S(1)}, bf16[512,128]{1,0:T(8,128)(2,1)S(1)}, u32[]{:S(2)}, u32[]{:S(2)}) collective-permute-start(bf16[512,128]{1,0:T(8,128)(2,1)S(1)} %get-tuple-element.88), channel_id=1, source_target_pairs={{0,2},{1,9},{2,0},{3,11},{4,6},{5,13},{6,4},{7,15},{8,10},{9,1},{1... | collective-permute-start | bytes 393224 | tf_op jit(solution)/shard_map/ppermute | solution.py:791
  60.4 4.7 %collective-permute-start.8 = (bf16[384,128]{1,0:T(8,128)(2,1)S(1)}, bf16[384,128]{1,0:T(8,128)(2,1)S(1)}, u32[]{:S(2)}, u32[]{:S(2)}) collective-permute-start(bf16[384,128]{1,0:T(8,128)(2,1)S(1)} %get-tuple-element.97), channel_id=1, source_target_pairs={{0,4},{1,9},{2,6},{3,11},{4,0},{5,13},{6,2},{7,15},{8,12},{9,1},{1... | collective-permute-start | bytes 294920 | tf_op jit(solution)/shard_map/ppermute | solution.py:791
  65.2 5.0 %collective-permute-start.9 = (f32[256,128]{1,0:T(8,128)S(1)}, f32[256,128]{1,0:T(8,128)S(1)}, u32[]{:S(2)}, u32[]{:S(2)}) collective-permute-start(f32[256,128]{1,0:T(8,128)S(1)} %get-tuple-element.99), channel_id=1, source_target_pairs={{0,8},{1,5},{2,10},{3,7},{4,12},{5,1},{6,14},{7,3},{8,0},{9,13},{1... | collective-permute-start | bytes 393224 | tf_op jit(solution)/shard_map/ppermute | solution.py:791
  65.2 4.7 %collective-permute-start.10 = (f32[192,128]{1,0:T(8,128)S(1)}, f32[192,128]{1,0:T(8,128)S(1)}, u32[]{:S(2)}, u32[]{:S(2)}) collective-permute-start(f32[192,128]{1,0:T(8,128)S(1)} %get-tuple-element.101), channel_id=1, source_target_pairs={{0,2},{1,5},{2,0},{3,7},{4,6},{5,1},{6,4},{7,3},{8,10},{9,13},{10,... | collective-permute-start | bytes 294920 | tf_op jit(solution)/shard_map/ppermute | solution.py:791
  70.2 8.3 %collective-permute-start.11 = (f32[224,128]{1,0:T(8,128)S(1)}, f32[224,128]{1,0:T(8,128)S(1)}, u32[]{:S(2)}, u32[]{:S(2)}) collective-permute-start(f32[224,128]{1,0:T(8,128)S(1)} %get-tuple-element.103), channel_id=1, source_target_pairs={{0,16},{1,17},{2,18},{3,19},{4,20},{5,21},{6,22},{7,23},{8,24},{9,... | collective-permute-start | bytes 344072 | tf_op jit(solution)/shard_map/ppermute | solution.py:791
  78.5 5.1 %collective-permute-start.12 = (bf16[224,128]{1,0:T(8,128)(2,1)S(1)}, bf16[224,128]{1,0:T(8,128)(2,1)S(1)}, u32[]{:S(2)}, u32[]{:S(2)}) collective-permute-start(bf16[224,128]{1,0:T(8,128)(2,1)S(1)} %shard_map.198.refs_0_), channel_id=1, source_target_pairs={{0,16},{1,17},{2,18},{3,19},{4,20},{5,21},{6,22},{7,23},{8,24},{9,... | collective-permute-start | bytes 172040 | tf_op jit(solution)/shard_map/ppermute | solution.py:791
  83.7 4.6 %collective-permute-start.13 = (bf16[256,128]{1,0:T(8,128)(2,1)S(1)}, bf16[256,128]{1,0:T(8,128)(2,1)S(1)}, u32[]{:S(2)}, u32[]{:S(2)}) collective-permute-start(bf16[256,128]{1,0:T(8,128)(2,1)S(1)} %get-tuple-element.104.refs_0_), channel_id=1, source_target_pairs={{0,8},{1,5},{2,10},{3,7},{4,12},{5,1},{6,14},{7,3},{8,0},{9,13},{1... | collective-permute-start | bytes 196616 | tf_op jit(solution)/shard_map/ppermute | solution.py:791
  83.8 4.2 %collective-permute-start.14 = (bf16[192,128]{1,0:T(8,128)(2,1)S(1)}, bf16[192,128]{1,0:T(8,128)(2,1)S(1)}, u32[]{:S(2)}, u32[]{:S(2)}) collective-permute-start(bf16[192,128]{1,0:T(8,128)(2,1)S(1)} %get-tuple-element.105.refs_2_), channel_id=1, source_target_pairs={{0,2},{1,5},{2,0},{3,7},{4,6},{5,1},{6,4},{7,3},{8,10},{9,13},{10,... | collective-permute-start | bytes 147464 | tf_op jit(solution)/shard_map/ppermute | solution.py:791
  88.3 5.4 %collective-permute-start.15 = (bf16[512,128]{1,0:T(8,128)(2,1)S(1)}, bf16[512,128]{1,0:T(8,128)(2,1)S(1)}, u32[]{:S(2)}, u32[]{:S(2)}) collective-permute-start(bf16[512,128]{1,0:T(8,128)(2,1)S(1)} %get-tuple-element.106.refs_0_), channel_id=1, source_target_pairs={{0,2},{1,9},{2,0},{3,11},{4,6},{5,13},{6,4},{7,15},{8,10},{9,1},{1... | collective-permute-start | bytes 393224 | tf_op jit(solution)/shard_map/ppermute | solution.py:791
  88.7 4.6 %collective-permute-start.16 = (bf16[384,128]{1,0:T(8,128)(2,1)S(1)}, bf16[384,128]{1,0:T(8,128)(2,1)S(1)}, u32[]{:S(2)}, u32[]{:S(2)}) collective-permute-start(bf16[384,128]{1,0:T(8,128)(2,1)S(1)} %get-tuple-element.107.refs_2_), channel_id=1, source_target_pairs={{0,4},{1,9},{2,6},{3,11},{4,0},{5,13},{6,2},{7,15},{8,12},{9,1},{1... | collective-permute-start | bytes 294920 | tf_op jit(solution)/shard_map/ppermute | solution.py:791
  93.7 6.4 %collective-permute-start.17 = (bf16[1024,128]{1,0:T(8,128)(2,1)S(1)}, bf16[1024,128]{1,0:T(8,128)(2,1)S(1)}, u32[]{:S(2)}, u32[]{:S(2)}) collective-permute-start(bf16[1024,128]{1,0:T(8,128)(2,1)S(1)} %get-tuple-element.108.refs_0_), channel_id=1, source_target_pairs={{0,4},{1,3},{2,6},{3,1},{4,0},{5,7},{6,2},{7,5},{8,12},{9,11},{10,... | collective-permute-start | bytes 786440 | tf_op jit(solution)/shard_map/ppermute | solution.py:791
  94.3 6.5 %collective-permute-start.19 = (bf16[768,128]{1,0:T(8,128)(2,1)S(1)}, bf16[768,128]{1,0:T(8,128)(2,1)S(1)}, u32[]{:S(2)}, u32[]{:S(2)}) collective-permute-start(bf16[768,128]{1,0:T(8,128)(2,1)S(1)} %get-tuple-element.109.refs_0_), channel_id=1, source_target_pairs={{0,8},{1,3},{2,10},{3,1},{4,12},{5,7},{6,14},{7,5},{8,0},{9,11},{1... | collective-permute-start | bytes 589832 | tf_op jit(solution)/shard_map/ppermute | solution.py:791
  100.2 2.5 %collective-permute-start.18 = (bf16[2048,128]{1,0:T(8,128)(2,1)S(1)}, bf16[2048,128]{1,0:T(8,128)(2,1)S(1)}, u32[]{:S(2)}, u32[]{:S(2)}) collective-permute-start(bf16[2048,128]{1,0:T(8,128)(2,1)S(1)} %shard_map.202.refs_0_), channel_id=1, source_target_pairs={{0,1},{1,0},{2,3},{3,2},{4,5},{5,4},{6,7},{7,6},{8,9},{9,8},{10,11... | collective-permute-start | bytes 1572872 | tf_op jit(solution)/shard_map/ppermute | solution.py:791
  100.9 1.8 %collective-permute-start.20 = (bf16[1536,128]{1,0:T(8,128)(2,1)S(1)}, bf16[1536,128]{1,0:T(8,128)(2,1)S(1)}, u32[]{:S(2)}, u32[]{:S(2)}) collective-permute-start(bf16[1536,128]{1,0:T(8,128)(2,1)S(1)} %shard_map.203.refs_2_), channel_id=1, source_target_pairs={{0,1},{1,0},{2,3},{3,2},{4,5},{5,4},{6,7},{7,6},{8,9},{9,8},{10,11... | collective-permute-start | bytes 1179656 | tf_op jit(solution)/shard_map/ppermute | solution.py:791
